TPU v7x, 512 devices: a whole 4x8x8 slice. The times are simulated.
512 devices in a mesh: wide: 64 (over y, z), narrow: 8 (over x, core).
Axes of the slice: x: 4, y: 8, z: 8, core: 2. Of those that a mesh axis runs over, the one named last changes fastest.
Arguments:
- state: float32 [100, 524288], P(None, ('wide', 'narrow')), may hold values from -6 to 6
- neighbours: int32 [4, 524288], P(None, ('wide', 'narrow')), may hold values from 0 to 4863, as said below
- elem_tent: int32 [524288], P(('wide', 'narrow')), may hold values from 0 to 63, as said below
- boundary: int32 [393216], P(('wide', 'narrow')), may hold values from 0 to 1023, as said below
- active: int32 [4, 32768], P(None, ('wide', 'narrow')), may hold values from 0 to 1, as said below
- tent_height: float32 [32768], P(('wide', 'narrow')), may hold values from 0.25 to 1
- volume_op: bfloat16 [100, 100], replicated, may hold values from -0.3125 to 0.3125
- lift_op: bfloat16 [4, 100, 50], replicated, may hold values from -0.875 to 0.875
- trace_op: bfloat16 [4, 50, 100], replicated, may hold values from -0.625 to 0.625
Outputs:
- advanced: float32 [100, 524288], P(None, ('wide', 'narrow'))
Inputs may be any that keep to these rules, and one draw needn't show every extreme that they name: `elem_tent`: each tent of a partition holds exactly 16 of its elements. `boundary`: the 768 entries of a partition are distinct local elements; the local face 3 of its k-th entry has neighbours value 4 * 1024 + k. `neighbours`: values below 4096 are g * 1024 + e for a local element e and face g; values 4 * 1024 + k name column k of remote. `active`: at most 24 tents of one partition are pitched in one layer, and in every layer some partition pitches exactly 24.
All inputs are finite; a program needn't handle non-finite values.
Results may differ from a plain program's by a relative error of at most 0.0037.
Values may be sent and summed in bfloat16 or wider, within the bound.
No kernel may reach another device: no remote copies, remote signals or barrier semaphores. Data moves between devices by JAX's collectives and lax.ppermute only.
A program may use at most 64 MiB of HBM per device.

v0:
```python
import jax
import jax.numpy as jnp
from jax import lax
from jax.sharding import PartitionSpec as P

TAYLOR = 4


def shifted(block, axis, distance):
    devices = range(lax.axis_size(axis))
    route = [(i - distance, i) for i in devices if i - distance in devices]
    return lax.ppermute(block, axis, route)


def advance(values, rounded, neighbour_rows, table_rows, heights, live_mask, volume_op, lift_op):
    picked = jnp.take(table_rows, neighbour_rows, axis=0)
    source = jnp.einsum("gct,get->ce", lift_op, picked, preferred_element_type=jnp.float32)
    summed = values
    current_term = rounded
    for order_index in range(1, TAYLOR + 1):
        product = jnp.dot(volume_op, current_term, preferred_element_type=jnp.float32)
        if order_index == 1:
            product = product + source
        taylor_term = heights / order_index * product
        summed = summed + taylor_term
        current_term = taylor_term.astype(jnp.bfloat16)
    return jnp.where(live_mask > 0.5, summed, values)


def swap_blocks(outgoing, wide_len, narrow_len):
    low_wide = outgoing[:wide_len]
    high_wide = outgoing[wide_len : 2 * wide_len]
    low_narrow = outgoing[2 * wide_len : 2 * wide_len + narrow_len]
    high_narrow = outgoing[2 * wide_len + narrow_len :]
    from_low_wide = shifted(high_wide, "wide", 1)
    from_high_wide = shifted(low_wide, "wide", -1)
    from_low_narrow = shifted(high_narrow, "narrow", 1)
    from_high_narrow = shifted(low_narrow, "narrow", -1)
    return jnp.concatenate(
        [from_low_wide, from_high_wide, from_low_narrow, from_high_narrow], axis=0
    )


def local(
    state, neighbours, elem_tent, boundary, active, tent_height, volume_op, lift_op, trace_op
):
    tent_count = active.shape[1]
    elem_count = state.shape[1]
    halo_count = boundary.shape[0]
    wide_len = halo_count // 3
    narrow_len = wide_len // 2
    onehot = (elem_tent[None, :] == jnp.arange(tent_count, dtype=jnp.int32)[:, None]).astype(
        jnp.float32
    )
    tables = jnp.concatenate([tent_height[None, :], active.astype(jnp.float32)], axis=0)
    per_elem = jnp.dot(tables, onehot, precision=lax.Precision.HIGHEST)
    heights_all = per_elem[0]
    current = state
    for layer_index in range(active.shape[0]):
        rounded = current.astype(jnp.bfloat16)
        trace_rows = jnp.einsum(
            "ce,gtc->get", rounded, trace_op, preferred_element_type=jnp.float32
        ).astype(jnp.bfloat16)
        outgoing = jnp.take(trace_rows[3], boundary, axis=0)
        received = swap_blocks(outgoing, wide_len, narrow_len)
        table_rows = jnp.concatenate([trace_rows.reshape(4 * elem_count, -1), received], axis=0)
        live_mask = per_elem[layer_index + 1]
        current = advance(
            current, rounded, neighbours, table_rows, heights_all, live_mask, volume_op, lift_op
        )
    return current


def solution(mesh):
    return jax.shard_map(
        local,
        mesh=mesh,
        in_specs=(
            P(None, ("wide", "narrow")),
            P(None, ("wide", "narrow")),
            P(("wide", "narrow")),
            P(("wide", "narrow")),
            P(None, ("wide", "narrow")),
            P(("wide", "narrow")),
            P(),
            P(),
            P(),
        ),
        out_specs=P(None, ("wide", "narrow")),
        check_vma=False,
    )
```

profile of v0, /device:TPU:35, one launch (start us, length us, event | category | flops | bytes accessed | tf_op | source)
XLA Modules:
  0.0 145.1 jit_solution(454074324069950237)
XLA Ops:
  0.0 0.7 compare_and_fusion.1
  0.7 0.7 compare_select_fusion.1
  1.4 1.3 fusion
  2.9 1.9 %gather_fusion = bf16[768,50]{1,0:T(8,128)(2,1)S(1)} fusion(bf16[1024,50]{1,0:T(8,128)(2,1)S(1)} %copy.92, s32[1024]{0:T(1024)S(1)} %pad_clamp_fusion), kind=kCustom, calls=%fused_computation.clone | custom fusion | bytes 156672 | tf_op jit(solution)/shard_map/jit(_take)/gather | solution.py:64
  5.1 2.6 %collective-permute-start.3 = (bf16[128,50]{1,0:T(8,128)(2,1)S(1)}, bf16[128,50]{1,0:T(8,128)(2,1)S(1)}, u32[]{:S(2)}, u32[]{:S(2)}) collective-permute-start(bf16[128,50]{1,0:T(8,128)(2,1)S(1)} %get-tuple-element.23), channel_id=1, source_target_pairs={{1,0},{2,1},{3,2},{4,3},{5,4},{6,5},{7,6},{9,8},{10,9},{11,10},{12... | collective-permute-start | bytes 38408 | tf_op jit(solution)/shard_map/ppermute | solution.py:12
  7.6 3.0 %collective-permute-start.2 = (bf16[128,50]{1,0:T(8,128)(2,1)S(1)}, bf16[128,50]{1,0:T(8,128)(2,1)S(1)}, u32[]{:S(2)}, u32[]{:S(2)}) collective-permute-start(bf16[128,50]{1,0:T(8,128)(2,1)S(1)} %get-tuple-element.24), channel_id=1, source_target_pairs={{0,1},{1,2},{2,3},{3,4},{4,5},{5,6},{6,7},{8,9},{9,10},{10,11},{11... | collective-permute-start | bytes 38408 | tf_op jit(solution)/shard_map/ppermute | solution.py:12
  10.7 10.5 %collective-permute-start.1 = (bf16[256,50]{1,0:T(8,128)(2,1)S(1)}, bf16[256,50]{1,0:T(8,128)(2,1)S(1)}, u32[]{:S(2)}, u32[]{:S(2)}) collective-permute-start(bf16[256,50]{1,0:T(8,128)(2,1)S(1)} %get-tuple-element.25), channel_id=1, source_target_pairs={{8,0},{16,8},{24,16},{32,24},{40,32},{48,40},{56,48},{64,56},{72,6... | collective-permute-start | bytes 76808 | tf_op jit(solution)/shard_map/ppermute | solution.py:12
  21.3 1.9 %collective-permute-start = (bf16[256,50]{1,0:T(8,128)(2,1)S(1)}, bf16[256,50]{1,0:T(8,128)(2,1)S(1)}, u32[]{:S(2)}, u32[]{:S(2)}) collective-permute-start(bf16[256,50]{1,0:T(8,128)(2,1)S(1)} %get-tuple-element.26), channel_id=1, source_target_pairs={{0,8},{8,16},{16,24},{24,32},{32,40},{40,48},{48,56},{56,64},{64,7... | collective-permute-start | bytes 76808 | tf_op jit(solution)/shard_map/ppermute | solution.py:12
  23.2 0.5 copy.114
  24.2 6.2 %collective-permute-done = bf16[256,50]{1,0:T(8,128)(2,1)S(1)} collective-permute-done((bf16[256,50]{1,0:T(8,128)(2,1)S(1)}, bf16[256,50]{1,0:T(8,128)(2,1)S(1)}, u32[]{:S(2)}, u32[]{:S(2)}) %collective-permute-start) | collective-permute-done | bytes 25632 | tf_op jit(solution)/shard_map/ppermute | solution.py:12
  30.5 12.1 %gather_fusion.1 = bf16[4096,50]{1,0:T(8,128)(2,1)S(1)} fusion(bf16[4864,50]{1,0:T(8,128)(2,1)S(1)} %constant_dynamic-update-slice_fusion, s32[4096]{0:T(1024)S(1)} %bitcast_clamp_fusion), kind=kCustom, calls=%fused_computation.1.clone | custom fusion | bytes 835584 | tf_op jit(solution)/shard_map/jit(_take)/gather | solution.py:16
  42.7 0.4 copy.94
  43.1 0.3 convolution_bitcast_fusion.3
  43.4 0.3 copy-done.2
  43.7 0.2 fusion.16
  43.9 0.2 fusion.15
  44.1 0.2 fusion.14
  44.3 0.2 fusion.18
  44.6 0.6 copy-done.3
  45.1 0.3 fusion.1
  45.6 1.9 %gather_fusion.2 = bf16[768,50]{1,0:T(8,128)(2,1)S(1)} fusion(bf16[1024,50]{1,0:T(8,128)(2,1)S(1)} %copy.98, s32[1024]{0:T(1024)S(1)} %pad_clamp_fusion), kind=kCustom, calls=%fused_computation.2.clone | custom fusion | bytes 156672 | tf_op jit(solution)/shard_map/jit(_take)/gather | solution.py:64
  47.7 0.5 copy.115
  48.2 2.4 %collective-permute-start.7 = (bf16[128,50]{1,0:T(8,128)(2,1)S(1)}, bf16[128,50]{1,0:T(8,128)(2,1)S(1)}, u32[]{:S(2)}, u32[]{:S(2)}) collective-permute-start(bf16[128,50]{1,0:T(8,128)(2,1)S(1)} %get-tuple-element.19), channel_id=1, source_target_pairs={{1,0},{2,1},{3,2},{4,3},{5,4},{6,5},{7,6},{9,8},{10,9},{11,10},{12... | collective-permute-start | bytes 38408 | tf_op jit(solution)/shard_map/ppermute | solution.py:12
  50.7 3.1 %collective-permute-start.6 = (bf16[128,50]{1,0:T(8,128)(2,1)S(1)}, bf16[128,50]{1,0:T(8,128)(2,1)S(1)}, u32[]{:S(2)}, u32[]{:S(2)}) collective-permute-start(bf16[128,50]{1,0:T(8,128)(2,1)S(1)} %get-tuple-element.20), channel_id=1, source_target_pairs={{0,1},{1,2},{2,3},{3,4},{4,5},{5,6},{6,7},{8,9},{9,10},{10,11},{11... | collective-permute-start | bytes 38408 | tf_op jit(solution)/shard_map/ppermute | solution.py:12
  53.8 1.9 %collective-permute-start.5 = (bf16[256,50]{1,0:T(8,128)(2,1)S(1)}, bf16[256,50]{1,0:T(8,128)(2,1)S(1)}, u32[]{:S(2)}, u32[]{:S(2)}) collective-permute-start(bf16[256,50]{1,0:T(8,128)(2,1)S(1)} %get-tuple-element.21), channel_id=1, source_target_pairs={{8,0},{16,8},{24,16},{32,24},{40,32},{48,40},{56,48},{64,56},{72,6... | collective-permute-start | bytes 76808 | tf_op jit(solution)/shard_map/ppermute | solution.py:12
  55.7 3.4 %collective-permute-start.4 = (bf16[256,50]{1,0:T(8,128)(2,1)S(1)}, bf16[256,50]{1,0:T(8,128)(2,1)S(1)}, u32[]{:S(2)}, u32[]{:S(2)}) collective-permute-start(bf16[256,50]{1,0:T(8,128)(2,1)S(1)} %get-tuple-element.22), channel_id=1, source_target_pairs={{0,8},{8,16},{16,24},{24,32},{32,40},{40,48},{48,56},{56,64},{64,7... | collective-permute-start | bytes 76808 | tf_op jit(solution)/shard_map/ppermute | solution.py:12
  59.2 5.4 %collective-permute-done.4 = bf16[256,50]{1,0:T(8,128)(2,1)S(1)} collective-permute-done((bf16[256,50]{1,0:T(8,128)(2,1)S(1)}, bf16[256,50]{1,0:T(8,128)(2,1)S(1)}, u32[]{:S(2)}, u32[]{:S(2)}) %collective-permute-start.4) | collective-permute-done | bytes 25632 | tf_op jit(solution)/shard_map/ppermute | solution.py:12
  64.7 12.1 %gather_fusion.3 = bf16[4096,50]{1,0:T(8,128)(2,1)S(1)} fusion(bf16[4864,50]{1,0:T(8,128)(2,1)S(1)} %constant_dynamic-update-slice_fusion.5, s32[4096]{0:T(1024)S(1)} %bitcast_clamp_fusion), kind=kCustom, calls=%fused_computation.5.clone | custom fusion | bytes 835584 | tf_op jit(solution)/shard_map/jit(_take)/gather | solution.py:16
  76.8 0.4 copy.100
  77.2 0.3 convolution_bitcast_fusion.2
  77.5 0.2 fusion.20
  77.7 0.2 fusion.12
  77.9 0.2 fusion.11
  78.1 0.2 fusion.22
  78.4 0.3 fusion.2
  78.8 1.9 %gather_fusion.4 = bf16[768,50]{1,0:T(8,128)(2,1)S(1)} fusion(bf16[1024,50]{1,0:T(8,128)(2,1)S(1)} %copy.104, s32[1024]{0:T(1024)S(1)} %pad_clamp_fusion), kind=kCustom, calls=%fused_computation.3.clone | custom fusion | bytes 156672 | tf_op jit(solution)/shard_map/jit(_take)/gather | solution.py:64
  80.9 0.5 copy.116
  81.4 2.3 %collective-permute-start.11 = (bf16[128,50]{1,0:T(8,128)(2,1)S(1)}, bf16[128,50]{1,0:T(8,128)(2,1)S(1)}, u32[]{:S(2)}, u32[]{:S(2)}) collective-permute-start(bf16[128,50]{1,0:T(8,128)(2,1)S(1)} %get-tuple-element.15), channel_id=1, source_target_pairs={{1,0},{2,1},{3,2},{4,3},{5,4},{6,5},{7,6},{9,8},{10,9},{11,10},{12... | collective-permute-start | bytes 38408 | tf_op jit(solution)/shard_map/ppermute | solution.py:12
  83.7 3.3 %collective-permute-start.10 = (bf16[128,50]{1,0:T(8,128)(2,1)S(1)}, bf16[128,50]{1,0:T(8,128)(2,1)S(1)}, u32[]{:S(2)}, u32[]{:S(2)}) collective-permute-start(bf16[128,50]{1,0:T(8,128)(2,1)S(1)} %get-tuple-element.16), channel_id=1, source_target_pairs={{0,1},{1,2},{2,3},{3,4},{4,5},{5,6},{6,7},{8,9},{9,10},{10,11},{11... | collective-permute-start | bytes 38408 | tf_op jit(solution)/shard_map/ppermute | solution.py:12
  87.0 1.9 %collective-permute-start.9 = (bf16[256,50]{1,0:T(8,128)(2,1)S(1)}, bf16[256,50]{1,0:T(8,128)(2,1)S(1)}, u32[]{:S(2)}, u32[]{:S(2)}) collective-permute-start(bf16[256,50]{1,0:T(8,128)(2,1)S(1)} %get-tuple-element.17), channel_id=1, source_target_pairs={{8,0},{16,8},{24,16},{32,24},{40,32},{48,40},{56,48},{64,56},{72,6... | collective-permute-start | bytes 76808 | tf_op jit(solution)/shard_map/ppermute | solution.py:12
  88.9 3.4 %collective-permute-start.8 = (bf16[256,50]{1,0:T(8,128)(2,1)S(1)}, bf16[256,50]{1,0:T(8,128)(2,1)S(1)}, u32[]{:S(2)}, u32[]{:S(2)}) collective-permute-start(bf16[256,50]{1,0:T(8,128)(2,1)S(1)} %get-tuple-element.18), channel_id=1, source_target_pairs={{0,8},{8,16},{16,24},{24,32},{32,40},{40,48},{48,56},{56,64},{64,7... | collective-permute-start | bytes 76808 | tf_op jit(solution)/shard_map/ppermute | solution.py:12
  92.4 5.2 %collective-permute-done.8 = bf16[256,50]{1,0:T(8,128)(2,1)S(1)} collective-permute-done((bf16[256,50]{1,0:T(8,128)(2,1)S(1)}, bf16[256,50]{1,0:T(8,128)(2,1)S(1)}, u32[]{:S(2)}, u32[]{:S(2)}) %collective-permute-start.8) | collective-permute-done | bytes 25632 | tf_op jit(solution)/shard_map/ppermute | solution.py:12
  97.7 12.1 %gather_fusion.5 = bf16[4096,50]{1,0:T(8,128)(2,1)S(1)} fusion(bf16[4864,50]{1,0:T(8,128)(2,1)S(1)} %constant_dynamic-update-slice_fusion.10, s32[4096]{0:T(1024)S(1)} %bitcast_clamp_fusion), kind=kCustom, calls=%fused_computation.6.clone | custom fusion | bytes 835584 | tf_op jit(solution)/shard_map/jit(_take)/gather | solution.py:16
  109.8 0.4 copy.106
  110.2 0.3 convolution_bitcast_fusion.1
  110.5 0.2 fusion.24
  110.7 0.2 fusion.9
  110.9 0.2 fusion.8
  111.1 0.2 fusion.26
  111.4 0.3 fusion.3
  111.9 1.9 %gather_fusion.6 = bf16[768,50]{1,0:T(8,128)(2,1)S(1)} fusion(bf16[1024,50]{1,0:T(8,128)(2,1)S(1)} %copy.110, s32[1024]{0:T(1024)S(1)} %pad_clamp_fusion), kind=kCustom, calls=%fused_computation.4.clone | custom fusion | bytes 156672 | tf_op jit(solution)/shard_map/jit(_take)/gather | solution.py:64
  114.0 0.5 copy.117
  114.5 2.3 %collective-permute-start.15 = (bf16[128,50]{1,0:T(8,128)(2,1)S(1)}, bf16[128,50]{1,0:T(8,128)(2,1)S(1)}, u32[]{:S(2)}, u32[]{:S(2)}) collective-permute-start(bf16[128,50]{1,0:T(8,128)(2,1)S(1)} %get-tuple-element.11), channel_id=1, source_target_pairs={{1,0},{2,1},{3,2},{4,3},{5,4},{6,5},{7,6},{9,8},{10,9},{11,10},{12... | collective-permute-start | bytes 38408 | tf_op jit(solution)/shard_map/ppermute | solution.py:12
  116.8 3.3 %collective-permute-start.14 = (bf16[128,50]{1,0:T(8,128)(2,1)S(1)}, bf16[128,50]{1,0:T(8,128)(2,1)S(1)}, u32[]{:S(2)}, u32[]{:S(2)}) collective-permute-start(bf16[128,50]{1,0:T(8,128)(2,1)S(1)} %get-tuple-element.12), channel_id=1, source_target_pairs={{0,1},{1,2},{2,3},{3,4},{4,5},{5,6},{6,7},{8,9},{9,10},{10,11},{11... | collective-permute-start | bytes 38408 | tf_op jit(solution)/shard_map/ppermute | solution.py:12
  120.0 1.9 %collective-permute-start.13 = (bf16[256,50]{1,0:T(8,128)(2,1)S(1)}, bf16[256,50]{1,0:T(8,128)(2,1)S(1)}, u32[]{:S(2)}, u32[]{:S(2)}) collective-permute-start(bf16[256,50]{1,0:T(8,128)(2,1)S(1)} %get-tuple-element.13), channel_id=1, source_target_pairs={{8,0},{16,8},{24,16},{32,24},{40,32},{48,40},{56,48},{64,56},{72,6... | collective-permute-start | bytes 76808 | tf_op jit(solution)/shard_map/ppermute | solution.py:12
  122.0 3.4 %collective-permute-start.12 = (bf16[256,50]{1,0:T(8,128)(2,1)S(1)}, bf16[256,50]{1,0:T(8,128)(2,1)S(1)}, u32[]{:S(2)}, u32[]{:S(2)}) collective-permute-start(bf16[256,50]{1,0:T(8,128)(2,1)S(1)} %get-tuple-element.14), channel_id=1, source_target_pairs={{0,8},{8,16},{16,24},{24,32},{32,40},{40,48},{48,56},{56,64},{64,7... | collective-permute-start | bytes 76808 | tf_op jit(solution)/shard_map/ppermute | solution.py:12
  125.4 5.2 %collective-permute-done.12 = bf16[256,50]{1,0:T(8,128)(2,1)S(1)} collective-permute-done((bf16[256,50]{1,0:T(8,128)(2,1)S(1)}, bf16[256,50]{1,0:T(8,128)(2,1)S(1)}, u32[]{:S(2)}, u32[]{:S(2)}) %collective-permute-start.12) | collective-permute-done | bytes 25632 | tf_op jit(solution)/shard_map/ppermute | solution.py:12
  130.7 12.1 %gather_fusion.7 = bf16[4096,50]{1,0:T(8,128)(2,1)S(1)} fusion(bf16[4864,50]{1,0:T(8,128)(2,1)S(1)} %constant_dynamic-update-slice_fusion.15, s32[4096]{0:T(1024)S(1)} %bitcast_clamp_fusion), kind=kCustom, calls=%fused_computation.7.clone | custom fusion | bytes 835584 | tf_op jit(solution)/shard_map/jit(_take)/gather | solution.py:16
  142.8 0.4 copy.112
  143.3 0.3 convolution_bitcast_fusion
  143.5 0.2 fusion.28
  143.7 0.2 fusion.6
  143.9 0.2 fusion.5
  144.2 1.0 fusion.30
  (74 shorter events, 2.5 us)
Async XLA Ops:
  0.0 43.1 %copy-start = (bf16[4,100,50]{1,0,2:T(4,128)(2,1)S(1)}, bf16[4,100,50]{1,0,2:T(4,128)(2,1)}, u32[]{:S(2)}) copy-start(bf16[4,100,50]{1,0,2:T(4,128)(2,1)} %param.20) | copy-start | bytes 120004
  2.9 20.3 %copy-start.4 = (s32[4,1024]{1,0:T(4,128)S(1)}, s32[4,1024]{1,0:T(4,128)}, u32[]{:S(2)}) copy-start(s32[4,1024]{1,0:T(4,128)} %param.14) | copy-start | bytes 49156
  4.8 19.0 %copy-start.5 = (s32[4,64]{1,0:T(4,128)S(1)}, s32[4,64]{1,0:T(4,128)}, u32[]{:S(2)}) copy-start(s32[4,64]{1,0:T(4,128)} %param.17) | copy-start | bytes 3076
  4.8 19.0 %copy-start.6 = (s32[1024]{0:T(1024)S(1)}, s32[1024]{0:T(1024)}, u32[]{:S(2)}) copy-start(s32[1024]{0:T(1024)} %param.15) | copy-start | bytes 12292
  4.8 19.0 %copy-start.7 = (f32[64]{0:T(128)S(1)}, f32[64]{0:T(128)}, u32[]{:S(2)}) copy-start(f32[64]{0:T(128)} %param.18) | copy-start | bytes 772
  5.1 25.5 %collective-permute-start.3 = (bf16[128,50]{1,0:T(8,128)(2,1)S(1)}, bf16[128,50]{1,0:T(8,128)(2,1)S(1)}, u32[]{:S(2)}, u32[]{:S(2)}) collective-permute-start(bf16[128,50]{1,0:T(8,128)(2,1)S(1)} %get-tuple-element.23), channel_id=1, source_target_pairs={{1,0},{2,1},{3,2},{4,3},{5,4},{6,5},{7,6},{9,8},{10,9},{11,10},{12... | collective-permute-start | bytes 38408 | tf_op jit(solution)/shard_map/ppermute | solution.py:12
  7.6 22.8 %collective-permute-start.2 = (bf16[128,50]{1,0:T(8,128)(2,1)S(1)}, bf16[128,50]{1,0:T(8,128)(2,1)S(1)}, u32[]{:S(2)}, u32[]{:S(2)}) collective-permute-start(bf16[128,50]{1,0:T(8,128)(2,1)S(1)} %get-tuple-element.24), channel_id=1, source_target_pairs={{0,1},{1,2},{2,3},{3,4},{4,5},{5,6},{6,7},{8,9},{9,10},{10,11},{11... | collective-permute-start | bytes 38408 | tf_op jit(solution)/shard_map/ppermute | solution.py:12
  10.7 19.8 %collective-permute-start.1 = (bf16[256,50]{1,0:T(8,128)(2,1)S(1)}, bf16[256,50]{1,0:T(8,128)(2,1)S(1)}, u32[]{:S(2)}, u32[]{:S(2)}) collective-permute-start(bf16[256,50]{1,0:T(8,128)(2,1)S(1)} %get-tuple-element.25), channel_id=1, source_target_pairs={{8,0},{16,8},{24,16},{32,24},{40,32},{48,40},{56,48},{64,56},{72,6... | collective-permute-start | bytes 76808 | tf_op jit(solution)/shard_map/ppermute | solution.py:12
  21.3 9.2 %collective-permute-start = (bf16[256,50]{1,0:T(8,128)(2,1)S(1)}, bf16[256,50]{1,0:T(8,128)(2,1)S(1)}, u32[]{:S(2)}, u32[]{:S(2)}) collective-permute-start(bf16[256,50]{1,0:T(8,128)(2,1)S(1)} %get-tuple-element.26), channel_id=1, source_target_pairs={{0,8},{8,16},{16,24},{24,32},{32,40},{40,48},{48,56},{56,64},{64,7... | collective-permute-start | bytes 76808 | tf_op jit(solution)/shard_map/ppermute | solution.py:12
  42.7 0.7 copy-start.1
  42.7 1.0 copy-start.2
  44.3 0.8 copy-start.3
  48.2 16.4 %collective-permute-start.7 = (bf16[128,50]{1,0:T(8,128)(2,1)S(1)}, bf16[128,50]{1,0:T(8,128)(2,1)S(1)}, u32[]{:S(2)}, u32[]{:S(2)}) collective-permute-start(bf16[128,50]{1,0:T(8,128)(2,1)S(1)} %get-tuple-element.19), channel_id=1, source_target_pairs={{1,0},{2,1},{3,2},{4,3},{5,4},{6,5},{7,6},{9,8},{10,9},{11,10},{12... | collective-permute-start | bytes 38408 | tf_op jit(solution)/shard_map/ppermute | solution.py:12
  50.7 14.0 %collective-permute-start.6 = (bf16[128,50]{1,0:T(8,128)(2,1)S(1)}, bf16[128,50]{1,0:T(8,128)(2,1)S(1)}, u32[]{:S(2)}, u32[]{:S(2)}) collective-permute-start(bf16[128,50]{1,0:T(8,128)(2,1)S(1)} %get-tuple-element.20), channel_id=1, source_target_pairs={{0,1},{1,2},{2,3},{3,4},{4,5},{5,6},{6,7},{8,9},{9,10},{10,11},{11... | collective-permute-start | bytes 38408 | tf_op jit(solution)/shard_map/ppermute | solution.py:12
  53.8 10.8 %collective-permute-start.5 = (bf16[256,50]{1,0:T(8,128)(2,1)S(1)}, bf16[256,50]{1,0:T(8,128)(2,1)S(1)}, u32[]{:S(2)}, u32[]{:S(2)}) collective-permute-start(bf16[256,50]{1,0:T(8,128)(2,1)S(1)} %get-tuple-element.21), channel_id=1, source_target_pairs={{8,0},{16,8},{24,16},{32,24},{40,32},{48,40},{56,48},{64,56},{72,6... | collective-permute-start | bytes 76808 | tf_op jit(solution)/shard_map/ppermute | solution.py:12
  55.7 8.9 %collective-permute-start.4 = (bf16[256,50]{1,0:T(8,128)(2,1)S(1)}, bf16[256,50]{1,0:T(8,128)(2,1)S(1)}, u32[]{:S(2)}, u32[]{:S(2)}) collective-permute-start(bf16[256,50]{1,0:T(8,128)(2,1)S(1)} %get-tuple-element.22), channel_id=1, source_target_pairs={{0,8},{8,16},{16,24},{24,32},{32,40},{40,48},{48,56},{56,64},{64,7... | collective-permute-start | bytes 76808 | tf_op jit(solution)/shard_map/ppermute | solution.py:12
  81.4 16.2 %collective-permute-start.11 = (bf16[128,50]{1,0:T(8,128)(2,1)S(1)}, bf16[128,50]{1,0:T(8,128)(2,1)S(1)}, u32[]{:S(2)}, u32[]{:S(2)}) collective-permute-start(bf16[128,50]{1,0:T(8,128)(2,1)S(1)} %get-tuple-element.15), channel_id=1, source_target_pairs={{1,0},{2,1},{3,2},{4,3},{5,4},{6,5},{7,6},{9,8},{10,9},{11,10},{12... | collective-permute-start | bytes 38408 | tf_op jit(solution)/shard_map/ppermute | solution.py:12
  83.7 13.9 %collective-permute-start.10 = (bf16[128,50]{1,0:T(8,128)(2,1)S(1)}, bf16[128,50]{1,0:T(8,128)(2,1)S(1)}, u32[]{:S(2)}, u32[]{:S(2)}) collective-permute-start(bf16[128,50]{1,0:T(8,128)(2,1)S(1)} %get-tuple-element.16), channel_id=1, source_target_pairs={{0,1},{1,2},{2,3},{3,4},{4,5},{5,6},{6,7},{8,9},{9,10},{10,11},{11... | collective-permute-start | bytes 38408 | tf_op jit(solution)/shard_map/ppermute | solution.py:12
  87.0 10.6 %collective-permute-start.9 = (bf16[256,50]{1,0:T(8,128)(2,1)S(1)}, bf16[256,50]{1,0:T(8,128)(2,1)S(1)}, u32[]{:S(2)}, u32[]{:S(2)}) collective-permute-start(bf16[256,50]{1,0:T(8,128)(2,1)S(1)} %get-tuple-element.17), channel_id=1, source_target_pairs={{8,0},{16,8},{24,16},{32,24},{40,32},{48,40},{56,48},{64,56},{72,6... | collective-permute-start | bytes 76808 | tf_op jit(solution)/shard_map/ppermute | solution.py:12
  88.9 8.7 %collective-permute-start.8 = (bf16[256,50]{1,0:T(8,128)(2,1)S(1)}, bf16[256,50]{1,0:T(8,128)(2,1)S(1)}, u32[]{:S(2)}, u32[]{:S(2)}) collective-permute-start(bf16[256,50]{1,0:T(8,128)(2,1)S(1)} %get-tuple-element.18), channel_id=1, source_target_pairs={{0,8},{8,16},{16,24},{24,32},{32,40},{40,48},{48,56},{56,64},{64,7... | collective-permute-start | bytes 76808 | tf_op jit(solution)/shard_map/ppermute | solution.py:12
  114.5 16.2 %collective-permute-start.15 = (bf16[128,50]{1,0:T(8,128)(2,1)S(1)}, bf16[128,50]{1,0:T(8,128)(2,1)S(1)}, u32[]{:S(2)}, u32[]{:S(2)}) collective-permute-start(bf16[128,50]{1,0:T(8,128)(2,1)S(1)} %get-tuple-element.11), channel_id=1, source_target_pairs={{1,0},{2,1},{3,2},{4,3},{5,4},{6,5},{7,6},{9,8},{10,9},{11,10},{12... | collective-permute-start | bytes 38408 | tf_op jit(solution)/shard_map/ppermute | solution.py:12
  116.8 13.9 %collective-permute-start.14 = (bf16[128,50]{1,0:T(8,128)(2,1)S(1)}, bf16[128,50]{1,0:T(8,128)(2,1)S(1)}, u32[]{:S(2)}, u32[]{:S(2)}) collective-permute-start(bf16[128,50]{1,0:T(8,128)(2,1)S(1)} %get-tuple-element.12), channel_id=1, source_target_pairs={{0,1},{1,2},{2,3},{3,4},{4,5},{5,6},{6,7},{8,9},{9,10},{10,11},{11... | collective-permute-start | bytes 38408 | tf_op jit(solution)/shard_map/ppermute | solution.py:12
  120.0 10.6 %collective-permute-start.13 = (bf16[256,50]{1,0:T(8,128)(2,1)S(1)}, bf16[256,50]{1,0:T(8,128)(2,1)S(1)}, u32[]{:S(2)}, u32[]{:S(2)}) collective-permute-start(bf16[256,50]{1,0:T(8,128)(2,1)S(1)} %get-tuple-element.13), channel_id=1, source_target_pairs={{8,0},{16,8},{24,16},{32,24},{40,32},{48,40},{56,48},{64,56},{72,6... | collective-permute-start | bytes 76808 | tf_op jit(solution)/shard_map/ppermute | solution.py:12
  122.0 8.7 %collective-permute-start.12 = (bf16[256,50]{1,0:T(8,128)(2,1)S(1)}, bf16[256,50]{1,0:T(8,128)(2,1)S(1)}, u32[]{:S(2)}, u32[]{:S(2)}) collective-permute-start(bf16[256,50]{1,0:T(8,128)(2,1)S(1)} %get-tuple-element.14), channel_id=1, source_target_pairs={{0,8},{8,16},{16,24},{24,32},{32,40},{40,48},{48,56},{56,64},{64,7... | collective-permute-start | bytes 76808 | tf_op jit(solution)/shard_map/ppermute | solution.py:12
where the time goes:
time: 146 us; the launch traced here: 145 us
  local copies, waits for them, and re-layouts  62 us (42%)
  starting transfers between devices  50.6 us (35%)
  waiting for transfers between devices  22.1 us (15%)
  matrix products  7.4 us (5%)
  other arithmetic  2.18 us (1%)
    ppermute x16, starting transfers between devices, shifted(): return lax.ppermute(block, axis, route)  50.6 us
    gather x8, local copies, waits for them, and re-layouts, advance(): picked = jnp.take(table_rows, neighbour_rows, axis=0)  50.2 us
    ppermute x16, waiting for transfers between devices, shifted(): return lax.ppermute(block, axis, route)  22.1 us
    gather x4, local copies, waits for them, and re-layouts, local(): outgoing = jnp.take(trace_rows[3], boundary, axis=0)  7.52 us
    dot_general x16, matrix products, advance(): jnp.dot(volume_op, current_term, preferred_element_type=jnp.float32)  4.08 us
  transfers between devices with their start and end apart: 16, of which 4 were waited for; matrix products, arithmetic and copies ran while one was open for 1% of the time, Pallas kernels for 0%

commit v1 on v0

v1 whole, which is shorter than its diff:
```python
import functools

import jax
import jax.numpy as jnp
from jax import lax
from jax.experimental import pallas as pl
from jax.experimental.pallas import tpu as pltpu
from jax.sharding import PartitionSpec as P

TAYLOR = 4
TENT_SIZE = 16
MAX_TENTS = 24
MAX_LIVE = TENT_SIZE * MAX_TENTS
ROWS = 64
BLOCK = 256
CHUNK = 512
LANES = 128
VMEM = 24 * 2**20
PHASES = (("wide", 1), ("narrow", 1), ("wide", 0), ("narrow", 0))
BF16, F32, I32 = jnp.bfloat16, jnp.float32, jnp.int32


def mm(left, right):
    return jnp.dot(left, right, preferred_element_type=F32)


def mm_t(left, right):
    return lax.dot_general(left, right, (((1,), (1,)), ((), ())), preferred_element_type=F32)


def low_of(index):
    return index & (BLOCK - 1)


def high_of(index):
    return index >> 8


def hot(index, depth):
    low, high = low_of(index), high_of(index)
    rows = lax.broadcasted_iota(I32, (BLOCK, index.shape[1]), 0).astype(F32).astype(BF16)
    parts = []
    for b in range(-(-depth // BLOCK)):
        here = jnp.where(high == b, low, -1).astype(F32).astype(BF16)
        count = min(BLOCK, depth - b * BLOCK)
        parts.append(jnp.where(rows[:count] == here, jnp.ones((), BF16), jnp.zeros((), BF16)))
    return parts[0] if len(parts) == 1 else jnp.concatenate(parts, axis=0)


def choose(found, key, first, rows, default=None):
    count = found.shape[0] // rows
    total = found[(count - 1) * rows :]
    if default is not None:
        total = jnp.where(key == first + count - 1, total, default)
    for b in range(count - 2, -1, -1):
        total = jnp.where(key == first + b, found[b * rows : (b + 1) * rows], total)
    return total


def stack(table):
    return jnp.concatenate([table[:, at : at + BLOCK] for at in range(0, table.shape[1], BLOCK)], axis=0)


def pick(table, low, high, first=0, default=0.0):
    return choose(mm(stack(table), hot(low, BLOCK)), high, first, table.shape[0], default)


def two_parts(values):
    rows = values.shape[0]
    start = -(-rows // 16) * 16
    top = values.astype(BF16).astype(F32)
    gap = jnp.zeros((start - rows, values.shape[1]), F32)
    return jnp.concatenate([jnp.concatenate([top, gap], axis=0), values - top], axis=0).astype(BF16), start


def three_parts(values):
    top = values.astype(BF16).astype(F32)
    mid = (values - top).astype(BF16).astype(F32)
    return top, mid, values - top - mid


def even(axis):
    return lax.axis_index(axis) % 2 == 0


def by_phase(columns):
    half, quarter = columns.shape[1] // 3, columns.shape[1] // 6
    low, high = columns[:, :half], columns[:, half : 2 * half]
    left, right = columns[:, 2 * half : 2 * half + quarter], columns[:, 2 * half + quarter :]
    wide, narrow = even("wide"), even("narrow")
    return jnp.concatenate(
        [
            jnp.where(wide, low, high),
            jnp.where(wide, high, low),
            jnp.where(narrow, left, right),
            jnp.where(narrow, right, left),
        ],
        axis=1,
    )


def remote_by_phase(near, local_columns, halo):
    half, quarter = halo // 3, halo // 6
    at = near - local_columns
    wide, narrow = even("wide"), even("narrow")
    in_wide = jnp.where(wide, at, jnp.where(at < half, at + half, at - half))
    in_narrow = jnp.where(narrow, at, jnp.where(at < 2 * half + quarter, at + quarter, at - quarter))
    return jnp.where(at < 0, near, local_columns + jnp.where(at < 2 * half, in_wide, in_narrow))


def store_blocks(out, refs):
    at = 0
    for ref in refs:
        width = ref.shape[1]
        ref[...] = out[:, at : at + width].astype(BF16)
        at += width


def row_of(ref):
    return jnp.concatenate([ref[i : i + 1, :] for i in range(ref.shape[0])], axis=1)


def face_rows(op, face):
    gap = jnp.zeros((ROWS - op.shape[0], op.shape[2]), F32)
    return jnp.concatenate([op[:, face, :].astype(F32), gap], axis=0)


def first_kernel(*refs):
    count = (len(refs) - 4) // 2
    inputs, blocks, held, sems = refs[:count], refs[count : count + 4], refs[count + 4 : -1], refs[-1]
    copies = [pltpu.make_async_copy(src, dst, sems.at[i]) for i, (src, dst) in enumerate(zip(inputs, held))]
    for copy in copies:
        copy.start()
    for copy in copies:
        copy.wait()
    state, boundary, trace_op = held[:3]
    traces = mm(face_rows(trace_op, 3).astype(BF16), state[...].astype(BF16)).astype(BF16)
    at = by_phase(row_of(boundary))
    store_blocks(pick(traces, low_of(at), high_of(at)), blocks)


def make_index(neighbours, elem_tent, boundary, active, height, compact, ranks, sent):
    tent = row_of(elem_tent)
    elems = tent.shape[1]
    tents = height.shape[1]
    layers = active.shape[0]
    act = active[...].astype(F32)
    top, mid, low = three_parts(height[...])
    row = lax.broadcasted_iota(I32, (2 * layers, tents), 0)
    high_rows = jnp.where(row == 0, top, jnp.where(row == 1, mid, jnp.where(row == 2, low, 0.0)))
    found = mm(jnp.concatenate([act, act, high_rows], axis=0).astype(BF16), hot(tent, tents))
    live, high_rows = found[: 2 * layers], found[2 * layers :]
    upto = jnp.where(
        lax.broadcasted_iota(I32, (LANES, LANES), 0) <= lax.broadcasted_iota(I32, (LANES, LANES), 1), 1.0, 0.0
    ).astype(BF16)
    chunks = [live[:, at : at + LANES] for at in range(0, elems, LANES)]
    counts = mm(jnp.concatenate(chunks, axis=0).astype(BF16), upto)
    offset = jnp.zeros((2 * layers, 1), F32)
    parts = []
    for c in range(len(chunks)):
        part = counts[c * 2 * layers : (c + 1) * 2 * layers]
        parts.append(part + offset)
        offset = offset + part[:, LANES - 1 :]
    place = jnp.where(live > 0.5, jnp.concatenate(parts, axis=1), 0.0).astype(I32)
    ranks[...] = place - 1
    row = lax.broadcasted_iota(I32, (2 * layers, elems), 0)
    digits = jnp.where(row < layers, low_of(place), high_of(place)).astype(F32)
    table = jnp.concatenate([digits, jnp.zeros_like(digits)], axis=0).astype(BF16)
    at = by_phase(row_of(boundary))
    found = pick(table, low_of(at), high_of(at))
    sent[...] = (found[:layers] + BLOCK * found[layers : 2 * layers]).astype(I32) - 1

    near = remote_by_phase(neighbours[...], 4 * elems, at.shape[1])
    near = jnp.concatenate([near, near], axis=0)
    near = jnp.where(row < layers, low_of(near), high_of(near)).astype(F32)
    elem = lax.broadcasted_iota(I32, (2 * layers, elems), 1)
    own = jnp.where(row == 3, low_of(elem).astype(F32), jnp.where(row == 4, high_of(elem).astype(F32), 0.0))
    rows16 = jnp.concatenate([near, high_rows + own], axis=0)
    count = MAX_LIVE // LANES
    for l in range(0, layers, 2):
        tables, columns = [], []
        for m in (l, l + 1):
            rank = place[m : m + 1] - 1
            tables += [jnp.where(rank >> 7 == b, rows16, 0.0) for b in range(count)]
            columns.append(hot(jnp.where(rank < 0, -1, rank & (LANES - 1)), LANES))
        found = mm_t(jnp.concatenate(tables, axis=0).astype(BF16), jnp.concatenate(columns, axis=0))
        for m in (0, 1):
            for b in range(count):
                at = 16 * (m * count + b)
                compact[l + m, :, b * LANES : (b + 1) * LANES] = found[at : at + 16, m * LANES : (m + 1) * LANES]


def whole(compact, row, count=1):
    rows = [compact[i : i + 1] for i in range(row, row + count)]
    return (rows[0] if count == 1 else jnp.concatenate(rows, axis=1)).astype(I32)


def by_face(columns):
    n = columns.shape[1] // 4
    return jnp.concatenate([columns[:, g * n : (g + 1) * n] for g in range(4)], axis=0)


def local_part(values, compact, volume, lift, trace, base, kept):
    comps, elems = values.shape
    blocks = elems // BLOCK
    parts, rows = two_parts(values)
    top = stack(parts[:rows])
    low = jnp.concatenate([whole(compact, 11), whole(compact, 0, 4)], axis=1)
    high = jnp.concatenate([whole(compact, 12), whole(compact, 4, 4)], axis=1)
    block, face = high & (blocks - 1), high // blocks
    near = []
    for at in range(0, low.shape[1], CHUNK):
        here = slice(at, at + CHUNK)
        near.append(choose(mm(top, hot(low[:, here], BLOCK)), block[:, here], 0, rows)[:comps].astype(BF16))
    near = jnp.concatenate(near, axis=1)
    mine, near, face = near[:, :MAX_LIVE], near[:, MAX_LIVE:], face[:, MAX_LIVE:]
    picked = []
    for at in range(0, near.shape[1], CHUNK):
        here = slice(at, at + CHUNK)
        picked.append(choose(mm(trace[...], near[:, here]), face[:, here], 0, ROWS, 0.0))
    picked = by_face(jnp.concatenate(picked, axis=1)).astype(BF16)
    if kept is not None:
        rest = stack(jnp.concatenate([parts[rows:].astype(F32), jnp.zeros((rows - comps, elems), F32)], axis=0))
        own = slice(0, MAX_LIVE)
        rest = choose(mm(rest.astype(BF16), hot(low[:, own], BLOCK)), block[:, own], 0, rows)
        kept[...] = mine.astype(F32) + rest[:comps]
    base[...] = mm(volume[...], mine) + mm(lift[...], picked)


def local_first_kernel(
    state, neighbours, elem_tent, boundary, active, height, volume, lift_op, trace_op,
    compact, ranks, sent, base, kept, lift, trace,
):
    make_index(neighbours, elem_tent, boundary, active, height, compact, ranks, sent)
    lifts = jnp.concatenate([face_rows(lift_op, g) for g in range(4)], axis=0).astype(BF16)
    comps = lifts.shape[1]
    diagonal = lax.broadcasted_iota(I32, (comps, comps), 0) == lax.broadcasted_iota(I32, (comps, comps), 1)
    lift[...] = mm_t(jnp.where(diagonal, 1.0, 0.0).astype(BF16), lifts).astype(BF16)
    trace[...] = jnp.concatenate([face_rows(trace_op, g) for g in range(4)], axis=0).astype(BF16)
    local_part(state[...], compact[0], volume, lift, trace, base, kept)


def scatter(delta, rank):
    parts, second = two_parts(delta)
    found = mm(parts, hot(rank, MAX_LIVE))
    return found[: delta.shape[0]] + found[second:]


def local_kernel(layer, state, delta, compact, ranks, volume, lift, trace, new_state, base, kept=None):
    values = state[...] + scatter(delta[...], ranks[layer - 1 : layer])
    new_state[...] = values
    local_part(values, compact[layer], volume, lift, trace, base, kept)


def taylor_terms(received, compact, base, volume, lift):
    remote = jnp.concatenate([ref[...] for ref in received], axis=1)
    first_block = 4 * 1024 // BLOCK
    picked = by_face(pick(remote, whole(compact, 0, 4), whole(compact, 4, 4), first_block)).astype(BF16)
    heights = compact[8:9] + compact[9:10] + compact[10:11]
    term = heights * (base[...] + mm(lift[...], picked))
    total = term
    for order in range(2, TAYLOR + 1):
        term = (heights / order) * mm(volume[...], term.astype(BF16))
        total = total + term
    return total


def advance_kernel(layer, r0, r1, r2, r3, o0, o1, o2, o3, compact, base, kept, sent, volume, lift, trace, delta, *outgoing):
    total = taylor_terms((r0, r1, r2, r3), compact[layer], base, volume, lift)
    delta[...] = total
    traces = mm(trace[3 * ROWS :, :], (kept[...] + total).astype(BF16))
    rest = -MAX_LIVE % BLOCK
    table = jnp.concatenate([traces, jnp.zeros((ROWS, rest), F32)], axis=1).astype(BF16)
    place = sent[layer : layer + 1]
    found = pick(table, low_of(place), high_of(place))
    before = jnp.concatenate([o0[...], o1[...], o2[...], o3[...]], axis=1).astype(F32)
    store_blocks(jnp.where(place >= 0, found, before), outgoing)


def last_kernel(layer, r0, r1, r2, r3, compact, base, ranks, volume, lift, state, advanced, held, sems):
    parts, second = two_parts(taylor_terms((r0, r1, r2, r3), compact[layer], base, volume, lift))
    comps, elems = state.shape
    copies = []
    for c in range(elems // BLOCK):
        here = slice(c * BLOCK, (c + 1) * BLOCK)
        found = mm(parts, hot(ranks[layer : layer + 1, here], MAX_LIVE))
        held[:, here] = state[:, here] + found[:comps] + found[second:]
        copies.append(pltpu.make_async_copy(held.at[:, here], advanced.at[:, here], sems.at[c]))
        copies[-1].start()
    for copy in copies:
        copy.wait()


def call(kernel, outs, args, flops):
    outs = [jax.ShapeDtypeStruct(shape, dtype) for shape, dtype in outs]
    return pl.pallas_call(
        kernel,
        out_shape=outs,
        compiler_params=pltpu.CompilerParams(vmem_limit_bytes=VMEM),
        cost_estimate=pl.CostEstimate(flops=flops, bytes_accessed=2**20, transcendentals=0),
    )(*args)


def swapped(block, axis, first):
    pairs = [(i, i + 1) for i in range(first, lax.axis_size(axis) - 1, 2)]
    return lax.ppermute(block, axis, pairs + [(j, i) for i, j in pairs])


def exchange(outgoing):
    wide_1, wide_0, narrow_1, narrow_0 = outgoing
    wide_1, narrow_1, wide_0, narrow_0 = [
        swapped(block, axis, first)
        for block, (axis, first) in zip((wide_1, narrow_1, wide_0, narrow_0), PHASES)
    ]
    return wide_1, wide_0, narrow_1, narrow_0


def local(state, neighbours, elem_tent, boundary, active, tent_height, volume_op, lift_op, trace_op):
    comps, elems = state.shape
    layers = active.shape[0]
    halo = boundary.shape[0]
    wide_len = halo // 3
    narrow_len = wide_len // 2
    boundary = boundary.reshape(-1, LANES)
    elem_tent = elem_tent.reshape(-1, LANES)
    tent_height = tent_height.reshape(1, -1)

    blocks = [((ROWS, width), BF16) for width in (wide_len, wide_len, narrow_len, narrow_len)]
    live = ((comps, MAX_LIVE), F32)
    all_columns = ((comps, elems), F32)
    args = (
        state, boundary, trace_op.transpose(1, 0, 2), neighbours, elem_tent, active, tent_height, volume_op,
        lift_op.transpose(2, 0, 1),
    )
    held = [jax.ShapeDtypeStruct(arg.shape, arg.dtype) for arg in args]
    outs = pl.pallas_call(
        first_kernel,
        in_specs=[pl.BlockSpec(memory_space=pltpu.MemorySpace.HBM)] * len(args),
        out_shape=[jax.ShapeDtypeStruct(shape, dtype) for shape, dtype in blocks] + held,
        scratch_shapes=[pltpu.SemaphoreType.DMA((len(args),))],
        compiler_params=pltpu.CompilerParams(vmem_limit_bytes=VMEM),
    )(*[pltpu.with_memory_space_constraint(arg, pltpu.MemorySpace.HBM) for arg in args])
    outgoing = outs[:4]
    state, boundary, trace, neighbours, elem_tent, active, tent_height, volume_op, lift = outs[4:]
    received = exchange(outgoing)
    compact, ranks, sent, base, kept, lift, trace = call(
        local_first_kernel,
        [
            ((layers, 16, MAX_LIVE), F32),
            ((2 * layers, elems), I32),
            ((layers, halo), I32),
            live,
            live,
            ((comps, 4 * ROWS), BF16),
            ((4 * ROWS, comps), BF16),
        ],
        (state, neighbours, elem_tent, boundary, active, tent_height, volume_op, lift, trace),
        10**9,
    )
    for layer in range(layers - 1):
        delta, *outgoing = call(
            functools.partial(advance_kernel, layer),
            [live] + blocks,
            (*received, *outgoing, compact, base, kept, sent, volume_op, lift, trace),
            10**9,
        )
        received = exchange(outgoing)
        state, base, *rest = call(
            functools.partial(local_kernel, layer + 1),
            [all_columns, live] + [live] * (layer + 2 < layers),
            (state, delta, compact, ranks, volume_op, lift, trace),
            10**9,
        )
        kept = rest[0] if rest else None
    return pl.pallas_call(
        functools.partial(last_kernel, layers - 1),
        out_specs=pl.BlockSpec(memory_space=pltpu.MemorySpace.HBM),
        out_shape=jax.ShapeDtypeStruct((comps, elems), F32),
        scratch_shapes=[pltpu.VMEM((comps, elems), F32), pltpu.SemaphoreType.DMA((elems // BLOCK,))],
        compiler_params=pltpu.CompilerParams(vmem_limit_bytes=VMEM),
    )(*received, compact, base, ranks, volume_op, lift, state)


def solution(mesh):
    both = ("wide", "narrow")
    return jax.shard_map(
        local,
        mesh=mesh,
        in_specs=(P(None, both), P(None, both), P(both), P(both), P(None, both), P(both), P(), P(), P()),
        out_specs=P(None, both),
        check_vma=False,
    )
```

time: 146 us -> 66.2 us (0.45)
  local copies, waits for them, and re-layouts: 62 us -> 0 us
  waiting for transfers between devices: 22.1 us -> 0.04 us
  Pallas kernels: 0 us -> 13.4 us
  matrix products: 7.4 us -> 0 us
  other arithmetic: 2.18 us -> 0 us
    gather x12 -> x0, local copies, waits for them, and re-layouts: 57.7 us -> none  [the longest x8 50.2 us: advance(): picked = jnp.take(table_rows, neighbour_rows, axis=0)]
    ppermute x16, waiting for transfers between devices: 22.1 us -> 0.04 us  [swapped(): return lax.ppermute(block, axis, pairs + [(j, i) for i, j in pairs])]
    pallas_call x0 -> x9, Pallas kernels: none -> 13.4 us  [the longest x7 9.83 us: call(): pl.pallas_call(kernel, out_shape=outs, compiler_params=pltpu.CompilerPara...]
    dot_general x25 -> x0, matrix products: 7.4 us -> none  [the longest x16 4.08 us: advance(): jnp.dot(volume_op, current_term, preferred_element_type=jnp.float32)]
    reshape x4 -> x0, local copies, waits for them, and re-layouts: 2.03 us -> none  [local(): trace_rows.reshape(4 * elem_count, -1)]
  transfers between devices with their start and end apart: 16 -> 16, of which waited for: 4 -> 0; matrix products, arithmetic and copies ran while one was open for 1% -> 0% of each run, Pallas kernels for 0% -> 9%
where the time goes in v1:
time: 66.2 us; the launch traced here: 65.7 us
  starting transfers between devices  51.9 us (78%)
  Pallas kernels  13.4 us (20%)
    ppermute x16, starting transfers between devices, swapped(): return lax.ppermute(block, axis, pairs + [(j, i) for i, j in pairs])  51.9 us
    pallas_call x7, Pallas kernels, call(): pl.pallas_call(kernel, out_shape=outs, compiler_params=pltpu.CompilerPara...  9.83 us
    pallas_call x1, Pallas kernels, local(): pl.pallas_call(functools.partial(last_kernel, layers - 1), out_specs=pl.B...  2.01 us
    pallas_call x1, Pallas kernels, local(): pl.pallas_call(first_kernel, in_specs=[pl.BlockSpec(memory_space=pltpu.Me...  1.52 us
  transfers between devices with their start and end apart: 16, of which 0 were waited for; matrix products, arithmetic and copies ran while one was open for 0% of the time, Pallas kernels for 9%

profile of v1, /device:TPU:35, one launch (start us, length us, event | category | flops | bytes accessed | tf_op | source)
XLA Modules:
  0.0 65.7 jit_solution(5237283841132803467)
XLA Ops:
  0.0 1.5 %shard_map.91 = (bf16[64,256]{1,0:T(8,128)(2,1)S(1)}, bf16[64,256]{1,0:T(8,128)(2,1)S(1)}, bf16[64,128]{1,0:T(8,128)(2,1)S(1)}, bf16[64,128]{1,0:T(8,128)(2,1)S(...) custom-call(f32[100,1024]{1,0:T(8,128)} %refs_0_.1, ...), custom_call_target="tpu_custom_call" | custom-call | tf_op jit(solution)/shard_map/pallas_call | solution.py:336
  1.5 10.6 %collective-permute-start = (bf16[64,256]{1,0:T(8,128)(2,1)S(1)}, bf16[64,256]{1,0:T(8,128)(2,1)S(1)}, u32[]{:S(2)}, u32[]{:S(2)}) collective-permute-start(bf16[64,256]{1,0:T(8,128)(2,1)S(1)} %get-tuple-element.48.o0), channel_id=1, source_target_pairs={{8,16},{24,32},{40,48},{56,64},{72,80},{88,96},{104,112},{120,128}... | collective-permute-start | bytes 98312 | tf_op jit(solution)/shard_map/ppermute | solution.py:306
  12.1 1.9 %collective-permute-start.1 = (bf16[64,256]{1,0:T(8,128)(2,1)S(1)}, bf16[64,256]{1,0:T(8,128)(2,1)S(1)}, u32[]{:S(2)}, u32[]{:S(2)}) collective-permute-start(bf16[64,256]{1,0:T(8,128)(2,1)S(1)} %get-tuple-element.49.o1), channel_id=1, source_target_pairs={{0,8},{16,24},{32,40},{48,56},{64,72},{80,88},{96,104},{112,120},{... | collective-permute-start | bytes 98312 | tf_op jit(solution)/shard_map/ppermute | solution.py:306
  14.0 4.0 %collective-permute-start.2 = (bf16[64,128]{1,0:T(8,128)(2,1)S(1)}, bf16[64,128]{1,0:T(8,128)(2,1)S(1)}, u32[]{:S(2)}, u32[]{:S(2)}) collective-permute-start(bf16[64,128]{1,0:T(8,128)(2,1)S(1)} %get-tuple-element.50.o2), channel_id=1, source_target_pairs={{1,2},{3,4},{5,6},{2,1},{4,3},{6,5},{9,10},{11,12},{13,14},{10,9},... | collective-permute-start | bytes 49160 | tf_op jit(solution)/shard_map/ppermute | solution.py:306
  18.0 1.9 %collective-permute-start.3 = (bf16[64,128]{1,0:T(8,128)(2,1)S(1)}, bf16[64,128]{1,0:T(8,128)(2,1)S(1)}, u32[]{:S(2)}, u32[]{:S(2)}) collective-permute-start(bf16[64,128]{1,0:T(8,128)(2,1)S(1)} %get-tuple-element.51.o3), channel_id=1, source_target_pairs={{0,1},{2,3},{4,5},{6,7},{1,0},{3,2},{5,4},{7,6},{8,9},{10,11},{12,... | collective-permute-start | bytes 49160 | tf_op jit(solution)/shard_map/ppermute | solution.py:306
  19.9 1.9 %shard_map.92 = (f32[4,16,384]{2,1,0:T(8,128)S(1)}, s32[8,1024]{1,0:T(8,128)S(1)}, s32[4,768]{1,0:T(4,128)S(1)}, f32[100,384]{1,0:T(8,128)S(1)}, f32[100,384]{1,...) custom-call(f32[100,1024]{1,0:T(8,128)S(1)} %get-tuple-element.52.state, ...), custom_call_target="tpu_custom_call" | custom-call | flops 1000000000 | bytes 1048576 | tf_op jit(solution)/shard_map/pallas_call | solution.py:296
  21.8 0.0 collective-permute-done.2.r2
  21.8 0.0 collective-permute-done.3.r3
  21.8 0.0 collective-permute-done.r0
  21.9 0.0 collective-permute-done.1.r1
  21.9 1.3 %shard_map.93 = (f32[100,384]{1,0:T(8,128)S(1)}, bf16[64,256]{1,0:T(8,128)(2,1)S(1)}, bf16[64,256]{1,0:T(8,128)(2,1)S(1)}, bf16[64,128]{1,0:T(8,128)(2,1)S(1)}, bf16[64,128]{1,0:T(8,128)(2,1)S(1)}) custom-call(bf16[64,256]{1,0:T(8,128)(2,1)S(1)} %collective-permute-done.r0, bf16[64,256]{1,0:T(8,128)(2,1)S(1)} %collective-permute-done.1.r1, ...), custom_call_target="tpu_custom_call" | custom-call | flops 1000000000 | bytes 1048576 | tf_op jit(solution)/shard_map/pallas_call | solution.py:296
  23.2 2.7 %collective-permute-start.4 = (bf16[64,256]{1,0:T(8,128)(2,1)S(1)}, bf16[64,256]{1,0:T(8,128)(2,1)S(1)}, u32[]{:S(2)}, u32[]{:S(2)}) collective-permute-start(bf16[64,256]{1,0:T(8,128)(2,1)S(1)} %get-tuple-element.67.o0), channel_id=1, source_target_pairs={{8,16},{24,32},{40,48},{56,64},{72,80},{88,96},{104,112},{120,128}... | collective-permute-start | bytes 98312 | tf_op jit(solution)/shard_map/ppermute | solution.py:306
  25.9 2.8 %collective-permute-start.5 = (bf16[64,256]{1,0:T(8,128)(2,1)S(1)}, bf16[64,256]{1,0:T(8,128)(2,1)S(1)}, u32[]{:S(2)}, u32[]{:S(2)}) collective-permute-start(bf16[64,256]{1,0:T(8,128)(2,1)S(1)} %get-tuple-element.68.o1), channel_id=1, source_target_pairs={{0,8},{16,24},{32,40},{48,56},{64,72},{80,88},{96,104},{112,120},{... | collective-permute-start | bytes 98312 | tf_op jit(solution)/shard_map/ppermute | solution.py:306
  28.7 3.5 %collective-permute-start.6 = (bf16[64,128]{1,0:T(8,128)(2,1)S(1)}, bf16[64,128]{1,0:T(8,128)(2,1)S(1)}, u32[]{:S(2)}, u32[]{:S(2)}) collective-permute-start(bf16[64,128]{1,0:T(8,128)(2,1)S(1)} %get-tuple-element.69.o2), channel_id=1, source_target_pairs={{1,2},{3,4},{5,6},{2,1},{4,3},{6,5},{9,10},{11,12},{13,14},{10,9},... | collective-permute-start | bytes 49160 | tf_op jit(solution)/shard_map/ppermute | solution.py:306
  32.2 1.9 %collective-permute-start.7 = (bf16[64,128]{1,0:T(8,128)(2,1)S(1)}, bf16[64,128]{1,0:T(8,128)(2,1)S(1)}, u32[]{:S(2)}, u32[]{:S(2)}) collective-permute-start(bf16[64,128]{1,0:T(8,128)(2,1)S(1)} %get-tuple-element.70.o3), channel_id=1, source_target_pairs={{0,1},{2,3},{4,5},{6,7},{1,0},{3,2},{5,4},{7,6},{8,9},{10,11},{12,... | collective-permute-start | bytes 49160 | tf_op jit(solution)/shard_map/ppermute | solution.py:306
  34.2 1.4 %shard_map.94 = (f32[100,1024]{1,0:T(8,128)S(1)}, f32[100,384]{1,0:T(8,128)S(1)}, f32[100,384]{1,0:T(8,128)S(1)}) custom-call(f32[100,1024]{1,0:T(8,128)S(1)} %get-tuple-element.52.state, f32[100,384]{1,0:T(8,128)S(1)} %get-tuple-element.71.delta, f32[4,16,384]{2,1,0:T(8,128)S(1)} %get-tuple-element.61.compact, s32[8,1024]{1,0:T(8,128)S(1)} %get-tuple-element.72.ranks, ...), custom_call_target="tpu_custom_call" | custom-call | flops 1000000000 | bytes 1048576 | tf_op jit(solution)/shard_map/pallas_call | solution.py:296
  35.5 0.0 collective-permute-done.6.r2
  35.5 0.0 collective-permute-done.7.r3
  35.5 0.0 collective-permute-done.4.r0
  35.6 0.0 collective-permute-done.5.r1
  35.6 1.3 %shard_map.95 = (f32[100,384]{1,0:T(8,128)S(1)}, bf16[64,256]{1,0:T(8,128)(2,1)S(1)}, bf16[64,256]{1,0:T(8,128)(2,1)S(1)}, bf16[64,128]{1,0:T(8,128)(2,1)S(1)}, bf16[64,128]{1,0:T(8,128)(2,1)S(1)}) custom-call(bf16[64,256]{1,0:T(8,128)(2,1)S(1)} %collective-permute-done.4.r0, bf16[64,256]{1,0:T(8,128)(2,1)S(1)} %collective-permute-done.5.r1, ...), custom_call_target="tpu_custom_call" | custom-call | flops 1000000000 | bytes 1048576 | tf_op jit(solution)/shard_map/pallas_call | solution.py:296
  36.9 5.0 %collective-permute-start.8 = (bf16[64,256]{1,0:T(8,128)(2,1)S(1)}, bf16[64,256]{1,0:T(8,128)(2,1)S(1)}, u32[]{:S(2)}, u32[]{:S(2)}) collective-permute-start(bf16[64,256]{1,0:T(8,128)(2,1)S(1)} %get-tuple-element.75.o0), channel_id=1, source_target_pairs={{8,16},{24,32},{40,48},{56,64},{72,80},{88,96},{104,112},{120,128}... | collective-permute-start | bytes 98312 | tf_op jit(solution)/shard_map/ppermute | solution.py:306
  41.8 1.9 %collective-permute-start.9 = (bf16[64,256]{1,0:T(8,128)(2,1)S(1)}, bf16[64,256]{1,0:T(8,128)(2,1)S(1)}, u32[]{:S(2)}, u32[]{:S(2)}) collective-permute-start(bf16[64,256]{1,0:T(8,128)(2,1)S(1)} %get-tuple-element.76.o1), channel_id=1, source_target_pairs={{0,8},{16,24},{32,40},{48,56},{64,72},{80,88},{96,104},{112,120},{... | collective-permute-start | bytes 98312 | tf_op jit(solution)/shard_map/ppermute | solution.py:306
  43.8 2.4 %collective-permute-start.10 = (bf16[64,128]{1,0:T(8,128)(2,1)S(1)}, bf16[64,128]{1,0:T(8,128)(2,1)S(1)}, u32[]{:S(2)}, u32[]{:S(2)}) collective-permute-start(bf16[64,128]{1,0:T(8,128)(2,1)S(1)} %get-tuple-element.77.o2), channel_id=1, source_target_pairs={{1,2},{3,4},{5,6},{2,1},{4,3},{6,5},{9,10},{11,12},{13,14},{10,9},... | collective-permute-start | bytes 49160 | tf_op jit(solution)/shard_map/ppermute | solution.py:306
  46.1 2.4 %collective-permute-start.11 = (bf16[64,128]{1,0:T(8,128)(2,1)S(1)}, bf16[64,128]{1,0:T(8,128)(2,1)S(1)}, u32[]{:S(2)}, u32[]{:S(2)}) collective-permute-start(bf16[64,128]{1,0:T(8,128)(2,1)S(1)} %get-tuple-element.78.o3), channel_id=1, source_target_pairs={{0,1},{2,3},{4,5},{6,7},{1,0},{3,2},{5,4},{7,6},{8,9},{10,11},{12,... | collective-permute-start | bytes 49160 | tf_op jit(solution)/shard_map/ppermute | solution.py:306
  48.5 1.4 %shard_map.96 = (f32[100,1024]{1,0:T(8,128)S(1)}, f32[100,384]{1,0:T(8,128)S(1)}, f32[100,384]{1,0:T(8,128)S(1)}) custom-call(f32[100,1024]{1,0:T(8,128)S(1)} %get-tuple-element.79.state, f32[100,384]{1,0:T(8,128)S(1)} %get-tuple-element.80.delta, f32[4,16,384]{2,1,0:T(8,128)S(1)} %get-tuple-element.61.compact, s32[8,1024]{1,0:T(8,128)S(1)} %get-tuple-element.72.ranks, ...), custom_call_target="tpu_custom_call" | custom-call | flops 1000000000 | bytes 1048576 | tf_op jit(solution)/shard_map/pallas_call | solution.py:296
  49.9 0.0 collective-permute-done.10.r2
  49.9 0.0 collective-permute-done.11.r3
  49.9 0.0 collective-permute-done.8.r0
  49.9 0.0 collective-permute-done.9.r1
  49.9 1.3 %shard_map.97 = (f32[100,384]{1,0:T(8,128)S(1)}, bf16[64,256]{1,0:T(8,128)(2,1)S(1)}, bf16[64,256]{1,0:T(8,128)(2,1)S(1)}, bf16[64,128]{1,0:T(8,128)(2,1)S(1)}, bf16[64,128]{1,0:T(8,128)(2,1)S(1)}) custom-call(bf16[64,256]{1,0:T(8,128)(2,1)S(1)} %collective-permute-done.8.r0, bf16[64,256]{1,0:T(8,128)(2,1)S(1)} %collective-permute-done.9.r1, ...), custom_call_target="tpu_custom_call" | custom-call | flops 1000000000 | bytes 1048576 | tf_op jit(solution)/shard_map/pallas_call | solution.py:296
  51.2 3.6 %collective-permute-start.12 = (bf16[64,256]{1,0:T(8,128)(2,1)S(1)}, bf16[64,256]{1,0:T(8,128)(2,1)S(1)}, u32[]{:S(2)}, u32[]{:S(2)}) collective-permute-start(bf16[64,256]{1,0:T(8,128)(2,1)S(1)} %get-tuple-element.83), channel_id=1, source_target_pairs={{8,16},{24,32},{40,48},{56,64},{72,80},{88,96},{104,112},{120,128}... | collective-permute-start | bytes 98312 | tf_op jit(solution)/shard_map/ppermute | solution.py:306
  54.9 1.9 %collective-permute-start.13 = (bf16[64,256]{1,0:T(8,128)(2,1)S(1)}, bf16[64,256]{1,0:T(8,128)(2,1)S(1)}, u32[]{:S(2)}, u32[]{:S(2)}) collective-permute-start(bf16[64,256]{1,0:T(8,128)(2,1)S(1)} %get-tuple-element.84), channel_id=1, source_target_pairs={{0,8},{16,24},{32,40},{48,56},{64,72},{80,88},{96,104},{112,120},{... | collective-permute-start | bytes 98312 | tf_op jit(solution)/shard_map/ppermute | solution.py:306
  56.8 3.0 %collective-permute-start.14 = (bf16[64,128]{1,0:T(8,128)(2,1)S(1)}, bf16[64,128]{1,0:T(8,128)(2,1)S(1)}, u32[]{:S(2)}, u32[]{:S(2)}) collective-permute-start(bf16[64,128]{1,0:T(8,128)(2,1)S(1)} %get-tuple-element.85), channel_id=1, source_target_pairs={{1,2},{3,4},{5,6},{2,1},{4,3},{6,5},{9,10},{11,12},{13,14},{10,9},... | collective-permute-start | bytes 49160 | tf_op jit(solution)/shard_map/ppermute | solution.py:306
  59.8 2.4 %collective-permute-start.15 = (bf16[64,128]{1,0:T(8,128)(2,1)S(1)}, bf16[64,128]{1,0:T(8,128)(2,1)S(1)}, u32[]{:S(2)}, u32[]{:S(2)}) collective-permute-start(bf16[64,128]{1,0:T(8,128)(2,1)S(1)} %get-tuple-element.86), channel_id=1, source_target_pairs={{0,1},{2,3},{4,5},{6,7},{1,0},{3,2},{5,4},{7,6},{8,9},{10,11},{12,... | collective-permute-start | bytes 49160 | tf_op jit(solution)/shard_map/ppermute | solution.py:306
  62.2 1.4 %shard_map.98 = (f32[100,1024]{1,0:T(8,128)S(1)}, f32[100,384]{1,0:T(8,128)S(1)}) custom-call(f32[100,1024]{1,0:T(8,128)S(1)} %get-tuple-element.87.state, f32[100,384]{1,0:T(8,128)S(1)} %get-tuple-element.88.delta, f32[4,16,384]{2,1,0:T(8,128)S(1)} %get-tuple-element.61.compact, s32[8,1024]{1,0:T(8,128)S(1)} %get-tuple-element.72.ranks, ...), custom_call_target="tpu_custom_call" | custom-call | flops 1000000000 | bytes 1048576 | tf_op jit(solution)/shard_map/pallas_call | solution.py:296
  63.6 0.0 collective-permute-done.14.r2
  63.6 0.0 collective-permute-done.15.r3
  63.6 0.0 collective-permute-done.12.r0
  63.6 0.0 collective-permute-done.13.r1
  63.6 2.0 %shard_map.99 = f32[100,1024]{1,0:T(8,128)} custom-call(bf16[64,256]{1,0:T(8,128)(2,1)S(1)} %collective-permute-done.12.r0, bf16[64,256]{1,0:T(8,128)(2,1)S(1)} %collective-permute-done.13.r1, bf16[64,128]{1,0:T(8,128)(2,1)S(1)} %collective-permute-done.14.r2, bf16[64,128]{1,0:T(8,128)(2,1)S(1)} %collective-permute-done.15.r3, ...), custom_call_target="tpu_custom_call" | custom-call | tf_op jit(solution)/shard_map/pallas_call | solution.py:375
Async XLA Ops:
  1.5 20.3 %collective-permute-start = (bf16[64,256]{1,0:T(8,128)(2,1)S(1)}, bf16[64,256]{1,0:T(8,128)(2,1)S(1)}, u32[]{:S(2)}, u32[]{:S(2)}) collective-permute-start(bf16[64,256]{1,0:T(8,128)(2,1)S(1)} %get-tuple-element.48.o0), channel_id=1, source_target_pairs={{8,16},{24,32},{40,48},{56,64},{72,80},{88,96},{104,112},{120,128}... | collective-permute-start | bytes 98312 | tf_op jit(solution)/shard_map/ppermute | solution.py:306
  12.1 9.8 %collective-permute-start.1 = (bf16[64,256]{1,0:T(8,128)(2,1)S(1)}, bf16[64,256]{1,0:T(8,128)(2,1)S(1)}, u32[]{:S(2)}, u32[]{:S(2)}) collective-permute-start(bf16[64,256]{1,0:T(8,128)(2,1)S(1)} %get-tuple-element.49.o1), channel_id=1, source_target_pairs={{0,8},{16,24},{32,40},{48,56},{64,72},{80,88},{96,104},{112,120},{... | collective-permute-start | bytes 98312 | tf_op jit(solution)/shard_map/ppermute | solution.py:306
  14.0 7.8 %collective-permute-start.2 = (bf16[64,128]{1,0:T(8,128)(2,1)S(1)}, bf16[64,128]{1,0:T(8,128)(2,1)S(1)}, u32[]{:S(2)}, u32[]{:S(2)}) collective-permute-start(bf16[64,128]{1,0:T(8,128)(2,1)S(1)} %get-tuple-element.50.o2), channel_id=1, source_target_pairs={{1,2},{3,4},{5,6},{2,1},{4,3},{6,5},{9,10},{11,12},{13,14},{10,9},... | collective-permute-start | bytes 49160 | tf_op jit(solution)/shard_map/ppermute | solution.py:306
  18.0 3.8 %collective-permute-start.3 = (bf16[64,128]{1,0:T(8,128)(2,1)S(1)}, bf16[64,128]{1,0:T(8,128)(2,1)S(1)}, u32[]{:S(2)}, u32[]{:S(2)}) collective-permute-start(bf16[64,128]{1,0:T(8,128)(2,1)S(1)} %get-tuple-element.51.o3), channel_id=1, source_target_pairs={{0,1},{2,3},{4,5},{6,7},{1,0},{3,2},{5,4},{7,6},{8,9},{10,11},{12,... | collective-permute-start | bytes 49160 | tf_op jit(solution)/shard_map/ppermute | solution.py:306
  23.2 12.4 %collective-permute-start.4 = (bf16[64,256]{1,0:T(8,128)(2,1)S(1)}, bf16[64,256]{1,0:T(8,128)(2,1)S(1)}, u32[]{:S(2)}, u32[]{:S(2)}) collective-permute-start(bf16[64,256]{1,0:T(8,128)(2,1)S(1)} %get-tuple-element.67.o0), channel_id=1, source_target_pairs={{8,16},{24,32},{40,48},{56,64},{72,80},{88,96},{104,112},{120,128}... | collective-permute-start | bytes 98312 | tf_op jit(solution)/shard_map/ppermute | solution.py:306
  25.9 9.7 %collective-permute-start.5 = (bf16[64,256]{1,0:T(8,128)(2,1)S(1)}, bf16[64,256]{1,0:T(8,128)(2,1)S(1)}, u32[]{:S(2)}, u32[]{:S(2)}) collective-permute-start(bf16[64,256]{1,0:T(8,128)(2,1)S(1)} %get-tuple-element.68.o1), channel_id=1, source_target_pairs={{0,8},{16,24},{32,40},{48,56},{64,72},{80,88},{96,104},{112,120},{... | collective-permute-start | bytes 98312 | tf_op jit(solution)/shard_map/ppermute | solution.py:306
  28.7 6.8 %collective-permute-start.6 = (bf16[64,128]{1,0:T(8,128)(2,1)S(1)}, bf16[64,128]{1,0:T(8,128)(2,1)S(1)}, u32[]{:S(2)}, u32[]{:S(2)}) collective-permute-start(bf16[64,128]{1,0:T(8,128)(2,1)S(1)} %get-tuple-element.69.o2), channel_id=1, source_target_pairs={{1,2},{3,4},{5,6},{2,1},{4,3},{6,5},{9,10},{11,12},{13,14},{10,9},... | collective-permute-start | bytes 49160 | tf_op jit(solution)/shard_map/ppermute | solution.py:306
  32.2 3.3 %collective-permute-start.7 = (bf16[64,128]{1,0:T(8,128)(2,1)S(1)}, bf16[64,128]{1,0:T(8,128)(2,1)S(1)}, u32[]{:S(2)}, u32[]{:S(2)}) collective-permute-start(bf16[64,128]{1,0:T(8,128)(2,1)S(1)} %get-tuple-element.70.o3), channel_id=1, source_target_pairs={{0,1},{2,3},{4,5},{6,7},{1,0},{3,2},{5,4},{7,6},{8,9},{10,11},{12,... | collective-permute-start | bytes 49160 | tf_op jit(solution)/shard_map/ppermute | solution.py:306
  36.9 13.1 %collective-permute-start.8 = (bf16[64,256]{1,0:T(8,128)(2,1)S(1)}, bf16[64,256]{1,0:T(8,128)(2,1)S(1)}, u32[]{:S(2)}, u32[]{:S(2)}) collective-permute-start(bf16[64,256]{1,0:T(8,128)(2,1)S(1)} %get-tuple-element.75.o0), channel_id=1, source_target_pairs={{8,16},{24,32},{40,48},{56,64},{72,80},{88,96},{104,112},{120,128}... | collective-permute-start | bytes 98312 | tf_op jit(solution)/shard_map/ppermute | solution.py:306
  41.8 8.1 %collective-permute-start.9 = (bf16[64,256]{1,0:T(8,128)(2,1)S(1)}, bf16[64,256]{1,0:T(8,128)(2,1)S(1)}, u32[]{:S(2)}, u32[]{:S(2)}) collective-permute-start(bf16[64,256]{1,0:T(8,128)(2,1)S(1)} %get-tuple-element.76.o1), channel_id=1, source_target_pairs={{0,8},{16,24},{32,40},{48,56},{64,72},{80,88},{96,104},{112,120},{... | collective-permute-start | bytes 98312 | tf_op jit(solution)/shard_map/ppermute | solution.py:306
  43.8 6.2 %collective-permute-start.10 = (bf16[64,128]{1,0:T(8,128)(2,1)S(1)}, bf16[64,128]{1,0:T(8,128)(2,1)S(1)}, u32[]{:S(2)}, u32[]{:S(2)}) collective-permute-start(bf16[64,128]{1,0:T(8,128)(2,1)S(1)} %get-tuple-element.77.o2), channel_id=1, source_target_pairs={{1,2},{3,4},{5,6},{2,1},{4,3},{6,5},{9,10},{11,12},{13,14},{10,9},... | collective-permute-start | bytes 49160 | tf_op jit(solution)/shard_map/ppermute | solution.py:306
  46.1 3.8 %collective-permute-start.11 = (bf16[64,128]{1,0:T(8,128)(2,1)S(1)}, bf16[64,128]{1,0:T(8,128)(2,1)S(1)}, u32[]{:S(2)}, u32[]{:S(2)}) collective-permute-start(bf16[64,128]{1,0:T(8,128)(2,1)S(1)} %get-tuple-element.78.o3), channel_id=1, source_target_pairs={{0,1},{2,3},{4,5},{6,7},{1,0},{3,2},{5,4},{7,6},{8,9},{10,11},{12,... | collective-permute-start | bytes 49160 | tf_op jit(solution)/shard_map/ppermute | solution.py:306
  51.2 12.4 %collective-permute-start.12 = (bf16[64,256]{1,0:T(8,128)(2,1)S(1)}, bf16[64,256]{1,0:T(8,128)(2,1)S(1)}, u32[]{:S(2)}, u32[]{:S(2)}) collective-permute-start(bf16[64,256]{1,0:T(8,128)(2,1)S(1)} %get-tuple-element.83), channel_id=1, source_target_pairs={{8,16},{24,32},{40,48},{56,64},{72,80},{88,96},{104,112},{120,128}... | collective-permute-start | bytes 98312 | tf_op jit(solution)/shard_map/ppermute | solution.py:306
  54.9 8.7 %collective-permute-start.13 = (bf16[64,256]{1,0:T(8,128)(2,1)S(1)}, bf16[64,256]{1,0:T(8,128)(2,1)S(1)}, u32[]{:S(2)}, u32[]{:S(2)}) collective-permute-start(bf16[64,256]{1,0:T(8,128)(2,1)S(1)} %get-tuple-element.84), channel_id=1, source_target_pairs={{0,8},{16,24},{32,40},{48,56},{64,72},{80,88},{96,104},{112,120},{... | collective-permute-start | bytes 98312 | tf_op jit(solution)/shard_map/ppermute | solution.py:306
  56.8 6.8 %collective-permute-start.14 = (bf16[64,128]{1,0:T(8,128)(2,1)S(1)}, bf16[64,128]{1,0:T(8,128)(2,1)S(1)}, u32[]{:S(2)}, u32[]{:S(2)}) collective-permute-start(bf16[64,128]{1,0:T(8,128)(2,1)S(1)} %get-tuple-element.85), channel_id=1, source_target_pairs={{1,2},{3,4},{5,6},{2,1},{4,3},{6,5},{9,10},{11,12},{13,14},{10,9},... | collective-permute-start | bytes 49160 | tf_op jit(solution)/shard_map/ppermute | solution.py:306
  59.8 3.8 %collective-permute-start.15 = (bf16[64,128]{1,0:T(8,128)(2,1)S(1)}, bf16[64,128]{1,0:T(8,128)(2,1)S(1)}, u32[]{:S(2)}, u32[]{:S(2)}) collective-permute-start(bf16[64,128]{1,0:T(8,128)(2,1)S(1)} %get-tuple-element.86), channel_id=1, source_target_pairs={{0,1},{2,3},{4,5},{6,7},{1,0},{3,2},{5,4},{7,6},{8,9},{10,11},{12,... | collective-permute-start | bytes 49160 | tf_op jit(solution)/shard_map/ppermute | solution.py:306

commit v2 on v1

--- a/solution.py
+++ b/solution.py
@@ -7,15 +7,16 @@
 from jax.experimental.pallas import tpu as pltpu
 from jax.sharding import PartitionSpec as P
 
-TAYLOR = 4
 TENT_SIZE = 16
 MAX_TENTS = 24
 MAX_LIVE = TENT_SIZE * MAX_TENTS
 ROWS = 64
 BLOCK = 256
+SPLIT = 256
 CHUNK = 512
 LANES = 128
 VMEM = 24 * 2**20
+POWER_ROWS = 112
 PHASES = (("wide", 1), ("narrow", 1), ("wide", 0), ("narrow", 0))
 BF16, F32, I32 = jnp.bfloat16, jnp.float32, jnp.int32
 
@@ -131,12 +132,17 @@
     copies = [pltpu.make_async_copy(src, dst, sems.at[i]) for i, (src, dst) in enumerate(zip(inputs, held))]
     for copy in copies:
         copy.start()
-    for copy in copies:
+    state, boundary, trace_op = held[:3]
+    copies[1].wait()
+    at = by_phase(row_of(boundary))
+    chosen, high = hot(low_of(at), BLOCK), high_of(at)
+    copies[2].wait()
+    face = face_rows(trace_op, 3).astype(BF16)
+    copies[0].wait()
+    traces = mm(face, state[...].astype(BF16)).astype(BF16)
+    store_blocks(choose(mm(stack(traces), chosen), high, 0, ROWS), blocks)
+    for copy in copies[3:]:
         copy.wait()
-    state, boundary, trace_op = held[:3]
-    traces = mm(face_rows(trace_op, 3).astype(BF16), state[...].astype(BF16)).astype(BF16)
-    at = by_phase(row_of(boundary))
-    store_blocks(pick(traces, low_of(at), high_of(at)), blocks)
 
 
 def make_index(neighbours, elem_tent, boundary, active, height, compact, ranks, sent):
@@ -188,11 +194,19 @@
             for b in range(count):
                 at = 16 * (m * count + b)
                 compact[l + m, :, b * LANES : (b + 1) * LANES] = found[at : at + 16, m * LANES : (m + 1) * LANES]
-
-
-def whole(compact, row, count=1):
-    rows = [compact[i : i + 1] for i in range(row, row + count)]
+            compact[l + m, 13:14, :LANES] = jnp.broadcast_to(offset[l + m : l + m + 1], (1, LANES))
+
+
+def whole(compact, row, count, here):
+    rows = [compact[i : i + 1, here] for i in range(row, row + count)]
     return (rows[0] if count == 1 else jnp.concatenate(rows, axis=1)).astype(I32)
+
+
+def many(compact):
+    return jnp.max(compact[13:14, :LANES]) > SPLIT
+
+
+FIRST, OTHERS = slice(0, SPLIT), slice(SPLIT, MAX_LIVE)
 
 
 def by_face(columns):
@@ -200,95 +214,134 @@
     return jnp.concatenate([columns[:, g * n : (g + 1) * n] for g in range(4)], axis=0)
 
 
-def local_part(values, compact, volume, lift, trace, base, kept):
+def local_part(values, compact, here, volume, lift, trace, base, kept):
     comps, elems = values.shape
     blocks = elems // BLOCK
+    count = here.stop - here.start
     parts, rows = two_parts(values)
     top = stack(parts[:rows])
-    low = jnp.concatenate([whole(compact, 11), whole(compact, 0, 4)], axis=1)
-    high = jnp.concatenate([whole(compact, 12), whole(compact, 4, 4)], axis=1)
+    low = jnp.concatenate([whole(compact, 11, 1, here), whole(compact, 0, 4, here)], axis=1)
+    high = jnp.concatenate([whole(compact, 12, 1, here), whole(compact, 4, 4, here)], axis=1)
     block, face = high & (blocks - 1), high // blocks
     near = []
     for at in range(0, low.shape[1], CHUNK):
-        here = slice(at, at + CHUNK)
-        near.append(choose(mm(top, hot(low[:, here], BLOCK)), block[:, here], 0, rows)[:comps].astype(BF16))
+        now = slice(at, at + CHUNK)
+        near.append(choose(mm(top, hot(low[:, now], BLOCK)), block[:, now], 0, rows)[:comps].astype(BF16))
     near = jnp.concatenate(near, axis=1)
-    mine, near, face = near[:, :MAX_LIVE], near[:, MAX_LIVE:], face[:, MAX_LIVE:]
+    mine, near, face = near[:, :count], near[:, count:], face[:, count:]
     picked = []
     for at in range(0, near.shape[1], CHUNK):
-        here = slice(at, at + CHUNK)
-        picked.append(choose(mm(trace[...], near[:, here]), face[:, here], 0, ROWS, 0.0))
+        now = slice(at, at + CHUNK)
+        picked.append(choose(mm(trace[...], near[:, now]), face[:, now], 0, ROWS, 0.0))
     picked = by_face(jnp.concatenate(picked, axis=1)).astype(BF16)
     if kept is not None:
         rest = stack(jnp.concatenate([parts[rows:].astype(F32), jnp.zeros((rows - comps, elems), F32)], axis=0))
-        own = slice(0, MAX_LIVE)
-        rest = choose(mm(rest.astype(BF16), hot(low[:, own], BLOCK)), block[:, own], 0, rows)
-        kept[...] = mine.astype(F32) + rest[:comps]
-    base[...] = mm(volume[...], mine) + mm(lift[...], picked)
+        rest = choose(mm(rest.astype(BF16), hot(low[:, :count], BLOCK)), block[:, :count], 0, rows)
+        kept[:, here] = mine.astype(F32) + rest[:comps]
+    base[:, here] = mm(volume[...], mine) + mm(lift[...], picked)
+
+
+def local_parts(values, compact, *refs):
+    local_part(values[...], compact, FIRST, *refs)
+
+    @pl.when(many(compact))
+    def _():
+        local_part(values[...], compact, OTHERS, *refs)
 
 
 def local_first_kernel(
     state, neighbours, elem_tent, boundary, active, height, volume, lift_op, trace_op,
-    compact, ranks, sent, base, kept, lift, trace,
+    compact, ranks, sent, base, kept, lift, trace, powers,
 ):
+    powers[...] = powers_of(volume[...])
     make_index(neighbours, elem_tent, boundary, active, height, compact, ranks, sent)
     lifts = jnp.concatenate([face_rows(lift_op, g) for g in range(4)], axis=0).astype(BF16)
     comps = lifts.shape[1]
     diagonal = lax.broadcasted_iota(I32, (comps, comps), 0) == lax.broadcasted_iota(I32, (comps, comps), 1)
     lift[...] = mm_t(jnp.where(diagonal, 1.0, 0.0).astype(BF16), lifts).astype(BF16)
     trace[...] = jnp.concatenate([face_rows(trace_op, g) for g in range(4)], axis=0).astype(BF16)
-    local_part(state[...], compact[0], volume, lift, trace, base, kept)
-
-
-def scatter(delta, rank):
+    local_parts(state, compact[0], volume, lift, trace, base, kept)
+
+
+def scatter(delta, rank, here):
     parts, second = two_parts(delta)
-    found = mm(parts, hot(rank, MAX_LIVE))
+    found = mm(parts, hot(rank - here.start, delta.shape[1]))
     return found[: delta.shape[0]] + found[second:]
 
 
 def local_kernel(layer, state, delta, compact, ranks, volume, lift, trace, new_state, base, kept=None):
-    values = state[...] + scatter(delta[...], ranks[layer - 1 : layer])
-    new_state[...] = values
-    local_part(values, compact[layer], volume, lift, trace, base, kept)
-
-
-def taylor_terms(received, compact, base, volume, lift):
+    rank = ranks[layer - 1 : layer]
+    new_state[...] = state[...] + scatter(delta[:, FIRST], rank, FIRST)
+
+    @pl.when(many(compact[layer - 1]))
+    def _():
+        new_state[...] = new_state[...] + scatter(delta[:, OTHERS], rank, OTHERS)
+
+    local_parts(new_state, compact[layer], volume, lift, trace, base, kept)
+
+
+def powers_of(volume):
+    gap = jnp.zeros((POWER_ROWS - volume.shape[0], volume.shape[1]), F32)
+    parts = [volume.astype(F32)]
+    for _ in range(2):
+        power = sum(mm(part.astype(BF16), volume) for part in parts[-2:])
+        top = power.astype(BF16).astype(F32)
+        parts += [top, power - top]
+    return jnp.concatenate([half for part in parts for half in (part, gap)], axis=0).astype(BF16)
+
+
+def taylor_terms(received, compact, here, base, powers, lift):
     remote = jnp.concatenate([ref[...] for ref in received], axis=1)
     first_block = 4 * 1024 // BLOCK
-    picked = by_face(pick(remote, whole(compact, 0, 4), whole(compact, 4, 4), first_block)).astype(BF16)
-    heights = compact[8:9] + compact[9:10] + compact[10:11]
-    term = heights * (base[...] + mm(lift[...], picked))
-    total = term
-    for order in range(2, TAYLOR + 1):
-        term = (heights / order) * mm(volume[...], term.astype(BF16))
-        total = total + term
+    picked = by_face(pick(remote, whole(compact, 0, 4, here), whole(compact, 4, 4, here), first_block)).astype(BF16)
+    heights = compact[8:9, here] + compact[9:10, here] + compact[10:11, here]
+    first = heights * (base[:, here] + mm(lift[...], picked))
+    found = mm(powers[...], first.astype(BF16))
+    comps = first.shape[0]
+    products = [found[at : at + comps] for at in range(0, found.shape[0], POWER_ROWS)]
+    total, scale = first, 1.0
+    for order, product in ((2, products[0]), (3, products[1] + products[2]), (4, products[3] + products[4])):
+        scale = scale * (heights / order)
+        total = total + scale * product
     return total
 
 
-def advance_kernel(layer, r0, r1, r2, r3, o0, o1, o2, o3, compact, base, kept, sent, volume, lift, trace, delta, *outgoing):
-    total = taylor_terms((r0, r1, r2, r3), compact[layer], base, volume, lift)
-    delta[...] = total
-    traces = mm(trace[3 * ROWS :, :], (kept[...] + total).astype(BF16))
-    rest = -MAX_LIVE % BLOCK
-    table = jnp.concatenate([traces, jnp.zeros((ROWS, rest), F32)], axis=1).astype(BF16)
-    place = sent[layer : layer + 1]
-    found = pick(table, low_of(place), high_of(place))
-    before = jnp.concatenate([o0[...], o1[...], o2[...], o3[...]], axis=1).astype(F32)
-    store_blocks(jnp.where(place >= 0, found, before), outgoing)
-
-
-def last_kernel(layer, r0, r1, r2, r3, compact, base, ranks, volume, lift, state, advanced, held, sems):
-    parts, second = two_parts(taylor_terms((r0, r1, r2, r3), compact[layer], base, volume, lift))
-    comps, elems = state.shape
-    copies = []
-    for c in range(elems // BLOCK):
-        here = slice(c * BLOCK, (c + 1) * BLOCK)
-        found = mm(parts, hot(ranks[layer : layer + 1, here], MAX_LIVE))
-        held[:, here] = state[:, here] + found[:comps] + found[second:]
-        copies.append(pltpu.make_async_copy(held.at[:, here], advanced.at[:, here], sems.at[c]))
-        copies[-1].start()
-    for copy in copies:
-        copy.wait()
+def advance_kernel(layer, r0, r1, r2, r3, o0, o1, o2, o3, compact, base, kept, sent, powers, lift, trace, delta, *outgoing):
+    rows = compact[layer]
+
+    def part(here, before):
+        place = sent[layer : layer + 1] - here.start
+        chosen = hot(place, here.stop - here.start)
+        total = taylor_terms((r0, r1, r2, r3), rows, here, base, powers, lift)
+        delta[:, here] = total
+        traces = mm(trace[3 * ROWS :, :], (kept[:, here] + total).astype(BF16)).astype(BF16)
+        before = jnp.concatenate([ref[...] for ref in before], axis=1).astype(F32)
+        inside = jnp.logical_and(place >= 0, place < here.stop - here.start)
+        store_blocks(jnp.where(inside, mm(traces, chosen), before), outgoing)
+
+    part(FIRST, (o0, o1, o2, o3))
+
+    @pl.when(many(rows))
+    def _():
+        part(OTHERS, outgoing)
+
+
+def last_kernel(layer, r0, r1, r2, r3, compact, base, ranks, powers, lift, state, advanced, held, sem):
+    rows, rank = compact[layer], ranks[layer : layer + 1]
+
+    def part(here, before):
+        total = taylor_terms((r0, r1, r2, r3), rows, here, base, powers, lift)
+        held[...] = before[...] + scatter(total, rank, here)
+
+    part(FIRST, state)
+
+    @pl.when(many(rows))
+    def _():
+        part(OTHERS, held)
+
+    copy = pltpu.make_async_copy(held, advanced, sem)
+    copy.start()
+    copy.wait()
 
 
 def call(kernel, outs, args, flops):
@@ -343,7 +396,7 @@
     outgoing = outs[:4]
     state, boundary, trace, neighbours, elem_tent, active, tent_height, volume_op, lift = outs[4:]
     received = exchange(outgoing)
-    compact, ranks, sent, base, kept, lift, trace = call(
+    compact, ranks, sent, base, kept, lift, trace, powers = call(
         local_first_kernel,
         [
             ((layers, 16, MAX_LIVE), F32),
@@ -353,6 +406,7 @@
             live,
             ((comps, 4 * ROWS), BF16),
             ((4 * ROWS, comps), BF16),
+            ((5 * POWER_ROWS, comps), BF16),
         ],
         (state, neighbours, elem_tent, boundary, active, tent_height, volume_op, lift, trace),
         10**9,
@@ -361,7 +415,7 @@
         delta, *outgoing = call(
             functools.partial(advance_kernel, layer),
             [live] + blocks,
-            (*received, *outgoing, compact, base, kept, sent, volume_op, lift, trace),
+            (*received, *outgoing, compact, base, kept, sent, powers, lift, trace),
             10**9,
         )
         received = exchange(outgoing)
@@ -376,9 +430,9 @@
         functools.partial(last_kernel, layers - 1),
         out_specs=pl.BlockSpec(memory_space=pltpu.MemorySpace.HBM),
         out_shape=jax.ShapeDtypeStruct((comps, elems), F32),
-        scratch_shapes=[pltpu.VMEM((comps, elems), F32), pltpu.SemaphoreType.DMA((elems // BLOCK,))],
+        scratch_shapes=[pltpu.VMEM((comps, elems), F32), pltpu.SemaphoreType.DMA],
         compiler_params=pltpu.CompilerParams(vmem_limit_bytes=VMEM),
-    )(*received, compact, base, ranks, volume_op, lift, state)
+    )(*received, compact, base, ranks, powers, lift, state)
 
 
 def solution(mesh):

time: 66.2 us -> 64.7 us (0.977)
  the two profiles are of different devices: /device:TPU:35 before, /device:TPU:11 now
where the time goes in v2:
time: 64.7 us; the launch traced here: 64.2 us
  starting transfers between devices  52.1 us (81%)
  Pallas kernels  11.8 us (18%)
    ppermute x16, starting transfers between devices, swapped(): return lax.ppermute(block, axis, pairs + [(j, i) for i, j in pairs])  52.1 us
    pallas_call x7, Pallas kernels, call(): pl.pallas_call(kernel, out_shape=outs, compiler_params=pltpu.CompilerPara...  8.56 us
    pallas_call x1, Pallas kernels, local(): pl.pallas_call(functools.partial(last_kernel, layers - 1), out_specs=pl.B...  1.76 us
    pallas_call x1, Pallas kernels, local(): pl.pallas_call(first_kernel, in_specs=[pl.BlockSpec(memory_space=pltpu.Me...  1.48 us
  transfers between devices with their start and end apart: 16, of which 0 were waited for; matrix products, arithmetic and copies ran while one was open for 0% of the time, Pallas kernels for 8%

profile of v2, /device:TPU:11, one launch (start us, length us, event | category | flops | bytes accessed | tf_op | source)
XLA Modules:
  0.0 64.2 jit_solution(14938564944783458797)
XLA Ops:
  0.0 1.5 %shard_map.91 = (bf16[64,256]{1,0:T(8,128)(2,1)S(1)}, bf16[64,256]{1,0:T(8,128)(2,1)S(1)}, bf16[64,128]{1,0:T(8,128)(2,1)S(1)}, bf16[64,128]{1,0:T(8,128)(2,1)S(...) custom-call(f32[100,1024]{1,0:T(8,128)} %refs_0_.1, ...), custom_call_target="tpu_custom_call" | custom-call | tf_op jit(solution)/shard_map/pallas_call | solution.py:389
  1.5 10.6 %collective-permute-start = (bf16[64,256]{1,0:T(8,128)(2,1)S(1)}, bf16[64,256]{1,0:T(8,128)(2,1)S(1)}, u32[]{:S(2)}, u32[]{:S(2)}) collective-permute-start(bf16[64,256]{1,0:T(8,128)(2,1)S(1)} %get-tuple-element.49.o0), channel_id=1, source_target_pairs={{8,16},{24,32},{40,48},{56,64},{72,80},{88,96},{104,112},{120,128}... | collective-permute-start | bytes 98312 | tf_op jit(solution)/shard_map/ppermute | solution.py:359
  12.1 1.9 %collective-permute-start.1 = (bf16[64,256]{1,0:T(8,128)(2,1)S(1)}, bf16[64,256]{1,0:T(8,128)(2,1)S(1)}, u32[]{:S(2)}, u32[]{:S(2)}) collective-permute-start(bf16[64,256]{1,0:T(8,128)(2,1)S(1)} %get-tuple-element.50.o1), channel_id=1, source_target_pairs={{0,8},{16,24},{32,40},{48,56},{64,72},{80,88},{96,104},{112,120},{... | collective-permute-start | bytes 98312 | tf_op jit(solution)/shard_map/ppermute | solution.py:359
  14.0 4.0 %collective-permute-start.2 = (bf16[64,128]{1,0:T(8,128)(2,1)S(1)}, bf16[64,128]{1,0:T(8,128)(2,1)S(1)}, u32[]{:S(2)}, u32[]{:S(2)}) collective-permute-start(bf16[64,128]{1,0:T(8,128)(2,1)S(1)} %get-tuple-element.51.o2), channel_id=1, source_target_pairs={{1,2},{3,4},{5,6},{2,1},{4,3},{6,5},{9,10},{11,12},{13,14},{10,9},... | collective-permute-start | bytes 49160 | tf_op jit(solution)/shard_map/ppermute | solution.py:359
  18.0 1.9 %collective-permute-start.3 = (bf16[64,128]{1,0:T(8,128)(2,1)S(1)}, bf16[64,128]{1,0:T(8,128)(2,1)S(1)}, u32[]{:S(2)}, u32[]{:S(2)}) collective-permute-start(bf16[64,128]{1,0:T(8,128)(2,1)S(1)} %get-tuple-element.52.o3), channel_id=1, source_target_pairs={{0,1},{2,3},{4,5},{6,7},{1,0},{3,2},{5,4},{7,6},{8,9},{10,11},{12,... | collective-permute-start | bytes 49160 | tf_op jit(solution)/shard_map/ppermute | solution.py:359
  19.9 1.8 %shard_map.92 = (f32[4,16,384]{2,1,0:T(8,128)S(1)}, s32[8,1024]{1,0:T(8,128)S(1)}, s32[4,768]{1,0:T(4,128)S(1)}, f32[100,384]{1,0:T(8,128)S(1)}, f32[100,384]{1,...) custom-call(f32[100,1024]{1,0:T(8,128)S(1)} %get-tuple-element.53.state, ...), custom_call_target="tpu_custom_call" | custom-call | flops 1000000000 | bytes 1048576 | tf_op jit(solution)/shard_map/pallas_call | solution.py:349
  21.7 0.0 collective-permute-done.2.r2
  21.7 0.0 collective-permute-done.3.r3
  21.7 0.0 collective-permute-done.r0
  21.7 0.0 collective-permute-done.1.r1
  21.7 1.0 %shard_map.93 = (f32[100,384]{1,0:T(8,128)S(1)}, bf16[64,256]{1,0:T(8,128)(2,1)S(1)}, bf16[64,256]{1,0:T(8,128)(2,1)S(1)}, bf16[64,128]{1,0:T(8,128)(2,1)S(1)}, bf16[64,128]{1,0:T(8,128)(2,1)S(1)}) custom-call(bf16[64,256]{1,0:T(8,128)(2,1)S(1)} %collective-permute-done.r0, bf16[64,256]{1,0:T(8,128)(2,1)S(1)} %collective-permute-done.1.r1, ...), custom_call_target="tpu_custom_call" | custom-call | flops 1000000000 | bytes 1048576 | tf_op jit(solution)/shard_map/pallas_call | solution.py:349
  22.8 2.7 %collective-permute-start.4 = (bf16[64,256]{1,0:T(8,128)(2,1)S(1)}, bf16[64,256]{1,0:T(8,128)(2,1)S(1)}, u32[]{:S(2)}, u32[]{:S(2)}) collective-permute-start(bf16[64,256]{1,0:T(8,128)(2,1)S(1)} %get-tuple-element.69.o0), channel_id=1, source_target_pairs={{8,16},{24,32},{40,48},{56,64},{72,80},{88,96},{104,112},{120,128}... | collective-permute-start | bytes 98312 | tf_op jit(solution)/shard_map/ppermute | solution.py:359
  25.5 2.8 %collective-permute-start.5 = (bf16[64,256]{1,0:T(8,128)(2,1)S(1)}, bf16[64,256]{1,0:T(8,128)(2,1)S(1)}, u32[]{:S(2)}, u32[]{:S(2)}) collective-permute-start(bf16[64,256]{1,0:T(8,128)(2,1)S(1)} %get-tuple-element.70.o1), channel_id=1, source_target_pairs={{0,8},{16,24},{32,40},{48,56},{64,72},{80,88},{96,104},{112,120},{... | collective-permute-start | bytes 98312 | tf_op jit(solution)/shard_map/ppermute | solution.py:359
  28.3 3.5 %collective-permute-start.6 = (bf16[64,128]{1,0:T(8,128)(2,1)S(1)}, bf16[64,128]{1,0:T(8,128)(2,1)S(1)}, u32[]{:S(2)}, u32[]{:S(2)}) collective-permute-start(bf16[64,128]{1,0:T(8,128)(2,1)S(1)} %get-tuple-element.71.o2), channel_id=1, source_target_pairs={{1,2},{3,4},{5,6},{2,1},{4,3},{6,5},{9,10},{11,12},{13,14},{10,9},... | collective-permute-start | bytes 49160 | tf_op jit(solution)/shard_map/ppermute | solution.py:359
  31.8 1.9 %collective-permute-start.7 = (bf16[64,128]{1,0:T(8,128)(2,1)S(1)}, bf16[64,128]{1,0:T(8,128)(2,1)S(1)}, u32[]{:S(2)}, u32[]{:S(2)}) collective-permute-start(bf16[64,128]{1,0:T(8,128)(2,1)S(1)} %get-tuple-element.72.o3), channel_id=1, source_target_pairs={{0,1},{2,3},{4,5},{6,7},{1,0},{3,2},{5,4},{7,6},{8,9},{10,11},{12,... | collective-permute-start | bytes 49160 | tf_op jit(solution)/shard_map/ppermute | solution.py:359
  33.8 1.2 %shard_map.94 = (f32[100,1024]{1,0:T(8,128)S(1)}, f32[100,384]{1,0:T(8,128)S(1)}, f32[100,384]{1,0:T(8,128)S(1)}) custom-call(f32[100,1024]{1,0:T(8,128)S(1)} %get-tuple-element.53.state, f32[100,384]{1,0:T(8,128)S(1)} %get-tuple-element.73.delta, f32[4,16,384]{2,1,0:T(8,128)S(1)} %get-tuple-element.62.compact, s32[8,1024]{1,0:T(8,128)S(1)} %get-tuple-element.74.ranks, ...), custom_call_target="tpu_custom_call" | custom-call | flops 1000000000 | bytes 1048576 | tf_op jit(solution)/shard_map/pallas_call | solution.py:349
  35.0 0.0 collective-permute-done.6.r2
  35.0 0.0 collective-permute-done.7.r3
  35.0 0.0 collective-permute-done.4.r0
  35.0 0.0 collective-permute-done.5.r1
  35.0 1.0 %shard_map.95 = (f32[100,384]{1,0:T(8,128)S(1)}, bf16[64,256]{1,0:T(8,128)(2,1)S(1)}, bf16[64,256]{1,0:T(8,128)(2,1)S(1)}, bf16[64,128]{1,0:T(8,128)(2,1)S(1)}, bf16[64,128]{1,0:T(8,128)(2,1)S(1)}) custom-call(bf16[64,256]{1,0:T(8,128)(2,1)S(1)} %collective-permute-done.4.r0, bf16[64,256]{1,0:T(8,128)(2,1)S(1)} %collective-permute-done.5.r1, ...), custom_call_target="tpu_custom_call" | custom-call | flops 1000000000 | bytes 1048576 | tf_op jit(solution)/shard_map/pallas_call | solution.py:349
  36.1 3.7 %collective-permute-start.8 = (bf16[64,256]{1,0:T(8,128)(2,1)S(1)}, bf16[64,256]{1,0:T(8,128)(2,1)S(1)}, u32[]{:S(2)}, u32[]{:S(2)}) collective-permute-start(bf16[64,256]{1,0:T(8,128)(2,1)S(1)} %get-tuple-element.77.o0), channel_id=1, source_target_pairs={{8,16},{24,32},{40,48},{56,64},{72,80},{88,96},{104,112},{120,128}... | collective-permute-start | bytes 98312 | tf_op jit(solution)/shard_map/ppermute | solution.py:359
  39.8 2.2 %collective-permute-start.9 = (bf16[64,256]{1,0:T(8,128)(2,1)S(1)}, bf16[64,256]{1,0:T(8,128)(2,1)S(1)}, u32[]{:S(2)}, u32[]{:S(2)}) collective-permute-start(bf16[64,256]{1,0:T(8,128)(2,1)S(1)} %get-tuple-element.78.o1), channel_id=1, source_target_pairs={{0,8},{16,24},{32,40},{48,56},{64,72},{80,88},{96,104},{112,120},{... | collective-permute-start | bytes 98312 | tf_op jit(solution)/shard_map/ppermute | solution.py:359
  42.0 2.5 %collective-permute-start.10 = (bf16[64,128]{1,0:T(8,128)(2,1)S(1)}, bf16[64,128]{1,0:T(8,128)(2,1)S(1)}, u32[]{:S(2)}, u32[]{:S(2)}) collective-permute-start(bf16[64,128]{1,0:T(8,128)(2,1)S(1)} %get-tuple-element.79.o2), channel_id=1, source_target_pairs={{1,2},{3,4},{5,6},{2,1},{4,3},{6,5},{9,10},{11,12},{13,14},{10,9},... | collective-permute-start | bytes 49160 | tf_op jit(solution)/shard_map/ppermute | solution.py:359
  44.5 2.4 %collective-permute-start.11 = (bf16[64,128]{1,0:T(8,128)(2,1)S(1)}, bf16[64,128]{1,0:T(8,128)(2,1)S(1)}, u32[]{:S(2)}, u32[]{:S(2)}) collective-permute-start(bf16[64,128]{1,0:T(8,128)(2,1)S(1)} %get-tuple-element.80.o3), channel_id=1, source_target_pairs={{0,1},{2,3},{4,5},{6,7},{1,0},{3,2},{5,4},{7,6},{8,9},{10,11},{12,... | collective-permute-start | bytes 49160 | tf_op jit(solution)/shard_map/ppermute | solution.py:359
  46.9 1.2 %shard_map.96 = (f32[100,1024]{1,0:T(8,128)S(1)}, f32[100,384]{1,0:T(8,128)S(1)}, f32[100,384]{1,0:T(8,128)S(1)}) custom-call(f32[100,1024]{1,0:T(8,128)S(1)} %get-tuple-element.81.state, f32[100,384]{1,0:T(8,128)S(1)} %get-tuple-element.82.delta, f32[4,16,384]{2,1,0:T(8,128)S(1)} %get-tuple-element.62.compact, s32[8,1024]{1,0:T(8,128)S(1)} %get-tuple-element.74.ranks, ...), custom_call_target="tpu_custom_call" | custom-call | flops 1000000000 | bytes 1048576 | tf_op jit(solution)/shard_map/pallas_call | solution.py:349
  48.2 0.0 collective-permute-done.10.r2
  48.2 0.0 collective-permute-done.11.r3
  48.2 0.0 collective-permute-done.8.r0
  48.2 0.0 collective-permute-done.9.r1
  48.2 1.0 %shard_map.97 = (f32[100,384]{1,0:T(8,128)S(1)}, bf16[64,256]{1,0:T(8,128)(2,1)S(1)}, bf16[64,256]{1,0:T(8,128)(2,1)S(1)}, bf16[64,128]{1,0:T(8,128)(2,1)S(1)}, bf16[64,128]{1,0:T(8,128)(2,1)S(1)}) custom-call(bf16[64,256]{1,0:T(8,128)(2,1)S(1)} %collective-permute-done.8.r0, bf16[64,256]{1,0:T(8,128)(2,1)S(1)} %collective-permute-done.9.r1, ...), custom_call_target="tpu_custom_call" | custom-call | flops 1000000000 | bytes 1048576 | tf_op jit(solution)/shard_map/pallas_call | solution.py:349
  49.2 3.2 %collective-permute-start.12 = (bf16[64,256]{1,0:T(8,128)(2,1)S(1)}, bf16[64,256]{1,0:T(8,128)(2,1)S(1)}, u32[]{:S(2)}, u32[]{:S(2)}) collective-permute-start(bf16[64,256]{1,0:T(8,128)(2,1)S(1)} %get-tuple-element.85), channel_id=1, source_target_pairs={{8,16},{24,32},{40,48},{56,64},{72,80},{88,96},{104,112},{120,128}... | collective-permute-start | bytes 98312 | tf_op jit(solution)/shard_map/ppermute | solution.py:359
  52.5 3.1 %collective-permute-start.13 = (bf16[64,256]{1,0:T(8,128)(2,1)S(1)}, bf16[64,256]{1,0:T(8,128)(2,1)S(1)}, u32[]{:S(2)}, u32[]{:S(2)}) collective-permute-start(bf16[64,256]{1,0:T(8,128)(2,1)S(1)} %get-tuple-element.86), channel_id=1, source_target_pairs={{0,8},{16,24},{32,40},{48,56},{64,72},{80,88},{96,104},{112,120},{... | collective-permute-start | bytes 98312 | tf_op jit(solution)/shard_map/ppermute | solution.py:359
  55.6 1.9 %collective-permute-start.14 = (bf16[64,128]{1,0:T(8,128)(2,1)S(1)}, bf16[64,128]{1,0:T(8,128)(2,1)S(1)}, u32[]{:S(2)}, u32[]{:S(2)}) collective-permute-start(bf16[64,128]{1,0:T(8,128)(2,1)S(1)} %get-tuple-element.87), channel_id=1, source_target_pairs={{1,2},{3,4},{5,6},{2,1},{4,3},{6,5},{9,10},{11,12},{13,14},{10,9},... | collective-permute-start | bytes 49160 | tf_op jit(solution)/shard_map/ppermute | solution.py:359
  57.6 3.6 %collective-permute-start.15 = (bf16[64,128]{1,0:T(8,128)(2,1)S(1)}, bf16[64,128]{1,0:T(8,128)(2,1)S(1)}, u32[]{:S(2)}, u32[]{:S(2)}) collective-permute-start(bf16[64,128]{1,0:T(8,128)(2,1)S(1)} %get-tuple-element.88), channel_id=1, source_target_pairs={{0,1},{2,3},{4,5},{6,7},{1,0},{3,2},{5,4},{7,6},{8,9},{10,11},{12,... | collective-permute-start | bytes 49160 | tf_op jit(solution)/shard_map/ppermute | solution.py:359
  61.2 1.2 %shard_map.98 = (f32[100,1024]{1,0:T(8,128)S(1)}, f32[100,384]{1,0:T(8,128)S(1)}) custom-call(f32[100,1024]{1,0:T(8,128)S(1)} %get-tuple-element.89.state, f32[100,384]{1,0:T(8,128)S(1)} %get-tuple-element.90.delta, f32[4,16,384]{2,1,0:T(8,128)S(1)} %get-tuple-element.62.compact, s32[8,1024]{1,0:T(8,128)S(1)} %get-tuple-element.74.ranks, ...), custom_call_target="tpu_custom_call" | custom-call | flops 1000000000 | bytes 1048576 | tf_op jit(solution)/shard_map/pallas_call | solution.py:349
  62.4 0.0 collective-permute-done.14.r2
  62.4 0.0 collective-permute-done.15.r3
  62.4 0.0 collective-permute-done.12.r0
  62.5 0.0 collective-permute-done.13.r1
  62.5 1.8 %shard_map.99 = f32[100,1024]{1,0:T(8,128)} custom-call(bf16[64,256]{1,0:T(8,128)(2,1)S(1)} %collective-permute-done.12.r0, bf16[64,256]{1,0:T(8,128)(2,1)S(1)} %collective-permute-done.13.r1, bf16[64,128]{1,0:T(8,128)(2,1)S(1)} %collective-permute-done.14.r2, bf16[64,128]{1,0:T(8,128)(2,1)S(1)} %collective-permute-done.15.r3, ...), custom_call_target="tpu_custom_call" | custom-call | tf_op jit(solution)/shard_map/pallas_call | solution.py:429
Async XLA Ops:
  1.5 20.2 %collective-permute-start = (bf16[64,256]{1,0:T(8,128)(2,1)S(1)}, bf16[64,256]{1,0:T(8,128)(2,1)S(1)}, u32[]{:S(2)}, u32[]{:S(2)}) collective-permute-start(bf16[64,256]{1,0:T(8,128)(2,1)S(1)} %get-tuple-element.49.o0), channel_id=1, source_target_pairs={{8,16},{24,32},{40,48},{56,64},{72,80},{88,96},{104,112},{120,128}... | collective-permute-start | bytes 98312 | tf_op jit(solution)/shard_map/ppermute | solution.py:359
  12.1 9.7 %collective-permute-start.1 = (bf16[64,256]{1,0:T(8,128)(2,1)S(1)}, bf16[64,256]{1,0:T(8,128)(2,1)S(1)}, u32[]{:S(2)}, u32[]{:S(2)}) collective-permute-start(bf16[64,256]{1,0:T(8,128)(2,1)S(1)} %get-tuple-element.50.o1), channel_id=1, source_target_pairs={{0,8},{16,24},{32,40},{48,56},{64,72},{80,88},{96,104},{112,120},{... | collective-permute-start | bytes 98312 | tf_op jit(solution)/shard_map/ppermute | solution.py:359
  14.0 7.7 %collective-permute-start.2 = (bf16[64,128]{1,0:T(8,128)(2,1)S(1)}, bf16[64,128]{1,0:T(8,128)(2,1)S(1)}, u32[]{:S(2)}, u32[]{:S(2)}) collective-permute-start(bf16[64,128]{1,0:T(8,128)(2,1)S(1)} %get-tuple-element.51.o2), channel_id=1, source_target_pairs={{1,2},{3,4},{5,6},{2,1},{4,3},{6,5},{9,10},{11,12},{13,14},{10,9},... | collective-permute-start | bytes 49160 | tf_op jit(solution)/shard_map/ppermute | solution.py:359
  18.0 3.7 %collective-permute-start.3 = (bf16[64,128]{1,0:T(8,128)(2,1)S(1)}, bf16[64,128]{1,0:T(8,128)(2,1)S(1)}, u32[]{:S(2)}, u32[]{:S(2)}) collective-permute-start(bf16[64,128]{1,0:T(8,128)(2,1)S(1)} %get-tuple-element.52.o3), channel_id=1, source_target_pairs={{0,1},{2,3},{4,5},{6,7},{1,0},{3,2},{5,4},{7,6},{8,9},{10,11},{12,... | collective-permute-start | bytes 49160 | tf_op jit(solution)/shard_map/ppermute | solution.py:359
  22.8 12.3 %collective-permute-start.4 = (bf16[64,256]{1,0:T(8,128)(2,1)S(1)}, bf16[64,256]{1,0:T(8,128)(2,1)S(1)}, u32[]{:S(2)}, u32[]{:S(2)}) collective-permute-start(bf16[64,256]{1,0:T(8,128)(2,1)S(1)} %get-tuple-element.69.o0), channel_id=1, source_target_pairs={{8,16},{24,32},{40,48},{56,64},{72,80},{88,96},{104,112},{120,128}... | collective-permute-start | bytes 98312 | tf_op jit(solution)/shard_map/ppermute | solution.py:359
  25.5 9.5 %collective-permute-start.5 = (bf16[64,256]{1,0:T(8,128)(2,1)S(1)}, bf16[64,256]{1,0:T(8,128)(2,1)S(1)}, u32[]{:S(2)}, u32[]{:S(2)}) collective-permute-start(bf16[64,256]{1,0:T(8,128)(2,1)S(1)} %get-tuple-element.70.o1), channel_id=1, source_target_pairs={{0,8},{16,24},{32,40},{48,56},{64,72},{80,88},{96,104},{112,120},{... | collective-permute-start | bytes 98312 | tf_op jit(solution)/shard_map/ppermute | solution.py:359
  28.3 6.7 %collective-permute-start.6 = (bf16[64,128]{1,0:T(8,128)(2,1)S(1)}, bf16[64,128]{1,0:T(8,128)(2,1)S(1)}, u32[]{:S(2)}, u32[]{:S(2)}) collective-permute-start(bf16[64,128]{1,0:T(8,128)(2,1)S(1)} %get-tuple-element.71.o2), channel_id=1, source_target_pairs={{1,2},{3,4},{5,6},{2,1},{4,3},{6,5},{9,10},{11,12},{13,14},{10,9},... | collective-permute-start | bytes 49160 | tf_op jit(solution)/shard_map/ppermute | solution.py:359
  31.8 3.2 %collective-permute-start.7 = (bf16[64,128]{1,0:T(8,128)(2,1)S(1)}, bf16[64,128]{1,0:T(8,128)(2,1)S(1)}, u32[]{:S(2)}, u32[]{:S(2)}) collective-permute-start(bf16[64,128]{1,0:T(8,128)(2,1)S(1)} %get-tuple-element.72.o3), channel_id=1, source_target_pairs={{0,1},{2,3},{4,5},{6,7},{1,0},{3,2},{5,4},{7,6},{8,9},{10,11},{12,... | collective-permute-start | bytes 49160 | tf_op jit(solution)/shard_map/ppermute | solution.py:359
  36.1 12.1 %collective-permute-start.8 = (bf16[64,256]{1,0:T(8,128)(2,1)S(1)}, bf16[64,256]{1,0:T(8,128)(2,1)S(1)}, u32[]{:S(2)}, u32[]{:S(2)}) collective-permute-start(bf16[64,256]{1,0:T(8,128)(2,1)S(1)} %get-tuple-element.77.o0), channel_id=1, source_target_pairs={{8,16},{24,32},{40,48},{56,64},{72,80},{88,96},{104,112},{120,128}... | collective-permute-start | bytes 98312 | tf_op jit(solution)/shard_map/ppermute | solution.py:359
  39.8 8.4 %collective-permute-start.9 = (bf16[64,256]{1,0:T(8,128)(2,1)S(1)}, bf16[64,256]{1,0:T(8,128)(2,1)S(1)}, u32[]{:S(2)}, u32[]{:S(2)}) collective-permute-start(bf16[64,256]{1,0:T(8,128)(2,1)S(1)} %get-tuple-element.78.o1), channel_id=1, source_target_pairs={{0,8},{16,24},{32,40},{48,56},{64,72},{80,88},{96,104},{112,120},{... | collective-permute-start | bytes 98312 | tf_op jit(solution)/shard_map/ppermute | solution.py:359
  42.0 6.1 %collective-permute-start.10 = (bf16[64,128]{1,0:T(8,128)(2,1)S(1)}, bf16[64,128]{1,0:T(8,128)(2,1)S(1)}, u32[]{:S(2)}, u32[]{:S(2)}) collective-permute-start(bf16[64,128]{1,0:T(8,128)(2,1)S(1)} %get-tuple-element.79.o2), channel_id=1, source_target_pairs={{1,2},{3,4},{5,6},{2,1},{4,3},{6,5},{9,10},{11,12},{13,14},{10,9},... | collective-permute-start | bytes 49160 | tf_op jit(solution)/shard_map/ppermute | solution.py:359
  44.5 3.6 %collective-permute-start.11 = (bf16[64,128]{1,0:T(8,128)(2,1)S(1)}, bf16[64,128]{1,0:T(8,128)(2,1)S(1)}, u32[]{:S(2)}, u32[]{:S(2)}) collective-permute-start(bf16[64,128]{1,0:T(8,128)(2,1)S(1)} %get-tuple-element.80.o3), channel_id=1, source_target_pairs={{0,1},{2,3},{4,5},{6,7},{1,0},{3,2},{5,4},{7,6},{8,9},{10,11},{12,... | collective-permute-start | bytes 49160 | tf_op jit(solution)/shard_map/ppermute | solution.py:359
  49.2 13.2 %collective-permute-start.12 = (bf16[64,256]{1,0:T(8,128)(2,1)S(1)}, bf16[64,256]{1,0:T(8,128)(2,1)S(1)}, u32[]{:S(2)}, u32[]{:S(2)}) collective-permute-start(bf16[64,256]{1,0:T(8,128)(2,1)S(1)} %get-tuple-element.85), channel_id=1, source_target_pairs={{8,16},{24,32},{40,48},{56,64},{72,80},{88,96},{104,112},{120,128}... | collective-permute-start | bytes 98312 | tf_op jit(solution)/shard_map/ppermute | solution.py:359
  52.5 10.0 %collective-permute-start.13 = (bf16[64,256]{1,0:T(8,128)(2,1)S(1)}, bf16[64,256]{1,0:T(8,128)(2,1)S(1)}, u32[]{:S(2)}, u32[]{:S(2)}) collective-permute-start(bf16[64,256]{1,0:T(8,128)(2,1)S(1)} %get-tuple-element.86), channel_id=1, source_target_pairs={{0,8},{16,24},{32,40},{48,56},{64,72},{80,88},{96,104},{112,120},{... | collective-permute-start | bytes 98312 | tf_op jit(solution)/shard_map/ppermute | solution.py:359
  55.6 6.8 %collective-permute-start.14 = (bf16[64,128]{1,0:T(8,128)(2,1)S(1)}, bf16[64,128]{1,0:T(8,128)(2,1)S(1)}, u32[]{:S(2)}, u32[]{:S(2)}) collective-permute-start(bf16[64,128]{1,0:T(8,128)(2,1)S(1)} %get-tuple-element.87), channel_id=1, source_target_pairs={{1,2},{3,4},{5,6},{2,1},{4,3},{6,5},{9,10},{11,12},{13,14},{10,9},... | collective-permute-start | bytes 49160 | tf_op jit(solution)/shard_map/ppermute | solution.py:359
  57.6 4.9 %collective-permute-start.15 = (bf16[64,128]{1,0:T(8,128)(2,1)S(1)}, bf16[64,128]{1,0:T(8,128)(2,1)S(1)}, u32[]{:S(2)}, u32[]{:S(2)}) collective-permute-start(bf16[64,128]{1,0:T(8,128)(2,1)S(1)} %get-tuple-element.88), channel_id=1, source_target_pairs={{0,1},{2,3},{4,5},{6,7},{1,0},{3,2},{5,4},{7,6},{8,9},{10,11},{12,... | collective-permute-start | bytes 49160 | tf_op jit(solution)/shard_map/ppermute | solution.py:359

commit v3 on v2

--- a/solution.py
+++ b/solution.py
@@ -1,5 +1,3 @@
-import functools
-
 import jax
 import jax.numpy as jnp
 from jax import lax
@@ -269,15 +267,24 @@
     return found[: delta.shape[0]] + found[second:]
 
 
-def local_kernel(layer, state, delta, compact, ranks, volume, lift, trace, new_state, base, kept=None):
-    rank = ranks[layer - 1 : layer]
+def local_kernel(
+    state, delta, compact, ranks, sent, volume, lift, trace, new_state, new_compact, new_ranks, new_sent, base, kept
+):
+    rank = ranks[0:1]
+    more = many(compact[0])
     new_state[...] = state[...] + scatter(delta[:, FIRST], rank, FIRST)
 
-    @pl.when(many(compact[layer - 1]))
+    @pl.when(more)
     def _():
         new_state[...] = new_state[...] + scatter(delta[:, OTHERS], rank, OTHERS)
 
-    local_parts(new_state, compact[layer], volume, lift, trace, base, kept)
+    tables = [compact[l] for l in range(1, compact.shape[0])]
+    for l, table in enumerate(tables):
+        new_compact[l] = table
+    later_ranks, later_sent = ranks[1:], sent[1:]
+    new_ranks[:-1, :] = later_ranks
+    new_sent[:-1, :] = later_sent
+    local_parts(new_state, tables[0], volume, lift, trace, base, kept)
 
 
 def powers_of(volume):
@@ -306,11 +313,11 @@
     return total
 
 
-def advance_kernel(layer, r0, r1, r2, r3, o0, o1, o2, o3, compact, base, kept, sent, powers, lift, trace, delta, *outgoing):
-    rows = compact[layer]
+def advance_kernel(r0, r1, r2, r3, o0, o1, o2, o3, compact, base, kept, sent, powers, lift, trace, delta, *outgoing):
+    rows = compact[0]
 
     def part(here, before):
-        place = sent[layer : layer + 1] - here.start
+        place = sent[0:1] - here.start
         chosen = hot(place, here.stop - here.start)
         total = taylor_terms((r0, r1, r2, r3), rows, here, base, powers, lift)
         delta[:, here] = total
@@ -326,8 +333,8 @@
         part(OTHERS, outgoing)
 
 
-def last_kernel(layer, r0, r1, r2, r3, compact, base, ranks, powers, lift, state, advanced, held, sem):
-    rows, rank = compact[layer], ranks[layer : layer + 1]
+def last_kernel(r0, r1, r2, r3, compact, base, ranks, powers, lift, state, advanced, held, sem):
+    rows, rank = compact[0], ranks[0:1]
 
     def part(here, before):
         total = taylor_terms((r0, r1, r2, r3), rows, here, base, powers, lift)
@@ -344,11 +351,12 @@
     copy.wait()
 
 
-def call(kernel, outs, args, flops):
+def call(kernel, outs, args, flops, aliases={}):
     outs = [jax.ShapeDtypeStruct(shape, dtype) for shape, dtype in outs]
     return pl.pallas_call(
         kernel,
         out_shape=outs,
+        input_output_aliases=aliases,
         compiler_params=pltpu.CompilerParams(vmem_limit_bytes=VMEM),
         cost_estimate=pl.CostEstimate(flops=flops, bytes_accessed=2**20, transcendentals=0),
     )(*args)
@@ -409,25 +417,34 @@
             ((5 * POWER_ROWS, comps), BF16),
         ],
         (state, neighbours, elem_tent, boundary, active, tent_height, volume_op, lift, trace),
-        10**9,
+        10**6,
     )
-    for layer in range(layers - 1):
+    tables = [(compact.shape, F32), (ranks.shape, I32), (sent.shape, I32)]
+
+    def layer(_, carry):
+        received, outgoing, state, compact, ranks, sent, base, kept = carry
         delta, *outgoing = call(
-            functools.partial(advance_kernel, layer),
+            advance_kernel,
             [live] + blocks,
             (*received, *outgoing, compact, base, kept, sent, powers, lift, trace),
-            10**9,
+            10**6,
+            {4 + i: 1 + i for i in range(4)},
         )
         received = exchange(outgoing)
-        state, base, *rest = call(
-            functools.partial(local_kernel, layer + 1),
-            [all_columns, live] + [live] * (layer + 2 < layers),
-            (state, delta, compact, ranks, volume_op, lift, trace),
-            10**9,
+        state, compact, ranks, sent, base, kept = call(
+            local_kernel,
+            [all_columns, *tables, live, live],
+            (state, delta, compact, ranks, sent, volume_op, lift, trace),
+            10**6,
+            {0: 0, 2: 1, 3: 2, 4: 3},
         )
-        kept = rest[0] if rest else None
+        return received, tuple(outgoing), state, compact, ranks, sent, base, kept
+
+    received, _, state, compact, ranks, _, base, _ = lax.fori_loop(
+        0, layers - 1, layer, (received, tuple(outgoing), state, compact, ranks, sent, base, kept)
+    )
     return pl.pallas_call(
-        functools.partial(last_kernel, layers - 1),
+        last_kernel,
         out_specs=pl.BlockSpec(memory_space=pltpu.MemorySpace.HBM),
         out_shape=jax.ShapeDtypeStruct((comps, elems), F32),
         scratch_shapes=[pltpu.VMEM((comps, elems), F32), pltpu.SemaphoreType.DMA],

time: 64.7 us -> 65.1 us (level)
  the two profiles are of different devices: /device:TPU:11 before, /device:TPU:19 now
where the time goes in v3:
time: 65.1 us; the launch traced here: 64.5 us
  starting transfers between devices  52.2 us (80%)
  Pallas kernels  11.9 us (18%)
    ppermute x16, starting transfers between devices, swapped(): return lax.ppermute(block, axis, pairs + [(j, i) for i, j in pairs])  52.2 us
    pallas_call x7, Pallas kernels, call(): pl.pallas_call(kernel, out_shape=outs, input_output_aliases=aliases, comp...  8.69 us
    pallas_call x1, Pallas kernels, local(): pl.pallas_call(last_kernel, out_specs=pl.BlockSpec(memory_space=pltpu.Mem...  1.76 us
    pallas_call x1, Pallas kernels, local(): pl.pallas_call(first_kernel, in_specs=[pl.BlockSpec(memory_space=pltpu.Me...  1.48 us
  transfers between devices with their start and end apart: 16, of which 0 were waited for; matrix products, arithmetic and copies ran while one was open for 0% of the time, Pallas kernels for 9%

profile of v3, /device:TPU:19, one launch (start us, length us, event | category | flops | bytes accessed | tf_op | source)
XLA Modules:
  0.0 64.5 jit_solution(6602180724507615748)
XLA Ops:
  0.0 1.5 %shard_map.91 = (bf16[64,256]{1,0:T(8,128)(2,1)S(1)}, bf16[64,256]{1,0:T(8,128)(2,1)S(1)}, bf16[64,128]{1,0:T(8,128)(2,1)S(1)}, bf16[64,128]{1,0:T(8,128)(2,1)S(...) custom-call(f32[100,1024]{1,0:T(8,128)} %refs_0_.1, ...), custom_call_target="tpu_custom_call" | custom-call | tf_op jit(solution)/shard_map/pallas_call | solution.py:397
  1.5 10.6 %collective-permute-start.4 = (bf16[64,256]{1,0:T(8,128)(2,1)S(1)}, bf16[64,256]{1,0:T(8,128)(2,1)S(1)}, u32[]{:S(2)}, u32[]{:S(2)}) collective-permute-start(bf16[64,256]{1,0:T(8,128)(2,1)S(1)} %get-tuple-element.350), channel_id=1, source_target_pairs={{8,16},{24,32},{40,48},{56,64},{72,80},{88,96},{104,112},{120,128}... | collective-permute-start | bytes 98312 | tf_op jit(solution)/shard_map/ppermute | solution.py:367
  12.1 1.9 %collective-permute-start.5 = (bf16[64,256]{1,0:T(8,128)(2,1)S(1)}, bf16[64,256]{1,0:T(8,128)(2,1)S(1)}, u32[]{:S(2)}, u32[]{:S(2)}) collective-permute-start(bf16[64,256]{1,0:T(8,128)(2,1)S(1)} %get-tuple-element.351), channel_id=1, source_target_pairs={{0,8},{16,24},{32,40},{48,56},{64,72},{80,88},{96,104},{112,120},{... | collective-permute-start | bytes 98312 | tf_op jit(solution)/shard_map/ppermute | solution.py:367
  14.0 4.0 %collective-permute-start.6 = (bf16[64,128]{1,0:T(8,128)(2,1)S(1)}, bf16[64,128]{1,0:T(8,128)(2,1)S(1)}, u32[]{:S(2)}, u32[]{:S(2)}) collective-permute-start(bf16[64,128]{1,0:T(8,128)(2,1)S(1)} %get-tuple-element.352), channel_id=1, source_target_pairs={{1,2},{3,4},{5,6},{2,1},{4,3},{6,5},{9,10},{11,12},{13,14},{10,9},... | collective-permute-start | bytes 49160 | tf_op jit(solution)/shard_map/ppermute | solution.py:367
  17.9 1.9 %collective-permute-start.7 = (bf16[64,128]{1,0:T(8,128)(2,1)S(1)}, bf16[64,128]{1,0:T(8,128)(2,1)S(1)}, u32[]{:S(2)}, u32[]{:S(2)}) collective-permute-start(bf16[64,128]{1,0:T(8,128)(2,1)S(1)} %get-tuple-element.353), channel_id=1, source_target_pairs={{0,1},{2,3},{4,5},{6,7},{1,0},{3,2},{5,4},{7,6},{8,9},{10,11},{12,... | collective-permute-start | bytes 49160 | tf_op jit(solution)/shard_map/ppermute | solution.py:367
  19.9 1.8 %shard_map.92 = (f32[4,16,384]{2,1,0:T(8,128)S(1)}, s32[8,1024]{1,0:T(8,128)S(1)}, s32[4,768]{1,0:T(4,128)S(1)}, f32[100,384]{1,0:T(8,128)S(1)}, f32[100,384]{1,...) custom-call(f32[100,1024]{1,0:T(8,128)S(1)} %get-tuple-element.354.state, ...), custom_call_target="tpu_custom_call" | custom-call | flops 1000000 | bytes 1048576 | tf_op jit(solution)/shard_map/pallas_call | solution.py:356
  21.7 0.0 collective-permute-done.6
  21.7 0.0 collective-permute-done.7
  21.7 0.0 collective-permute-done.4
  21.7 0.0 collective-permute-done.5
  21.7 41.0 %while.36 = (s32[]{:T(128)}, bf16[64,256]{1,0:T(8,128)(2,1)S(1)}, bf16[64,256]{1,0:T(8,128)(2,1)S(1)}, bf16[64,128]{1,0:T(8,128)(2,1)S(1)}, bf16[64,128]{1,0:T(8...) while((s32[]{:T(128)}, bf16[64,256]{1,0:T(8,128)(2,1)S(1)}, ...), condition=%wide.region_1.0_spmd, body=%wide.region_0.0_spmd.sunk | while | flops 2000002 | bytes 2490709 | solution.py:443
  21.7 1.0 %eval_jaxpr.2 = (f32[100,384]{1,0:T(8,128)S(1)}, bf16[64,256]{1,0:T(8,128)(2,1)S(1)}, bf16[64,256]{1,0:T(8,128)(2,1)S(1)}, bf16[64,128]{1,0:T(8,128)(2,1)S(1)}, bf16[64,128]{1,0:T(8,128)(2,1)S(1)}) custom-call(bf16[64,256]{1,0:T(8,128)(2,1)S(1)} %get-tuple-element.366.r0, ...), custom_call_target="tpu_custom_call", output_to_operand_aliasing={{1}: (4, {}), {2}: (5, {}), {3}: (6, {}), {4}: (7, {})} | custom-call | flops 1000000 | bytes 1048576 | tf_op jit(solution)/shard_map/while/body/eval_jaxpr/pallas_call | solution.py:356
  22.8 2.7 %collective-permute-start = (bf16[64,256]{1,0:T(8,128)(2,1)S(1)}, bf16[64,256]{1,0:T(8,128)(2,1)S(1)}, u32[]{:S(2)}, u32[]{:S(2)}) collective-permute-start(bf16[64,256]{1,0:T(8,128)(2,1)S(1)} %get-tuple-element.390), channel_id=1, source_target_pairs={{8,16},{24,32},{40,48},{56,64},{72,80},{88,96},{104,112},{120,128}... | collective-permute-start | bytes 98312 | tf_op jit(solution)/shard_map/while/body/eval_jaxpr/ppermute | solution.py:367
  25.5 2.8 %collective-permute-start.1 = (bf16[64,256]{1,0:T(8,128)(2,1)S(1)}, bf16[64,256]{1,0:T(8,128)(2,1)S(1)}, u32[]{:S(2)}, u32[]{:S(2)}) collective-permute-start(bf16[64,256]{1,0:T(8,128)(2,1)S(1)} %get-tuple-element.391), channel_id=1, source_target_pairs={{0,8},{16,24},{32,40},{48,56},{64,72},{80,88},{96,104},{112,120},{... | collective-permute-start | bytes 98312 | tf_op jit(solution)/shard_map/while/body/eval_jaxpr/ppermute | solution.py:367
  28.4 3.5 %collective-permute-start.2 = (bf16[64,128]{1,0:T(8,128)(2,1)S(1)}, bf16[64,128]{1,0:T(8,128)(2,1)S(1)}, u32[]{:S(2)}, u32[]{:S(2)}) collective-permute-start(bf16[64,128]{1,0:T(8,128)(2,1)S(1)} %get-tuple-element.392), channel_id=1, source_target_pairs={{1,2},{3,4},{5,6},{2,1},{4,3},{6,5},{9,10},{11,12},{13,14},{10,9},... | collective-permute-start | bytes 49160 | tf_op jit(solution)/shard_map/while/body/eval_jaxpr/ppermute | solution.py:367
  31.9 1.9 %collective-permute-start.3 = (bf16[64,128]{1,0:T(8,128)(2,1)S(1)}, bf16[64,128]{1,0:T(8,128)(2,1)S(1)}, u32[]{:S(2)}, u32[]{:S(2)}) collective-permute-start(bf16[64,128]{1,0:T(8,128)(2,1)S(1)} %get-tuple-element.393), channel_id=1, source_target_pairs={{0,1},{2,3},{4,5},{6,7},{1,0},{3,2},{5,4},{7,6},{8,9},{10,11},{12,... | collective-permute-start | bytes 49160 | tf_op jit(solution)/shard_map/while/body/eval_jaxpr/ppermute | solution.py:367
  33.8 1.3 %eval_jaxpr.3 = (f32[100,1024]{1,0:T(8,128)S(1)}, f32[4,16,384]{2,1,0:T(8,128)S(1)}, s32[8,1024]{1,0:T(8,128)S(1)}, s32[4,768]{1,0:T(4,128)S(1)}, f32[100,384]{1,0:T(8,128)S(1)}, /*index=5*/f32[100,384]{1,0:T(8,128)S(1)}) custom-call(f32[100,1024]{1,0:T(8,128)S(1)} %get-tuple-element.374.stat, ...), custom_call_target="tpu_custom_call", output_to_operand_aliasing={{0}: (0, {}), {1}: (2, {}), {2}: (3, {}), {3}: (4, {})} | custom-call | flops 1000000 | bytes 1048576 | tf_op jit(solution)/shard_map/while/body/eval_jaxpr/pallas_call | solution.py:356
  35.0 0.0 collective-permute-done.2
  35.1 0.0 collective-permute-done.3
  35.1 0.0 collective-permute-done
  35.1 0.0 collective-permute-done.1
  35.1 1.0 %eval_jaxpr.2 = (f32[100,384]{1,0:T(8,128)S(1)}, bf16[64,256]{1,0:T(8,128)(2,1)S(1)}, bf16[64,256]{1,0:T(8,128)(2,1)S(1)}, bf16[64,128]{1,0:T(8,128)(2,1)S(1)}, bf16[64,128]{1,0:T(8,128)(2,1)S(1)}) custom-call(bf16[64,256]{1,0:T(8,128)(2,1)S(1)} %get-tuple-element.366.r0, ...), custom_call_target="tpu_custom_call", output_to_operand_aliasing={{1}: (4, {}), {2}: (5, {}), {3}: (6, {}), {4}: (7, {})} | custom-call | flops 1000000 | bytes 1048576 | tf_op jit(solution)/shard_map/while/body/eval_jaxpr/pallas_call | solution.py:356
  36.1 3.8 %collective-permute-start = (bf16[64,256]{1,0:T(8,128)(2,1)S(1)}, bf16[64,256]{1,0:T(8,128)(2,1)S(1)}, u32[]{:S(2)}, u32[]{:S(2)}) collective-permute-start(bf16[64,256]{1,0:T(8,128)(2,1)S(1)} %get-tuple-element.390), channel_id=1, source_target_pairs={{8,16},{24,32},{40,48},{56,64},{72,80},{88,96},{104,112},{120,128}... | collective-permute-start | bytes 98312 | tf_op jit(solution)/shard_map/while/body/eval_jaxpr/ppermute | solution.py:367
  39.9 2.2 %collective-permute-start.1 = (bf16[64,256]{1,0:T(8,128)(2,1)S(1)}, bf16[64,256]{1,0:T(8,128)(2,1)S(1)}, u32[]{:S(2)}, u32[]{:S(2)}) collective-permute-start(bf16[64,256]{1,0:T(8,128)(2,1)S(1)} %get-tuple-element.391), channel_id=1, source_target_pairs={{0,8},{16,24},{32,40},{48,56},{64,72},{80,88},{96,104},{112,120},{... | collective-permute-start | bytes 98312 | tf_op jit(solution)/shard_map/while/body/eval_jaxpr/ppermute | solution.py:367
  42.1 2.5 %collective-permute-start.2 = (bf16[64,128]{1,0:T(8,128)(2,1)S(1)}, bf16[64,128]{1,0:T(8,128)(2,1)S(1)}, u32[]{:S(2)}, u32[]{:S(2)}) collective-permute-start(bf16[64,128]{1,0:T(8,128)(2,1)S(1)} %get-tuple-element.392), channel_id=1, source_target_pairs={{1,2},{3,4},{5,6},{2,1},{4,3},{6,5},{9,10},{11,12},{13,14},{10,9},... | collective-permute-start | bytes 49160 | tf_op jit(solution)/shard_map/while/body/eval_jaxpr/ppermute | solution.py:367
  44.6 2.4 %collective-permute-start.3 = (bf16[64,128]{1,0:T(8,128)(2,1)S(1)}, bf16[64,128]{1,0:T(8,128)(2,1)S(1)}, u32[]{:S(2)}, u32[]{:S(2)}) collective-permute-start(bf16[64,128]{1,0:T(8,128)(2,1)S(1)} %get-tuple-element.393), channel_id=1, source_target_pairs={{0,1},{2,3},{4,5},{6,7},{1,0},{3,2},{5,4},{7,6},{8,9},{10,11},{12,... | collective-permute-start | bytes 49160 | tf_op jit(solution)/shard_map/while/body/eval_jaxpr/ppermute | solution.py:367
  47.0 1.3 %eval_jaxpr.3 = (f32[100,1024]{1,0:T(8,128)S(1)}, f32[4,16,384]{2,1,0:T(8,128)S(1)}, s32[8,1024]{1,0:T(8,128)S(1)}, s32[4,768]{1,0:T(4,128)S(1)}, f32[100,384]{1,0:T(8,128)S(1)}, /*index=5*/f32[100,384]{1,0:T(8,128)S(1)}) custom-call(f32[100,1024]{1,0:T(8,128)S(1)} %get-tuple-element.374.stat, ...), custom_call_target="tpu_custom_call", output_to_operand_aliasing={{0}: (0, {}), {1}: (2, {}), {2}: (3, {}), {3}: (4, {})} | custom-call | flops 1000000 | bytes 1048576 | tf_op jit(solution)/shard_map/while/body/eval_jaxpr/pallas_call | solution.py:356
  48.3 0.0 collective-permute-done.2
  48.3 0.0 collective-permute-done.3
  48.3 0.0 collective-permute-done
  48.3 0.0 collective-permute-done.1
  48.3 1.0 %eval_jaxpr.2 = (f32[100,384]{1,0:T(8,128)S(1)}, bf16[64,256]{1,0:T(8,128)(2,1)S(1)}, bf16[64,256]{1,0:T(8,128)(2,1)S(1)}, bf16[64,128]{1,0:T(8,128)(2,1)S(1)}, bf16[64,128]{1,0:T(8,128)(2,1)S(1)}) custom-call(bf16[64,256]{1,0:T(8,128)(2,1)S(1)} %get-tuple-element.366.r0, ...), custom_call_target="tpu_custom_call", output_to_operand_aliasing={{1}: (4, {}), {2}: (5, {}), {3}: (6, {}), {4}: (7, {})} | custom-call | flops 1000000 | bytes 1048576 | tf_op jit(solution)/shard_map/while/body/eval_jaxpr/pallas_call | solution.py:356
  49.4 3.2 %collective-permute-start = (bf16[64,256]{1,0:T(8,128)(2,1)S(1)}, bf16[64,256]{1,0:T(8,128)(2,1)S(1)}, u32[]{:S(2)}, u32[]{:S(2)}) collective-permute-start(bf16[64,256]{1,0:T(8,128)(2,1)S(1)} %get-tuple-element.390), channel_id=1, source_target_pairs={{8,16},{24,32},{40,48},{56,64},{72,80},{88,96},{104,112},{120,128}... | collective-permute-start | bytes 98312 | tf_op jit(solution)/shard_map/while/body/eval_jaxpr/ppermute | solution.py:367
  52.6 3.2 %collective-permute-start.1 = (bf16[64,256]{1,0:T(8,128)(2,1)S(1)}, bf16[64,256]{1,0:T(8,128)(2,1)S(1)}, u32[]{:S(2)}, u32[]{:S(2)}) collective-permute-start(bf16[64,256]{1,0:T(8,128)(2,1)S(1)} %get-tuple-element.391), channel_id=1, source_target_pairs={{0,8},{16,24},{32,40},{48,56},{64,72},{80,88},{96,104},{112,120},{... | collective-permute-start | bytes 98312 | tf_op jit(solution)/shard_map/while/body/eval_jaxpr/ppermute | solution.py:367
  55.9 3.2 %collective-permute-start.2 = (bf16[64,128]{1,0:T(8,128)(2,1)S(1)}, bf16[64,128]{1,0:T(8,128)(2,1)S(1)}, u32[]{:S(2)}, u32[]{:S(2)}) collective-permute-start(bf16[64,128]{1,0:T(8,128)(2,1)S(1)} %get-tuple-element.392), channel_id=1, source_target_pairs={{1,2},{3,4},{5,6},{2,1},{4,3},{6,5},{9,10},{11,12},{13,14},{10,9},... | collective-permute-start | bytes 49160 | tf_op jit(solution)/shard_map/while/body/eval_jaxpr/ppermute | solution.py:367
  59.0 2.4 %collective-permute-start.3 = (bf16[64,128]{1,0:T(8,128)(2,1)S(1)}, bf16[64,128]{1,0:T(8,128)(2,1)S(1)}, u32[]{:S(2)}, u32[]{:S(2)}) collective-permute-start(bf16[64,128]{1,0:T(8,128)(2,1)S(1)} %get-tuple-element.393), channel_id=1, source_target_pairs={{0,1},{2,3},{4,5},{6,7},{1,0},{3,2},{5,4},{7,6},{8,9},{10,11},{12,... | collective-permute-start | bytes 49160 | tf_op jit(solution)/shard_map/while/body/eval_jaxpr/ppermute | solution.py:367
  61.5 1.3 %eval_jaxpr.3 = (f32[100,1024]{1,0:T(8,128)S(1)}, f32[4,16,384]{2,1,0:T(8,128)S(1)}, s32[8,1024]{1,0:T(8,128)S(1)}, s32[4,768]{1,0:T(4,128)S(1)}, f32[100,384]{1,0:T(8,128)S(1)}, /*index=5*/f32[100,384]{1,0:T(8,128)S(1)}) custom-call(f32[100,1024]{1,0:T(8,128)S(1)} %get-tuple-element.374.stat, ...), custom_call_target="tpu_custom_call", output_to_operand_aliasing={{0}: (0, {}), {1}: (2, {}), {2}: (3, {}), {3}: (4, {})} | custom-call | flops 1000000 | bytes 1048576 | tf_op jit(solution)/shard_map/while/body/eval_jaxpr/pallas_call | solution.py:356
  62.7 0.0 collective-permute-done.2
  62.7 0.0 collective-permute-done.3
  62.7 0.0 collective-permute-done
  62.8 0.0 collective-permute-done.1
  62.8 1.8 %shard_map.93 = f32[100,1024]{1,0:T(8,128)} custom-call(bf16[64,256]{1,0:T(8,128)(2,1)S(1)} %get-tuple-element.162.r0, bf16[64,256]{1,0:T(8,128)(2,1)S(1)} %get-tuple-element.163.r1, bf16[64,128]{1,0:T(8,128)(2,1)S(1)} %get-tuple-element.164.r2, bf16[64,128]{1,0:T(8,128)(2,1)S(1)} %get-tuple-element.165.r3, f32[4,16,384]{2,1,0:T(8,128)S(1)} %get-tuple-element.166.compact, ...), custom_call_target="tpu_custom_call" | custom-call | tf_op jit(solution)/shard_map/pallas_call | solution.py:446
Async XLA Ops:
  1.5 20.2 %collective-permute-start.4 = (bf16[64,256]{1,0:T(8,128)(2,1)S(1)}, bf16[64,256]{1,0:T(8,128)(2,1)S(1)}, u32[]{:S(2)}, u32[]{:S(2)}) collective-permute-start(bf16[64,256]{1,0:T(8,128)(2,1)S(1)} %get-tuple-element.350), channel_id=1, source_target_pairs={{8,16},{24,32},{40,48},{56,64},{72,80},{88,96},{104,112},{120,128}... | collective-permute-start | bytes 98312 | tf_op jit(solution)/shard_map/ppermute | solution.py:367
  12.1 9.7 %collective-permute-start.5 = (bf16[64,256]{1,0:T(8,128)(2,1)S(1)}, bf16[64,256]{1,0:T(8,128)(2,1)S(1)}, u32[]{:S(2)}, u32[]{:S(2)}) collective-permute-start(bf16[64,256]{1,0:T(8,128)(2,1)S(1)} %get-tuple-element.351), channel_id=1, source_target_pairs={{0,8},{16,24},{32,40},{48,56},{64,72},{80,88},{96,104},{112,120},{... | collective-permute-start | bytes 98312 | tf_op jit(solution)/shard_map/ppermute | solution.py:367
  14.0 7.7 %collective-permute-start.6 = (bf16[64,128]{1,0:T(8,128)(2,1)S(1)}, bf16[64,128]{1,0:T(8,128)(2,1)S(1)}, u32[]{:S(2)}, u32[]{:S(2)}) collective-permute-start(bf16[64,128]{1,0:T(8,128)(2,1)S(1)} %get-tuple-element.352), channel_id=1, source_target_pairs={{1,2},{3,4},{5,6},{2,1},{4,3},{6,5},{9,10},{11,12},{13,14},{10,9},... | collective-permute-start | bytes 49160 | tf_op jit(solution)/shard_map/ppermute | solution.py:367
  17.9 3.7 %collective-permute-start.7 = (bf16[64,128]{1,0:T(8,128)(2,1)S(1)}, bf16[64,128]{1,0:T(8,128)(2,1)S(1)}, u32[]{:S(2)}, u32[]{:S(2)}) collective-permute-start(bf16[64,128]{1,0:T(8,128)(2,1)S(1)} %get-tuple-element.353), channel_id=1, source_target_pairs={{0,1},{2,3},{4,5},{6,7},{1,0},{3,2},{5,4},{7,6},{8,9},{10,11},{12,... | collective-permute-start | bytes 49160 | tf_op jit(solution)/shard_map/ppermute | solution.py:367
  22.8 12.3 %collective-permute-start = (bf16[64,256]{1,0:T(8,128)(2,1)S(1)}, bf16[64,256]{1,0:T(8,128)(2,1)S(1)}, u32[]{:S(2)}, u32[]{:S(2)}) collective-permute-start(bf16[64,256]{1,0:T(8,128)(2,1)S(1)} %get-tuple-element.390), channel_id=1, source_target_pairs={{8,16},{24,32},{40,48},{56,64},{72,80},{88,96},{104,112},{120,128}... | collective-permute-start | bytes 98312 | tf_op jit(solution)/shard_map/while/body/eval_jaxpr/ppermute | solution.py:367
  25.5 9.6 %collective-permute-start.1 = (bf16[64,256]{1,0:T(8,128)(2,1)S(1)}, bf16[64,256]{1,0:T(8,128)(2,1)S(1)}, u32[]{:S(2)}, u32[]{:S(2)}) collective-permute-start(bf16[64,256]{1,0:T(8,128)(2,1)S(1)} %get-tuple-element.391), channel_id=1, source_target_pairs={{0,8},{16,24},{32,40},{48,56},{64,72},{80,88},{96,104},{112,120},{... | collective-permute-start | bytes 98312 | tf_op jit(solution)/shard_map/while/body/eval_jaxpr/ppermute | solution.py:367
  28.4 6.7 %collective-permute-start.2 = (bf16[64,128]{1,0:T(8,128)(2,1)S(1)}, bf16[64,128]{1,0:T(8,128)(2,1)S(1)}, u32[]{:S(2)}, u32[]{:S(2)}) collective-permute-start(bf16[64,128]{1,0:T(8,128)(2,1)S(1)} %get-tuple-element.392), channel_id=1, source_target_pairs={{1,2},{3,4},{5,6},{2,1},{4,3},{6,5},{9,10},{11,12},{13,14},{10,9},... | collective-permute-start | bytes 49160 | tf_op jit(solution)/shard_map/while/body/eval_jaxpr/ppermute | solution.py:367
  31.9 3.2 %collective-permute-start.3 = (bf16[64,128]{1,0:T(8,128)(2,1)S(1)}, bf16[64,128]{1,0:T(8,128)(2,1)S(1)}, u32[]{:S(2)}, u32[]{:S(2)}) collective-permute-start(bf16[64,128]{1,0:T(8,128)(2,1)S(1)} %get-tuple-element.393), channel_id=1, source_target_pairs={{0,1},{2,3},{4,5},{6,7},{1,0},{3,2},{5,4},{7,6},{8,9},{10,11},{12,... | collective-permute-start | bytes 49160 | tf_op jit(solution)/shard_map/while/body/eval_jaxpr/ppermute | solution.py:367
  36.1 12.1 %collective-permute-start = (bf16[64,256]{1,0:T(8,128)(2,1)S(1)}, bf16[64,256]{1,0:T(8,128)(2,1)S(1)}, u32[]{:S(2)}, u32[]{:S(2)}) collective-permute-start(bf16[64,256]{1,0:T(8,128)(2,1)S(1)} %get-tuple-element.390), channel_id=1, source_target_pairs={{8,16},{24,32},{40,48},{56,64},{72,80},{88,96},{104,112},{120,128}... | collective-permute-start | bytes 98312 | tf_op jit(solution)/shard_map/while/body/eval_jaxpr/ppermute | solution.py:367
  39.9 8.4 %collective-permute-start.1 = (bf16[64,256]{1,0:T(8,128)(2,1)S(1)}, bf16[64,256]{1,0:T(8,128)(2,1)S(1)}, u32[]{:S(2)}, u32[]{:S(2)}) collective-permute-start(bf16[64,256]{1,0:T(8,128)(2,1)S(1)} %get-tuple-element.391), channel_id=1, source_target_pairs={{0,8},{16,24},{32,40},{48,56},{64,72},{80,88},{96,104},{112,120},{... | collective-permute-start | bytes 98312 | tf_op jit(solution)/shard_map/while/body/eval_jaxpr/ppermute | solution.py:367
  42.1 6.2 %collective-permute-start.2 = (bf16[64,128]{1,0:T(8,128)(2,1)S(1)}, bf16[64,128]{1,0:T(8,128)(2,1)S(1)}, u32[]{:S(2)}, u32[]{:S(2)}) collective-permute-start(bf16[64,128]{1,0:T(8,128)(2,1)S(1)} %get-tuple-element.392), channel_id=1, source_target_pairs={{1,2},{3,4},{5,6},{2,1},{4,3},{6,5},{9,10},{11,12},{13,14},{10,9},... | collective-permute-start | bytes 49160 | tf_op jit(solution)/shard_map/while/body/eval_jaxpr/ppermute | solution.py:367
  44.6 3.7 %collective-permute-start.3 = (bf16[64,128]{1,0:T(8,128)(2,1)S(1)}, bf16[64,128]{1,0:T(8,128)(2,1)S(1)}, u32[]{:S(2)}, u32[]{:S(2)}) collective-permute-start(bf16[64,128]{1,0:T(8,128)(2,1)S(1)} %get-tuple-element.393), channel_id=1, source_target_pairs={{0,1},{2,3},{4,5},{6,7},{1,0},{3,2},{5,4},{7,6},{8,9},{10,11},{12,... | collective-permute-start | bytes 49160 | tf_op jit(solution)/shard_map/while/body/eval_jaxpr/ppermute | solution.py:367
  49.4 13.4 %collective-permute-start = (bf16[64,256]{1,0:T(8,128)(2,1)S(1)}, bf16[64,256]{1,0:T(8,128)(2,1)S(1)}, u32[]{:S(2)}, u32[]{:S(2)}) collective-permute-start(bf16[64,256]{1,0:T(8,128)(2,1)S(1)} %get-tuple-element.390), channel_id=1, source_target_pairs={{8,16},{24,32},{40,48},{56,64},{72,80},{88,96},{104,112},{120,128}... | collective-permute-start | bytes 98312 | tf_op jit(solution)/shard_map/while/body/eval_jaxpr/ppermute | solution.py:367
  52.6 10.1 %collective-permute-start.1 = (bf16[64,256]{1,0:T(8,128)(2,1)S(1)}, bf16[64,256]{1,0:T(8,128)(2,1)S(1)}, u32[]{:S(2)}, u32[]{:S(2)}) collective-permute-start(bf16[64,256]{1,0:T(8,128)(2,1)S(1)} %get-tuple-element.391), channel_id=1, source_target_pairs={{0,8},{16,24},{32,40},{48,56},{64,72},{80,88},{96,104},{112,120},{... | collective-permute-start | bytes 98312 | tf_op jit(solution)/shard_map/while/body/eval_jaxpr/ppermute | solution.py:367
  55.9 6.8 %collective-permute-start.2 = (bf16[64,128]{1,0:T(8,128)(2,1)S(1)}, bf16[64,128]{1,0:T(8,128)(2,1)S(1)}, u32[]{:S(2)}, u32[]{:S(2)}) collective-permute-start(bf16[64,128]{1,0:T(8,128)(2,1)S(1)} %get-tuple-element.392), channel_id=1, source_target_pairs={{1,2},{3,4},{5,6},{2,1},{4,3},{6,5},{9,10},{11,12},{13,14},{10,9},... | collective-permute-start | bytes 49160 | tf_op jit(solution)/shard_map/while/body/eval_jaxpr/ppermute | solution.py:367
  59.0 3.7 %collective-permute-start.3 = (bf16[64,128]{1,0:T(8,128)(2,1)S(1)}, bf16[64,128]{1,0:T(8,128)(2,1)S(1)}, u32[]{:S(2)}, u32[]{:S(2)}) collective-permute-start(bf16[64,128]{1,0:T(8,128)(2,1)S(1)} %get-tuple-element.393), channel_id=1, source_target_pairs={{0,1},{2,3},{4,5},{6,7},{1,0},{3,2},{5,4},{7,6},{8,9},{10,11},{12,... | collective-permute-start | bytes 49160 | tf_op jit(solution)/shard_map/while/body/eval_jaxpr/ppermute | solution.py:367

commit v4 on v3

--- a/solution.py
+++ b/solution.py
@@ -239,12 +239,12 @@
     base[:, here] = mm(volume[...], mine) + mm(lift[...], picked)
 
 
-def local_parts(values, compact, *refs):
-    local_part(values[...], compact, FIRST, *refs)
+def local_parts(values, state, compact, *refs):
+    local_part(values, compact, FIRST, *refs)
 
     @pl.when(many(compact))
     def _():
-        local_part(values[...], compact, OTHERS, *refs)
+        local_part(state[...], compact, OTHERS, *refs)
 
 
 def local_first_kernel(
@@ -258,7 +258,7 @@
     diagonal = lax.broadcasted_iota(I32, (comps, comps), 0) == lax.broadcasted_iota(I32, (comps, comps), 1)
     lift[...] = mm_t(jnp.where(diagonal, 1.0, 0.0).astype(BF16), lifts).astype(BF16)
     trace[...] = jnp.concatenate([face_rows(trace_op, g) for g in range(4)], axis=0).astype(BF16)
-    local_parts(state, compact[0], volume, lift, trace, base, kept)
+    local_parts(state[...], state, compact[0], volume, lift, trace, base, kept)
 
 
 def scatter(delta, rank, here):
@@ -270,21 +270,15 @@
 def local_kernel(
     state, delta, compact, ranks, sent, volume, lift, trace, new_state, new_compact, new_ranks, new_sent, base, kept
 ):
-    rank = ranks[0:1]
-    more = many(compact[0])
-    new_state[...] = state[...] + scatter(delta[:, FIRST], rank, FIRST)
-
-    @pl.when(more)
-    def _():
-        new_state[...] = new_state[...] + scatter(delta[:, OTHERS], rank, OTHERS)
-
+    values = state[...] + scatter(delta[...], ranks[0:1], FIRST)
+    new_state[...] = values
     tables = [compact[l] for l in range(1, compact.shape[0])]
     for l, table in enumerate(tables):
         new_compact[l] = table
     later_ranks, later_sent = ranks[1:], sent[1:]
     new_ranks[:-1, :] = later_ranks
     new_sent[:-1, :] = later_sent
-    local_parts(new_state, tables[0], volume, lift, trace, base, kept)
+    local_parts(values, new_state, tables[0], volume, lift, trace, base, kept)
 
 
 def powers_of(volume):
@@ -313,24 +307,29 @@
     return total
 
 
-def advance_kernel(r0, r1, r2, r3, o0, o1, o2, o3, compact, base, kept, sent, powers, lift, trace, delta, *outgoing):
+def advance_kernel(
+    r0, r1, r2, r3, o0, o1, o2, o3, state, compact, base, kept, sent, ranks, powers, lift, trace,
+    delta, out_0, out_1, out_2, out_3, new_state,
+):
     rows = compact[0]
+    outgoing = (out_0, out_1, out_2, out_3)
 
     def part(here, before):
         place = sent[0:1] - here.start
         chosen = hot(place, here.stop - here.start)
         total = taylor_terms((r0, r1, r2, r3), rows, here, base, powers, lift)
-        delta[:, here] = total
         traces = mm(trace[3 * ROWS :, :], (kept[:, here] + total).astype(BF16)).astype(BF16)
         before = jnp.concatenate([ref[...] for ref in before], axis=1).astype(F32)
         inside = jnp.logical_and(place >= 0, place < here.stop - here.start)
         store_blocks(jnp.where(inside, mm(traces, chosen), before), outgoing)
-
-    part(FIRST, (o0, o1, o2, o3))
+        return total
+
+    new_state[...] = state[...]
+    delta[...] = part(FIRST, (o0, o1, o2, o3))
 
     @pl.when(many(rows))
     def _():
-        part(OTHERS, outgoing)
+        new_state[...] = new_state[...] + scatter(part(OTHERS, outgoing), ranks[0:1], OTHERS)
 
 
 def last_kernel(r0, r1, r2, r3, compact, base, ranks, powers, lift, state, advanced, held, sem):
@@ -423,12 +422,12 @@
 
     def layer(_, carry):
         received, outgoing, state, compact, ranks, sent, base, kept = carry
-        delta, *outgoing = call(
+        delta, *outgoing, state = call(
             advance_kernel,
-            [live] + blocks,
-            (*received, *outgoing, compact, base, kept, sent, powers, lift, trace),
+            [((comps, SPLIT), F32)] + blocks + [all_columns],
+            (*received, *outgoing, state, compact, base, kept, sent, ranks, powers, lift, trace),
             10**6,
-            {4 + i: 1 + i for i in range(4)},
+            {4 + i: 1 + i for i in range(5)},
         )
         received = exchange(outgoing)
         state, compact, ranks, sent, base, kept = call(

time: 65.1 us -> 66.7 us (1.025)
  the two profiles are of different devices: /device:TPU:19 before, /device:TPU:41 now
where the time goes in v4:
time: 66.7 us; the launch traced here: 66.1 us
  starting transfers between devices  52.2 us (78%)
  Pallas kernels  13.5 us (20%)
    ppermute x16, starting transfers between devices, swapped(): return lax.ppermute(block, axis, pairs + [(j, i) for i, j in pairs])  52.2 us
    pallas_call x7, Pallas kernels, call(): pl.pallas_call(kernel, out_shape=outs, input_output_aliases=aliases, comp...  9.32 us
    pallas_call x1, Pallas kernels, local(): pl.pallas_call(last_kernel, out_specs=pl.BlockSpec(memory_space=pltpu.Mem...  2.69 us
    pallas_call x1, Pallas kernels, local(): pl.pallas_call(first_kernel, in_specs=[pl.BlockSpec(memory_space=pltpu.Me...  1.48 us
  transfers between devices with their start and end apart: 16, of which 0 were waited for; matrix products, arithmetic and copies ran while one was open for 0% of the time, Pallas kernels for 9%

profile of v4, /device:TPU:41, one launch (start us, length us, event | category | flops | bytes accessed | tf_op | source)
XLA Modules:
  0.0 66.1 jit_solution(11301210574591405837)
XLA Ops:
  0.0 1.5 %shard_map.91 = (bf16[64,256]{1,0:T(8,128)(2,1)S(1)}, bf16[64,256]{1,0:T(8,128)(2,1)S(1)}, bf16[64,128]{1,0:T(8,128)(2,1)S(1)}, bf16[64,128]{1,0:T(8,128)(2,1)S(...) custom-call(f32[100,1024]{1,0:T(8,128)} %refs_0_.1, ...), custom_call_target="tpu_custom_call" | custom-call | tf_op jit(solution)/shard_map/pallas_call | solution.py:396
  1.5 11.5 %collective-permute-start.4 = (bf16[64,256]{1,0:T(8,128)(2,1)S(1)}, bf16[64,256]{1,0:T(8,128)(2,1)S(1)}, u32[]{:S(2)}, u32[]{:S(2)}) collective-permute-start(bf16[64,256]{1,0:T(8,128)(2,1)S(1)} %get-tuple-element.353), channel_id=1, source_target_pairs={{8,16},{24,32},{40,48},{56,64},{72,80},{88,96},{104,112},{120,128}... | collective-permute-start | bytes 98312 | tf_op jit(solution)/shard_map/ppermute | solution.py:366
  13.0 1.9 %collective-permute-start.5 = (bf16[64,256]{1,0:T(8,128)(2,1)S(1)}, bf16[64,256]{1,0:T(8,128)(2,1)S(1)}, u32[]{:S(2)}, u32[]{:S(2)}) collective-permute-start(bf16[64,256]{1,0:T(8,128)(2,1)S(1)} %get-tuple-element.354), channel_id=1, source_target_pairs={{0,8},{16,24},{32,40},{48,56},{64,72},{80,88},{96,104},{112,120},{... | collective-permute-start | bytes 98312 | tf_op jit(solution)/shard_map/ppermute | solution.py:366
  14.9 4.0 %collective-permute-start.6 = (bf16[64,128]{1,0:T(8,128)(2,1)S(1)}, bf16[64,128]{1,0:T(8,128)(2,1)S(1)}, u32[]{:S(2)}, u32[]{:S(2)}) collective-permute-start(bf16[64,128]{1,0:T(8,128)(2,1)S(1)} %get-tuple-element.355), channel_id=1, source_target_pairs={{1,2},{3,4},{5,6},{2,1},{4,3},{6,5},{9,10},{11,12},{13,14},{10,9},... | collective-permute-start | bytes 49160 | tf_op jit(solution)/shard_map/ppermute | solution.py:366
  18.9 1.9 %collective-permute-start.7 = (bf16[64,128]{1,0:T(8,128)(2,1)S(1)}, bf16[64,128]{1,0:T(8,128)(2,1)S(1)}, u32[]{:S(2)}, u32[]{:S(2)}) collective-permute-start(bf16[64,128]{1,0:T(8,128)(2,1)S(1)} %get-tuple-element.356), channel_id=1, source_target_pairs={{0,1},{2,3},{4,5},{6,7},{1,0},{3,2},{5,4},{7,6},{8,9},{10,11},{12,... | collective-permute-start | bytes 49160 | tf_op jit(solution)/shard_map/ppermute | solution.py:366
  20.8 1.8 %shard_map.92 = (f32[4,16,384]{2,1,0:T(8,128)S(1)}, s32[8,1024]{1,0:T(8,128)S(1)}, s32[4,768]{1,0:T(4,128)S(1)}, f32[100,384]{1,0:T(8,128)S(1)}, f32[100,384]{1,...) custom-call(f32[100,1024]{1,0:T(8,128)S(1)} %get-tuple-element.357.state, ...), custom_call_target="tpu_custom_call" | custom-call | flops 1000000 | bytes 1048576 | tf_op jit(solution)/shard_map/pallas_call | solution.py:355
  22.6 0.0 collective-permute-done.6
  22.6 0.0 collective-permute-done.7
  22.6 0.0 collective-permute-done.4
  22.6 0.0 collective-permute-done.5
  22.6 40.8 %while.36 = (s32[]{:T(128)}, bf16[64,256]{1,0:T(8,128)(2,1)S(1)}, bf16[64,256]{1,0:T(8,128)(2,1)S(1)}, bf16[64,128]{1,0:T(8,128)(2,1)S(1)}, bf16[64,128]{1,0:T(8...) while((s32[]{:T(128)}, bf16[64,256]{1,0:T(8,128)(2,1)S(1)}, ...), condition=%wide.region_1.0_spmd, body=%wide.region_0.0_spmd.sunk | while | flops 2000002 | bytes 2490709 | solution.py:442
  22.6 1.1 %eval_jaxpr.2 = (f32[100,256]{1,0:T(8,128)S(1)}, bf16[64,256]{1,0:T(8,128)(2,1)S(1)}, bf16[64,256]{1,0:T(8,128)(2,1)S(1)}, bf16[64,128]{1,0:T(8,128)(2,1)S(1)}, ...) custom-call(bf16[64,256]{1,0:T(8,128)(2,1)S(1)} %get-tuple-element.3, ...), custom_call_target="tpu_custom_call", output_to_operand_aliasing={{1}: (4, {}), {2}: (5, {}), {3}: (6, {}), {4}: (7, {}), {5}... | custom-call | flops 1000000 | bytes 1048576 | tf_op jit(solution)/shard_map/while/body/eval_jaxpr/pallas_call | solution.py:355
  23.7 2.7 %collective-permute-start = (bf16[64,256]{1,0:T(8,128)(2,1)S(1)}, bf16[64,256]{1,0:T(8,128)(2,1)S(1)}, u32[]{:S(2)}, u32[]{:S(2)}) collective-permute-start(bf16[64,256]{1,0:T(8,128)(2,1)S(1)} %get-tuple-element.393), channel_id=1, source_target_pairs={{8,16},{24,32},{40,48},{56,64},{72,80},{88,96},{104,112},{120,128}... | collective-permute-start | bytes 98312 | tf_op jit(solution)/shard_map/while/body/eval_jaxpr/ppermute | solution.py:366
  26.5 2.8 %collective-permute-start.1 = (bf16[64,256]{1,0:T(8,128)(2,1)S(1)}, bf16[64,256]{1,0:T(8,128)(2,1)S(1)}, u32[]{:S(2)}, u32[]{:S(2)}) collective-permute-start(bf16[64,256]{1,0:T(8,128)(2,1)S(1)} %get-tuple-element.394), channel_id=1, source_target_pairs={{0,8},{16,24},{32,40},{48,56},{64,72},{80,88},{96,104},{112,120},{... | collective-permute-start | bytes 98312 | tf_op jit(solution)/shard_map/while/body/eval_jaxpr/ppermute | solution.py:366
  29.3 3.8 %collective-permute-start.2 = (bf16[64,128]{1,0:T(8,128)(2,1)S(1)}, bf16[64,128]{1,0:T(8,128)(2,1)S(1)}, u32[]{:S(2)}, u32[]{:S(2)}) collective-permute-start(bf16[64,128]{1,0:T(8,128)(2,1)S(1)} %get-tuple-element.395), channel_id=1, source_target_pairs={{1,2},{3,4},{5,6},{2,1},{4,3},{6,5},{9,10},{11,12},{13,14},{10,9},... | collective-permute-start | bytes 49160 | tf_op jit(solution)/shard_map/while/body/eval_jaxpr/ppermute | solution.py:366
  33.1 1.9 %collective-permute-start.3 = (bf16[64,128]{1,0:T(8,128)(2,1)S(1)}, bf16[64,128]{1,0:T(8,128)(2,1)S(1)}, u32[]{:S(2)}, u32[]{:S(2)}) collective-permute-start(bf16[64,128]{1,0:T(8,128)(2,1)S(1)} %get-tuple-element.396), channel_id=1, source_target_pairs={{0,1},{2,3},{4,5},{6,7},{1,0},{3,2},{5,4},{7,6},{8,9},{10,11},{12,... | collective-permute-start | bytes 49160 | tf_op jit(solution)/shard_map/while/body/eval_jaxpr/ppermute | solution.py:366
  35.0 1.1 %eval_jaxpr.3 = (f32[100,1024]{1,0:T(8,128)S(1)}, f32[4,16,384]{2,1,0:T(8,128)S(1)}, s32[8,1024]{1,0:T(8,128)S(1)}, s32[4,768]{1,0:T(4,128)S(1)}, f32[100,384]{1,0:T(8,128)S(1)}, /*index=5*/f32[100,384]{1,0:T(8,128)S(1)}) custom-call(f32[100,1024]{1,0:T(8,128)S(1)} %get-tuple-element.340.stat, ...), custom_call_target="tpu_custom_call", output_to_operand_aliasing={{0}: (0, {}), {1}: (2, {}), {2}: (3, {}), {3}: (4, {})} | custom-call | flops 1000000 | bytes 1048576 | tf_op jit(solution)/shard_map/while/body/eval_jaxpr/pallas_call | solution.py:355
  36.2 0.0 collective-permute-done.2
  36.2 0.0 collective-permute-done.3
  36.2 0.0 collective-permute-done
  36.2 0.0 collective-permute-done.1
  36.2 1.1 %eval_jaxpr.2 = (f32[100,256]{1,0:T(8,128)S(1)}, bf16[64,256]{1,0:T(8,128)(2,1)S(1)}, bf16[64,256]{1,0:T(8,128)(2,1)S(1)}, bf16[64,128]{1,0:T(8,128)(2,1)S(1)}, ...) custom-call(bf16[64,256]{1,0:T(8,128)(2,1)S(1)} %get-tuple-element.3, ...), custom_call_target="tpu_custom_call", output_to_operand_aliasing={{1}: (4, {}), {2}: (5, {}), {3}: (6, {}), {4}: (7, {}), {5}... | custom-call | flops 1000000 | bytes 1048576 | tf_op jit(solution)/shard_map/while/body/eval_jaxpr/pallas_call | solution.py:355
  37.3 3.8 %collective-permute-start = (bf16[64,256]{1,0:T(8,128)(2,1)S(1)}, bf16[64,256]{1,0:T(8,128)(2,1)S(1)}, u32[]{:S(2)}, u32[]{:S(2)}) collective-permute-start(bf16[64,256]{1,0:T(8,128)(2,1)S(1)} %get-tuple-element.393), channel_id=1, source_target_pairs={{8,16},{24,32},{40,48},{56,64},{72,80},{88,96},{104,112},{120,128}... | collective-permute-start | bytes 98312 | tf_op jit(solution)/shard_map/while/body/eval_jaxpr/ppermute | solution.py:366
  41.1 1.9 %collective-permute-start.1 = (bf16[64,256]{1,0:T(8,128)(2,1)S(1)}, bf16[64,256]{1,0:T(8,128)(2,1)S(1)}, u32[]{:S(2)}, u32[]{:S(2)}) collective-permute-start(bf16[64,256]{1,0:T(8,128)(2,1)S(1)} %get-tuple-element.394), channel_id=1, source_target_pairs={{0,8},{16,24},{32,40},{48,56},{64,72},{80,88},{96,104},{112,120},{... | collective-permute-start | bytes 98312 | tf_op jit(solution)/shard_map/while/body/eval_jaxpr/ppermute | solution.py:366
  43.0 3.5 %collective-permute-start.2 = (bf16[64,128]{1,0:T(8,128)(2,1)S(1)}, bf16[64,128]{1,0:T(8,128)(2,1)S(1)}, u32[]{:S(2)}, u32[]{:S(2)}) collective-permute-start(bf16[64,128]{1,0:T(8,128)(2,1)S(1)} %get-tuple-element.395), channel_id=1, source_target_pairs={{1,2},{3,4},{5,6},{2,1},{4,3},{6,5},{9,10},{11,12},{13,14},{10,9},... | collective-permute-start | bytes 49160 | tf_op jit(solution)/shard_map/while/body/eval_jaxpr/ppermute | solution.py:366
  46.5 1.9 %collective-permute-start.3 = (bf16[64,128]{1,0:T(8,128)(2,1)S(1)}, bf16[64,128]{1,0:T(8,128)(2,1)S(1)}, u32[]{:S(2)}, u32[]{:S(2)}) collective-permute-start(bf16[64,128]{1,0:T(8,128)(2,1)S(1)} %get-tuple-element.396), channel_id=1, source_target_pairs={{0,1},{2,3},{4,5},{6,7},{1,0},{3,2},{5,4},{7,6},{8,9},{10,11},{12,... | collective-permute-start | bytes 49160 | tf_op jit(solution)/shard_map/while/body/eval_jaxpr/ppermute | solution.py:366
  48.5 1.2 %eval_jaxpr.3 = (f32[100,1024]{1,0:T(8,128)S(1)}, f32[4,16,384]{2,1,0:T(8,128)S(1)}, s32[8,1024]{1,0:T(8,128)S(1)}, s32[4,768]{1,0:T(4,128)S(1)}, f32[100,384]{1,0:T(8,128)S(1)}, /*index=5*/f32[100,384]{1,0:T(8,128)S(1)}) custom-call(f32[100,1024]{1,0:T(8,128)S(1)} %get-tuple-element.340.stat, ...), custom_call_target="tpu_custom_call", output_to_operand_aliasing={{0}: (0, {}), {1}: (2, {}), {2}: (3, {}), {3}: (4, {})} | custom-call | flops 1000000 | bytes 1048576 | tf_op jit(solution)/shard_map/while/body/eval_jaxpr/pallas_call | solution.py:355
  49.6 0.0 collective-permute-done.2
  49.6 0.0 collective-permute-done.3
  49.6 0.0 collective-permute-done
  49.6 0.0 collective-permute-done.1
  49.7 1.1 %eval_jaxpr.2 = (f32[100,256]{1,0:T(8,128)S(1)}, bf16[64,256]{1,0:T(8,128)(2,1)S(1)}, bf16[64,256]{1,0:T(8,128)(2,1)S(1)}, bf16[64,128]{1,0:T(8,128)(2,1)S(1)}, ...) custom-call(bf16[64,256]{1,0:T(8,128)(2,1)S(1)} %get-tuple-element.3, ...), custom_call_target="tpu_custom_call", output_to_operand_aliasing={{1}: (4, {}), {2}: (5, {}), {3}: (6, {}), {4}: (7, {}), {5}... | custom-call | flops 1000000 | bytes 1048576 | tf_op jit(solution)/shard_map/while/body/eval_jaxpr/pallas_call | solution.py:355
  50.8 3.6 %collective-permute-start = (bf16[64,256]{1,0:T(8,128)(2,1)S(1)}, bf16[64,256]{1,0:T(8,128)(2,1)S(1)}, u32[]{:S(2)}, u32[]{:S(2)}) collective-permute-start(bf16[64,256]{1,0:T(8,128)(2,1)S(1)} %get-tuple-element.393), channel_id=1, source_target_pairs={{8,16},{24,32},{40,48},{56,64},{72,80},{88,96},{104,112},{120,128}... | collective-permute-start | bytes 98312 | tf_op jit(solution)/shard_map/while/body/eval_jaxpr/ppermute | solution.py:366
  54.4 1.9 %collective-permute-start.1 = (bf16[64,256]{1,0:T(8,128)(2,1)S(1)}, bf16[64,256]{1,0:T(8,128)(2,1)S(1)}, u32[]{:S(2)}, u32[]{:S(2)}) collective-permute-start(bf16[64,256]{1,0:T(8,128)(2,1)S(1)} %get-tuple-element.394), channel_id=1, source_target_pairs={{0,8},{16,24},{32,40},{48,56},{64,72},{80,88},{96,104},{112,120},{... | collective-permute-start | bytes 98312 | tf_op jit(solution)/shard_map/while/body/eval_jaxpr/ppermute | solution.py:366
  56.3 3.2 %collective-permute-start.2 = (bf16[64,128]{1,0:T(8,128)(2,1)S(1)}, bf16[64,128]{1,0:T(8,128)(2,1)S(1)}, u32[]{:S(2)}, u32[]{:S(2)}) collective-permute-start(bf16[64,128]{1,0:T(8,128)(2,1)S(1)} %get-tuple-element.395), channel_id=1, source_target_pairs={{1,2},{3,4},{5,6},{2,1},{4,3},{6,5},{9,10},{11,12},{13,14},{10,9},... | collective-permute-start | bytes 49160 | tf_op jit(solution)/shard_map/while/body/eval_jaxpr/ppermute | solution.py:366
  59.5 1.9 %collective-permute-start.3 = (bf16[64,128]{1,0:T(8,128)(2,1)S(1)}, bf16[64,128]{1,0:T(8,128)(2,1)S(1)}, u32[]{:S(2)}, u32[]{:S(2)}) collective-permute-start(bf16[64,128]{1,0:T(8,128)(2,1)S(1)} %get-tuple-element.396), channel_id=1, source_target_pairs={{0,1},{2,3},{4,5},{6,7},{1,0},{3,2},{5,4},{7,6},{8,9},{10,11},{12,... | collective-permute-start | bytes 49160 | tf_op jit(solution)/shard_map/while/body/eval_jaxpr/ppermute | solution.py:366
  61.5 1.9 %eval_jaxpr.3 = (f32[100,1024]{1,0:T(8,128)S(1)}, f32[4,16,384]{2,1,0:T(8,128)S(1)}, s32[8,1024]{1,0:T(8,128)S(1)}, s32[4,768]{1,0:T(4,128)S(1)}, f32[100,384]{1,0:T(8,128)S(1)}, /*index=5*/f32[100,384]{1,0:T(8,128)S(1)}) custom-call(f32[100,1024]{1,0:T(8,128)S(1)} %get-tuple-element.340.stat, ...), custom_call_target="tpu_custom_call", output_to_operand_aliasing={{0}: (0, {}), {1}: (2, {}), {2}: (3, {}), {3}: (4, {})} | custom-call | flops 1000000 | bytes 1048576 | tf_op jit(solution)/shard_map/while/body/eval_jaxpr/pallas_call | solution.py:355
  63.4 0.0 collective-permute-done.2
  63.4 0.0 collective-permute-done.3
  63.4 0.0 collective-permute-done
  63.4 0.0 collective-permute-done.1
  63.4 2.7 %shard_map.93 = f32[100,1024]{1,0:T(8,128)} custom-call(bf16[64,256]{1,0:T(8,128)(2,1)S(1)} %get-tuple-element.163.r0, bf16[64,256]{1,0:T(8,128)(2,1)S(1)} %get-tuple-element.164.r1, bf16[64,128]{1,0:T(8,128)(2,1)S(1)} %get-tuple-element.165.r2, bf16[64,128]{1,0:T(8,128)(2,1)S(1)} %get-tuple-element.166.r3, f32[4,16,384]{2,1,0:T(8,128)S(1)} %get-tuple-element.167.compact, ...), custom_call_target="tpu_custom_call" | custom-call | tf_op jit(solution)/shard_map/pallas_call | solution.py:445
Async XLA Ops:
  1.5 21.1 %collective-permute-start.4 = (bf16[64,256]{1,0:T(8,128)(2,1)S(1)}, bf16[64,256]{1,0:T(8,128)(2,1)S(1)}, u32[]{:S(2)}, u32[]{:S(2)}) collective-permute-start(bf16[64,256]{1,0:T(8,128)(2,1)S(1)} %get-tuple-element.353), channel_id=1, source_target_pairs={{8,16},{24,32},{40,48},{56,64},{72,80},{88,96},{104,112},{120,128}... | collective-permute-start | bytes 98312 | tf_op jit(solution)/shard_map/ppermute | solution.py:366
  13.0 9.7 %collective-permute-start.5 = (bf16[64,256]{1,0:T(8,128)(2,1)S(1)}, bf16[64,256]{1,0:T(8,128)(2,1)S(1)}, u32[]{:S(2)}, u32[]{:S(2)}) collective-permute-start(bf16[64,256]{1,0:T(8,128)(2,1)S(1)} %get-tuple-element.354), channel_id=1, source_target_pairs={{0,8},{16,24},{32,40},{48,56},{64,72},{80,88},{96,104},{112,120},{... | collective-permute-start | bytes 98312 | tf_op jit(solution)/shard_map/ppermute | solution.py:366
  14.9 7.7 %collective-permute-start.6 = (bf16[64,128]{1,0:T(8,128)(2,1)S(1)}, bf16[64,128]{1,0:T(8,128)(2,1)S(1)}, u32[]{:S(2)}, u32[]{:S(2)}) collective-permute-start(bf16[64,128]{1,0:T(8,128)(2,1)S(1)} %get-tuple-element.355), channel_id=1, source_target_pairs={{1,2},{3,4},{5,6},{2,1},{4,3},{6,5},{9,10},{11,12},{13,14},{10,9},... | collective-permute-start | bytes 49160 | tf_op jit(solution)/shard_map/ppermute | solution.py:366
  18.9 3.7 %collective-permute-start.7 = (bf16[64,128]{1,0:T(8,128)(2,1)S(1)}, bf16[64,128]{1,0:T(8,128)(2,1)S(1)}, u32[]{:S(2)}, u32[]{:S(2)}) collective-permute-start(bf16[64,128]{1,0:T(8,128)(2,1)S(1)} %get-tuple-element.356), channel_id=1, source_target_pairs={{0,1},{2,3},{4,5},{6,7},{1,0},{3,2},{5,4},{7,6},{8,9},{10,11},{12,... | collective-permute-start | bytes 49160 | tf_op jit(solution)/shard_map/ppermute | solution.py:366
  23.7 12.5 %collective-permute-start = (bf16[64,256]{1,0:T(8,128)(2,1)S(1)}, bf16[64,256]{1,0:T(8,128)(2,1)S(1)}, u32[]{:S(2)}, u32[]{:S(2)}) collective-permute-start(bf16[64,256]{1,0:T(8,128)(2,1)S(1)} %get-tuple-element.393), channel_id=1, source_target_pairs={{8,16},{24,32},{40,48},{56,64},{72,80},{88,96},{104,112},{120,128}... | collective-permute-start | bytes 98312 | tf_op jit(solution)/shard_map/while/body/eval_jaxpr/ppermute | solution.py:366
  26.5 9.7 %collective-permute-start.1 = (bf16[64,256]{1,0:T(8,128)(2,1)S(1)}, bf16[64,256]{1,0:T(8,128)(2,1)S(1)}, u32[]{:S(2)}, u32[]{:S(2)}) collective-permute-start(bf16[64,256]{1,0:T(8,128)(2,1)S(1)} %get-tuple-element.394), channel_id=1, source_target_pairs={{0,8},{16,24},{32,40},{48,56},{64,72},{80,88},{96,104},{112,120},{... | collective-permute-start | bytes 98312 | tf_op jit(solution)/shard_map/while/body/eval_jaxpr/ppermute | solution.py:366
  29.3 6.9 %collective-permute-start.2 = (bf16[64,128]{1,0:T(8,128)(2,1)S(1)}, bf16[64,128]{1,0:T(8,128)(2,1)S(1)}, u32[]{:S(2)}, u32[]{:S(2)}) collective-permute-start(bf16[64,128]{1,0:T(8,128)(2,1)S(1)} %get-tuple-element.395), channel_id=1, source_target_pairs={{1,2},{3,4},{5,6},{2,1},{4,3},{6,5},{9,10},{11,12},{13,14},{10,9},... | collective-permute-start | bytes 49160 | tf_op jit(solution)/shard_map/while/body/eval_jaxpr/ppermute | solution.py:366
  33.1 3.1 %collective-permute-start.3 = (bf16[64,128]{1,0:T(8,128)(2,1)S(1)}, bf16[64,128]{1,0:T(8,128)(2,1)S(1)}, u32[]{:S(2)}, u32[]{:S(2)}) collective-permute-start(bf16[64,128]{1,0:T(8,128)(2,1)S(1)} %get-tuple-element.396), channel_id=1, source_target_pairs={{0,1},{2,3},{4,5},{6,7},{1,0},{3,2},{5,4},{7,6},{8,9},{10,11},{12,... | collective-permute-start | bytes 49160 | tf_op jit(solution)/shard_map/while/body/eval_jaxpr/ppermute | solution.py:366
  37.3 12.3 %collective-permute-start = (bf16[64,256]{1,0:T(8,128)(2,1)S(1)}, bf16[64,256]{1,0:T(8,128)(2,1)S(1)}, u32[]{:S(2)}, u32[]{:S(2)}) collective-permute-start(bf16[64,256]{1,0:T(8,128)(2,1)S(1)} %get-tuple-element.393), channel_id=1, source_target_pairs={{8,16},{24,32},{40,48},{56,64},{72,80},{88,96},{104,112},{120,128}... | collective-permute-start | bytes 98312 | tf_op jit(solution)/shard_map/while/body/eval_jaxpr/ppermute | solution.py:366
  41.1 8.5 %collective-permute-start.1 = (bf16[64,256]{1,0:T(8,128)(2,1)S(1)}, bf16[64,256]{1,0:T(8,128)(2,1)S(1)}, u32[]{:S(2)}, u32[]{:S(2)}) collective-permute-start(bf16[64,256]{1,0:T(8,128)(2,1)S(1)} %get-tuple-element.394), channel_id=1, source_target_pairs={{0,8},{16,24},{32,40},{48,56},{64,72},{80,88},{96,104},{112,120},{... | collective-permute-start | bytes 98312 | tf_op jit(solution)/shard_map/while/body/eval_jaxpr/ppermute | solution.py:366
  43.0 6.6 %collective-permute-start.2 = (bf16[64,128]{1,0:T(8,128)(2,1)S(1)}, bf16[64,128]{1,0:T(8,128)(2,1)S(1)}, u32[]{:S(2)}, u32[]{:S(2)}) collective-permute-start(bf16[64,128]{1,0:T(8,128)(2,1)S(1)} %get-tuple-element.395), channel_id=1, source_target_pairs={{1,2},{3,4},{5,6},{2,1},{4,3},{6,5},{9,10},{11,12},{13,14},{10,9},... | collective-permute-start | bytes 49160 | tf_op jit(solution)/shard_map/while/body/eval_jaxpr/ppermute | solution.py:366
  46.5 3.1 %collective-permute-start.3 = (bf16[64,128]{1,0:T(8,128)(2,1)S(1)}, bf16[64,128]{1,0:T(8,128)(2,1)S(1)}, u32[]{:S(2)}, u32[]{:S(2)}) collective-permute-start(bf16[64,128]{1,0:T(8,128)(2,1)S(1)} %get-tuple-element.396), channel_id=1, source_target_pairs={{0,1},{2,3},{4,5},{6,7},{1,0},{3,2},{5,4},{7,6},{8,9},{10,11},{12,... | collective-permute-start | bytes 49160 | tf_op jit(solution)/shard_map/while/body/eval_jaxpr/ppermute | solution.py:366
  50.8 12.6 %collective-permute-start = (bf16[64,256]{1,0:T(8,128)(2,1)S(1)}, bf16[64,256]{1,0:T(8,128)(2,1)S(1)}, u32[]{:S(2)}, u32[]{:S(2)}) collective-permute-start(bf16[64,256]{1,0:T(8,128)(2,1)S(1)} %get-tuple-element.393), channel_id=1, source_target_pairs={{8,16},{24,32},{40,48},{56,64},{72,80},{88,96},{104,112},{120,128}... | collective-permute-start | bytes 98312 | tf_op jit(solution)/shard_map/while/body/eval_jaxpr/ppermute | solution.py:366
  54.4 9.0 %collective-permute-start.1 = (bf16[64,256]{1,0:T(8,128)(2,1)S(1)}, bf16[64,256]{1,0:T(8,128)(2,1)S(1)}, u32[]{:S(2)}, u32[]{:S(2)}) collective-permute-start(bf16[64,256]{1,0:T(8,128)(2,1)S(1)} %get-tuple-element.394), channel_id=1, source_target_pairs={{0,8},{16,24},{32,40},{48,56},{64,72},{80,88},{96,104},{112,120},{... | collective-permute-start | bytes 98312 | tf_op jit(solution)/shard_map/while/body/eval_jaxpr/ppermute | solution.py:366
  56.3 7.0 %collective-permute-start.2 = (bf16[64,128]{1,0:T(8,128)(2,1)S(1)}, bf16[64,128]{1,0:T(8,128)(2,1)S(1)}, u32[]{:S(2)}, u32[]{:S(2)}) collective-permute-start(bf16[64,128]{1,0:T(8,128)(2,1)S(1)} %get-tuple-element.395), channel_id=1, source_target_pairs={{1,2},{3,4},{5,6},{2,1},{4,3},{6,5},{9,10},{11,12},{13,14},{10,9},... | collective-permute-start | bytes 49160 | tf_op jit(solution)/shard_map/while/body/eval_jaxpr/ppermute | solution.py:366
  59.5 3.9 %collective-permute-start.3 = (bf16[64,128]{1,0:T(8,128)(2,1)S(1)}, bf16[64,128]{1,0:T(8,128)(2,1)S(1)}, u32[]{:S(2)}, u32[]{:S(2)}) collective-permute-start(bf16[64,128]{1,0:T(8,128)(2,1)S(1)} %get-tuple-element.396), channel_id=1, source_target_pairs={{0,1},{2,3},{4,5},{6,7},{1,0},{3,2},{5,4},{7,6},{8,9},{10,11},{12,... | collective-permute-start | bytes 49160 | tf_op jit(solution)/shard_map/while/body/eval_jaxpr/ppermute | solution.py:366

commit v5 on v4

--- a/solution.py
+++ b/solution.py
@@ -205,6 +205,7 @@
 
 
 FIRST, OTHERS = slice(0, SPLIT), slice(SPLIT, MAX_LIVE)
+ALL = slice(0, MAX_LIVE)
 
 
 def by_face(columns):
@@ -241,6 +242,8 @@
 
 def local_parts(values, state, compact, *refs):
     local_part(values, compact, FIRST, *refs)
+    for ref in refs[3:]:
+        ref[:, OTHERS] = jnp.zeros((ref.shape[0], MAX_LIVE - SPLIT), F32)
 
     @pl.when(many(compact))
     def _():
@@ -261,16 +264,16 @@
     local_parts(state[...], state, compact[0], volume, lift, trace, base, kept)
 
 
-def scatter(delta, rank, here):
+def scatter(delta, rank):
     parts, second = two_parts(delta)
-    found = mm(parts, hot(rank - here.start, delta.shape[1]))
+    found = mm(parts, hot(rank, MAX_LIVE))
     return found[: delta.shape[0]] + found[second:]
 
 
 def local_kernel(
     state, delta, compact, ranks, sent, volume, lift, trace, new_state, new_compact, new_ranks, new_sent, base, kept
 ):
-    values = state[...] + scatter(delta[...], ranks[0:1], FIRST)
+    values = state[...] + scatter(delta[...], ranks[0:1])
     new_state[...] = values
     tables = [compact[l] for l in range(1, compact.shape[0])]
     for l, table in enumerate(tables):
@@ -307,44 +310,21 @@
     return total
 
 
-def advance_kernel(
-    r0, r1, r2, r3, o0, o1, o2, o3, state, compact, base, kept, sent, ranks, powers, lift, trace,
-    delta, out_0, out_1, out_2, out_3, new_state,
-):
-    rows = compact[0]
-    outgoing = (out_0, out_1, out_2, out_3)
-
-    def part(here, before):
-        place = sent[0:1] - here.start
-        chosen = hot(place, here.stop - here.start)
-        total = taylor_terms((r0, r1, r2, r3), rows, here, base, powers, lift)
-        traces = mm(trace[3 * ROWS :, :], (kept[:, here] + total).astype(BF16)).astype(BF16)
-        before = jnp.concatenate([ref[...] for ref in before], axis=1).astype(F32)
-        inside = jnp.logical_and(place >= 0, place < here.stop - here.start)
-        store_blocks(jnp.where(inside, mm(traces, chosen), before), outgoing)
-        return total
-
-    new_state[...] = state[...]
-    delta[...] = part(FIRST, (o0, o1, o2, o3))
-
-    @pl.when(many(rows))
-    def _():
-        new_state[...] = new_state[...] + scatter(part(OTHERS, outgoing), ranks[0:1], OTHERS)
+def advance_kernel(r0, r1, r2, r3, o0, o1, o2, o3, compact, base, kept, sent, powers, lift, trace, delta, *outgoing):
+    place = sent[0:1]
+    chosen, high = hot(low_of(place), BLOCK), high_of(place)
+    total = taylor_terms((r0, r1, r2, r3), compact[0], ALL, base, powers, lift)
+    delta[...] = total
+    traces = mm(trace[3 * ROWS :, :], (kept[...] + total).astype(BF16))
+    rest = -MAX_LIVE % BLOCK
+    table = jnp.concatenate([traces, jnp.zeros((ROWS, rest), F32)], axis=1).astype(BF16)
+    before = jnp.concatenate([o0[...], o1[...], o2[...], o3[...]], axis=1).astype(F32)
+    store_blocks(choose(mm(stack(table), chosen), high, 0, ROWS, before), outgoing)
 
 
 def last_kernel(r0, r1, r2, r3, compact, base, ranks, powers, lift, state, advanced, held, sem):
-    rows, rank = compact[0], ranks[0:1]
-
-    def part(here, before):
-        total = taylor_terms((r0, r1, r2, r3), rows, here, base, powers, lift)
-        held[...] = before[...] + scatter(total, rank, here)
-
-    part(FIRST, state)
-
-    @pl.when(many(rows))
-    def _():
-        part(OTHERS, held)
-
+    total = taylor_terms((r0, r1, r2, r3), compact[0], ALL, base, powers, lift)
+    held[...] = state[...] + scatter(total, ranks[0:1])
     copy = pltpu.make_async_copy(held, advanced, sem)
     copy.start()
     copy.wait()
@@ -422,12 +402,12 @@
 
     def layer(_, carry):
         received, outgoing, state, compact, ranks, sent, base, kept = carry
-        delta, *outgoing, state = call(
+        delta, *outgoing = call(
             advance_kernel,
-            [((comps, SPLIT), F32)] + blocks + [all_columns],
-            (*received, *outgoing, state, compact, base, kept, sent, ranks, powers, lift, trace),
+            [live] + blocks,
+            (*received, *outgoing, compact, base, kept, sent, powers, lift, trace),
             10**6,
-            {4 + i: 1 + i for i in range(5)},
+            {4 + i: 1 + i for i in range(4)},
         )
         received = exchange(outgoing)
         state, compact, ranks, sent, base, kept = call(

time: 66.7 us -> 64.8 us (0.972)
  the two profiles are of different devices: /device:TPU:41 before, /device:TPU:35 now
where the time goes in v5:
time: 64.8 us; the launch traced here: 64.3 us
  starting transfers between devices  51.9 us (80%)
  Pallas kernels  12 us (19%)
    ppermute x16, starting transfers between devices, swapped(): return lax.ppermute(block, axis, pairs + [(j, i) for i, j in pairs])  51.9 us
    pallas_call x7, Pallas kernels, call(): pl.pallas_call(kernel, out_shape=outs, input_output_aliases=aliases, comp...  8.62 us
    pallas_call x1, Pallas kernels, local(): pl.pallas_call(last_kernel, out_specs=pl.BlockSpec(memory_space=pltpu.Mem...  1.89 us
    pallas_call x1, Pallas kernels, local(): pl.pallas_call(first_kernel, in_specs=[pl.BlockSpec(memory_space=pltpu.Me...  1.48 us
  transfers between devices with their start and end apart: 16, of which 0 were waited for; matrix products, arithmetic and copies ran while one was open for 0% of the time, Pallas kernels for 8%

profile of v5, /device:TPU:35, one launch (start us, length us, event | category | flops | bytes accessed | tf_op | source)
XLA Modules:
  0.0 64.3 jit_solution(8616468141989449457)
XLA Ops:
  0.0 1.5 %shard_map.91 = (bf16[64,256]{1,0:T(8,128)(2,1)S(1)}, bf16[64,256]{1,0:T(8,128)(2,1)S(1)}, bf16[64,128]{1,0:T(8,128)(2,1)S(1)}, bf16[64,128]{1,0:T(8,128)(2,1)S(...) custom-call(f32[100,1024]{1,0:T(8,128)} %refs_0_.1, ...), custom_call_target="tpu_custom_call" | custom-call | tf_op jit(solution)/shard_map/pallas_call | solution.py:376
  1.5 10.6 %collective-permute-start.4 = (bf16[64,256]{1,0:T(8,128)(2,1)S(1)}, bf16[64,256]{1,0:T(8,128)(2,1)S(1)}, u32[]{:S(2)}, u32[]{:S(2)}) collective-permute-start(bf16[64,256]{1,0:T(8,128)(2,1)S(1)} %get-tuple-element.350), channel_id=1, source_target_pairs={{8,16},{24,32},{40,48},{56,64},{72,80},{88,96},{104,112},{120,128}... | collective-permute-start | bytes 98312 | tf_op jit(solution)/shard_map/ppermute | solution.py:346
  12.1 1.9 %collective-permute-start.5 = (bf16[64,256]{1,0:T(8,128)(2,1)S(1)}, bf16[64,256]{1,0:T(8,128)(2,1)S(1)}, u32[]{:S(2)}, u32[]{:S(2)}) collective-permute-start(bf16[64,256]{1,0:T(8,128)(2,1)S(1)} %get-tuple-element.351), channel_id=1, source_target_pairs={{0,8},{16,24},{32,40},{48,56},{64,72},{80,88},{96,104},{112,120},{... | collective-permute-start | bytes 98312 | tf_op jit(solution)/shard_map/ppermute | solution.py:346
  14.0 4.0 %collective-permute-start.6 = (bf16[64,128]{1,0:T(8,128)(2,1)S(1)}, bf16[64,128]{1,0:T(8,128)(2,1)S(1)}, u32[]{:S(2)}, u32[]{:S(2)}) collective-permute-start(bf16[64,128]{1,0:T(8,128)(2,1)S(1)} %get-tuple-element.352), channel_id=1, source_target_pairs={{1,2},{3,4},{5,6},{2,1},{4,3},{6,5},{9,10},{11,12},{13,14},{10,9},... | collective-permute-start | bytes 49160 | tf_op jit(solution)/shard_map/ppermute | solution.py:346
  17.9 1.9 %collective-permute-start.7 = (bf16[64,128]{1,0:T(8,128)(2,1)S(1)}, bf16[64,128]{1,0:T(8,128)(2,1)S(1)}, u32[]{:S(2)}, u32[]{:S(2)}) collective-permute-start(bf16[64,128]{1,0:T(8,128)(2,1)S(1)} %get-tuple-element.353), channel_id=1, source_target_pairs={{0,1},{2,3},{4,5},{6,7},{1,0},{3,2},{5,4},{7,6},{8,9},{10,11},{12,... | collective-permute-start | bytes 49160 | tf_op jit(solution)/shard_map/ppermute | solution.py:346
  19.9 1.8 %shard_map.92 = (f32[4,16,384]{2,1,0:T(8,128)S(1)}, s32[8,1024]{1,0:T(8,128)S(1)}, s32[4,768]{1,0:T(4,128)S(1)}, f32[100,384]{1,0:T(8,128)S(1)}, f32[100,384]{1,...) custom-call(f32[100,1024]{1,0:T(8,128)S(1)} %get-tuple-element.354.state, ...), custom_call_target="tpu_custom_call" | custom-call | flops 1000000 | bytes 1048576 | tf_op jit(solution)/shard_map/pallas_call | solution.py:335
  21.7 0.0 collective-permute-done.6
  21.7 0.0 collective-permute-done.7
  21.7 0.0 collective-permute-done.4
  21.7 0.0 collective-permute-done.5
  21.7 40.7 %while.36 = (s32[]{:T(128)}, bf16[64,256]{1,0:T(8,128)(2,1)S(1)}, bf16[64,256]{1,0:T(8,128)(2,1)S(1)}, bf16[64,128]{1,0:T(8,128)(2,1)S(1)}, bf16[64,128]{1,0:T(8...) while((s32[]{:T(128)}, bf16[64,256]{1,0:T(8,128)(2,1)S(1)}, ...), condition=%wide.region_1.0_spmd, body=%wide.region_0.0_spmd.sunk | while | flops 2000002 | bytes 2490709 | solution.py:422
  21.7 1.1 %eval_jaxpr.2 = (f32[100,384]{1,0:T(8,128)S(1)}, bf16[64,256]{1,0:T(8,128)(2,1)S(1)}, bf16[64,256]{1,0:T(8,128)(2,1)S(1)}, bf16[64,128]{1,0:T(8,128)(2,1)S(1)}, bf16[64,128]{1,0:T(8,128)(2,1)S(1)}) custom-call(bf16[64,256]{1,0:T(8,128)(2,1)S(1)} %get-tuple-element.366.r0, ...), custom_call_target="tpu_custom_call", output_to_operand_aliasing={{1}: (4, {}), {2}: (5, {}), {3}: (6, {}), {4}: (7, {})} | custom-call | flops 1000000 | bytes 1048576 | tf_op jit(solution)/shard_map/while/body/eval_jaxpr/pallas_call | solution.py:335
  22.8 2.7 %collective-permute-start = (bf16[64,256]{1,0:T(8,128)(2,1)S(1)}, bf16[64,256]{1,0:T(8,128)(2,1)S(1)}, u32[]{:S(2)}, u32[]{:S(2)}) collective-permute-start(bf16[64,256]{1,0:T(8,128)(2,1)S(1)} %get-tuple-element.390), channel_id=1, source_target_pairs={{8,16},{24,32},{40,48},{56,64},{72,80},{88,96},{104,112},{120,128}... | collective-permute-start | bytes 98312 | tf_op jit(solution)/shard_map/while/body/eval_jaxpr/ppermute | solution.py:346
  25.6 2.8 %collective-permute-start.1 = (bf16[64,256]{1,0:T(8,128)(2,1)S(1)}, bf16[64,256]{1,0:T(8,128)(2,1)S(1)}, u32[]{:S(2)}, u32[]{:S(2)}) collective-permute-start(bf16[64,256]{1,0:T(8,128)(2,1)S(1)} %get-tuple-element.391), channel_id=1, source_target_pairs={{0,8},{16,24},{32,40},{48,56},{64,72},{80,88},{96,104},{112,120},{... | collective-permute-start | bytes 98312 | tf_op jit(solution)/shard_map/while/body/eval_jaxpr/ppermute | solution.py:346
  28.4 3.5 %collective-permute-start.2 = (bf16[64,128]{1,0:T(8,128)(2,1)S(1)}, bf16[64,128]{1,0:T(8,128)(2,1)S(1)}, u32[]{:S(2)}, u32[]{:S(2)}) collective-permute-start(bf16[64,128]{1,0:T(8,128)(2,1)S(1)} %get-tuple-element.392), channel_id=1, source_target_pairs={{1,2},{3,4},{5,6},{2,1},{4,3},{6,5},{9,10},{11,12},{13,14},{10,9},... | collective-permute-start | bytes 49160 | tf_op jit(solution)/shard_map/while/body/eval_jaxpr/ppermute | solution.py:346
  31.9 1.9 %collective-permute-start.3 = (bf16[64,128]{1,0:T(8,128)(2,1)S(1)}, bf16[64,128]{1,0:T(8,128)(2,1)S(1)}, u32[]{:S(2)}, u32[]{:S(2)}) collective-permute-start(bf16[64,128]{1,0:T(8,128)(2,1)S(1)} %get-tuple-element.393), channel_id=1, source_target_pairs={{0,1},{2,3},{4,5},{6,7},{1,0},{3,2},{5,4},{7,6},{8,9},{10,11},{12,... | collective-permute-start | bytes 49160 | tf_op jit(solution)/shard_map/while/body/eval_jaxpr/ppermute | solution.py:346
  33.8 1.2 %eval_jaxpr.3 = (f32[100,1024]{1,0:T(8,128)S(1)}, f32[4,16,384]{2,1,0:T(8,128)S(1)}, s32[8,1024]{1,0:T(8,128)S(1)}, s32[4,768]{1,0:T(4,128)S(1)}, f32[100,384]{1,0:T(8,128)S(1)}, /*index=5*/f32[100,384]{1,0:T(8,128)S(1)}) custom-call(f32[100,1024]{1,0:T(8,128)S(1)} %get-tuple-element.374.stat, ...), custom_call_target="tpu_custom_call", output_to_operand_aliasing={{0}: (0, {}), {1}: (2, {}), {2}: (3, {}), {3}: (4, {})} | custom-call | flops 1000000 | bytes 1048576 | tf_op jit(solution)/shard_map/while/body/eval_jaxpr/pallas_call | solution.py:335
  35.0 0.0 collective-permute-done.2
  35.0 0.0 collective-permute-done.3
  35.0 0.0 collective-permute-done
  35.1 0.0 collective-permute-done.1
  35.1 1.1 %eval_jaxpr.2 = (f32[100,384]{1,0:T(8,128)S(1)}, bf16[64,256]{1,0:T(8,128)(2,1)S(1)}, bf16[64,256]{1,0:T(8,128)(2,1)S(1)}, bf16[64,128]{1,0:T(8,128)(2,1)S(1)}, bf16[64,128]{1,0:T(8,128)(2,1)S(1)}) custom-call(bf16[64,256]{1,0:T(8,128)(2,1)S(1)} %get-tuple-element.366.r0, ...), custom_call_target="tpu_custom_call", output_to_operand_aliasing={{1}: (4, {}), {2}: (5, {}), {3}: (6, {}), {4}: (7, {})} | custom-call | flops 1000000 | bytes 1048576 | tf_op jit(solution)/shard_map/while/body/eval_jaxpr/pallas_call | solution.py:335
  36.2 5.0 %collective-permute-start = (bf16[64,256]{1,0:T(8,128)(2,1)S(1)}, bf16[64,256]{1,0:T(8,128)(2,1)S(1)}, u32[]{:S(2)}, u32[]{:S(2)}) collective-permute-start(bf16[64,256]{1,0:T(8,128)(2,1)S(1)} %get-tuple-element.390), channel_id=1, source_target_pairs={{8,16},{24,32},{40,48},{56,64},{72,80},{88,96},{104,112},{120,128}... | collective-permute-start | bytes 98312 | tf_op jit(solution)/shard_map/while/body/eval_jaxpr/ppermute | solution.py:346
  41.1 1.9 %collective-permute-start.1 = (bf16[64,256]{1,0:T(8,128)(2,1)S(1)}, bf16[64,256]{1,0:T(8,128)(2,1)S(1)}, u32[]{:S(2)}, u32[]{:S(2)}) collective-permute-start(bf16[64,256]{1,0:T(8,128)(2,1)S(1)} %get-tuple-element.391), channel_id=1, source_target_pairs={{0,8},{16,24},{32,40},{48,56},{64,72},{80,88},{96,104},{112,120},{... | collective-permute-start | bytes 98312 | tf_op jit(solution)/shard_map/while/body/eval_jaxpr/ppermute | solution.py:346
  43.1 2.4 %collective-permute-start.2 = (bf16[64,128]{1,0:T(8,128)(2,1)S(1)}, bf16[64,128]{1,0:T(8,128)(2,1)S(1)}, u32[]{:S(2)}, u32[]{:S(2)}) collective-permute-start(bf16[64,128]{1,0:T(8,128)(2,1)S(1)} %get-tuple-element.392), channel_id=1, source_target_pairs={{1,2},{3,4},{5,6},{2,1},{4,3},{6,5},{9,10},{11,12},{13,14},{10,9},... | collective-permute-start | bytes 49160 | tf_op jit(solution)/shard_map/while/body/eval_jaxpr/ppermute | solution.py:346
  45.4 2.4 %collective-permute-start.3 = (bf16[64,128]{1,0:T(8,128)(2,1)S(1)}, bf16[64,128]{1,0:T(8,128)(2,1)S(1)}, u32[]{:S(2)}, u32[]{:S(2)}) collective-permute-start(bf16[64,128]{1,0:T(8,128)(2,1)S(1)} %get-tuple-element.393), channel_id=1, source_target_pairs={{0,1},{2,3},{4,5},{6,7},{1,0},{3,2},{5,4},{7,6},{8,9},{10,11},{12,... | collective-permute-start | bytes 49160 | tf_op jit(solution)/shard_map/while/body/eval_jaxpr/ppermute | solution.py:346
  47.9 1.2 %eval_jaxpr.3 = (f32[100,1024]{1,0:T(8,128)S(1)}, f32[4,16,384]{2,1,0:T(8,128)S(1)}, s32[8,1024]{1,0:T(8,128)S(1)}, s32[4,768]{1,0:T(4,128)S(1)}, f32[100,384]{1,0:T(8,128)S(1)}, /*index=5*/f32[100,384]{1,0:T(8,128)S(1)}) custom-call(f32[100,1024]{1,0:T(8,128)S(1)} %get-tuple-element.374.stat, ...), custom_call_target="tpu_custom_call", output_to_operand_aliasing={{0}: (0, {}), {1}: (2, {}), {2}: (3, {}), {3}: (4, {})} | custom-call | flops 1000000 | bytes 1048576 | tf_op jit(solution)/shard_map/while/body/eval_jaxpr/pallas_call | solution.py:335
  49.0 0.0 collective-permute-done.2
  49.0 0.0 collective-permute-done.3
  49.1 0.0 collective-permute-done
  49.1 0.0 collective-permute-done.1
  49.1 1.1 %eval_jaxpr.2 = (f32[100,384]{1,0:T(8,128)S(1)}, bf16[64,256]{1,0:T(8,128)(2,1)S(1)}, bf16[64,256]{1,0:T(8,128)(2,1)S(1)}, bf16[64,128]{1,0:T(8,128)(2,1)S(1)}, bf16[64,128]{1,0:T(8,128)(2,1)S(1)}) custom-call(bf16[64,256]{1,0:T(8,128)(2,1)S(1)} %get-tuple-element.366.r0, ...), custom_call_target="tpu_custom_call", output_to_operand_aliasing={{1}: (4, {}), {2}: (5, {}), {3}: (6, {}), {4}: (7, {})} | custom-call | flops 1000000 | bytes 1048576 | tf_op jit(solution)/shard_map/while/body/eval_jaxpr/pallas_call | solution.py:335
  50.2 3.6 %collective-permute-start = (bf16[64,256]{1,0:T(8,128)(2,1)S(1)}, bf16[64,256]{1,0:T(8,128)(2,1)S(1)}, u32[]{:S(2)}, u32[]{:S(2)}) collective-permute-start(bf16[64,256]{1,0:T(8,128)(2,1)S(1)} %get-tuple-element.390), channel_id=1, source_target_pairs={{8,16},{24,32},{40,48},{56,64},{72,80},{88,96},{104,112},{120,128}... | collective-permute-start | bytes 98312 | tf_op jit(solution)/shard_map/while/body/eval_jaxpr/ppermute | solution.py:346
  53.8 1.9 %collective-permute-start.1 = (bf16[64,256]{1,0:T(8,128)(2,1)S(1)}, bf16[64,256]{1,0:T(8,128)(2,1)S(1)}, u32[]{:S(2)}, u32[]{:S(2)}) collective-permute-start(bf16[64,256]{1,0:T(8,128)(2,1)S(1)} %get-tuple-element.391), channel_id=1, source_target_pairs={{0,8},{16,24},{32,40},{48,56},{64,72},{80,88},{96,104},{112,120},{... | collective-permute-start | bytes 98312 | tf_op jit(solution)/shard_map/while/body/eval_jaxpr/ppermute | solution.py:346
  55.8 3.0 %collective-permute-start.2 = (bf16[64,128]{1,0:T(8,128)(2,1)S(1)}, bf16[64,128]{1,0:T(8,128)(2,1)S(1)}, u32[]{:S(2)}, u32[]{:S(2)}) collective-permute-start(bf16[64,128]{1,0:T(8,128)(2,1)S(1)} %get-tuple-element.392), channel_id=1, source_target_pairs={{1,2},{3,4},{5,6},{2,1},{4,3},{6,5},{9,10},{11,12},{13,14},{10,9},... | collective-permute-start | bytes 49160 | tf_op jit(solution)/shard_map/while/body/eval_jaxpr/ppermute | solution.py:346
  58.8 2.4 %collective-permute-start.3 = (bf16[64,128]{1,0:T(8,128)(2,1)S(1)}, bf16[64,128]{1,0:T(8,128)(2,1)S(1)}, u32[]{:S(2)}, u32[]{:S(2)}) collective-permute-start(bf16[64,128]{1,0:T(8,128)(2,1)S(1)} %get-tuple-element.393), channel_id=1, source_target_pairs={{0,1},{2,3},{4,5},{6,7},{1,0},{3,2},{5,4},{7,6},{8,9},{10,11},{12,... | collective-permute-start | bytes 49160 | tf_op jit(solution)/shard_map/while/body/eval_jaxpr/ppermute | solution.py:346
  61.2 1.2 %eval_jaxpr.3 = (f32[100,1024]{1,0:T(8,128)S(1)}, f32[4,16,384]{2,1,0:T(8,128)S(1)}, s32[8,1024]{1,0:T(8,128)S(1)}, s32[4,768]{1,0:T(4,128)S(1)}, f32[100,384]{1,0:T(8,128)S(1)}, /*index=5*/f32[100,384]{1,0:T(8,128)S(1)}) custom-call(f32[100,1024]{1,0:T(8,128)S(1)} %get-tuple-element.374.stat, ...), custom_call_target="tpu_custom_call", output_to_operand_aliasing={{0}: (0, {}), {1}: (2, {}), {2}: (3, {}), {3}: (4, {})} | custom-call | flops 1000000 | bytes 1048576 | tf_op jit(solution)/shard_map/while/body/eval_jaxpr/pallas_call | solution.py:335
  62.4 0.0 collective-permute-done.2
  62.4 0.0 collective-permute-done.3
  62.4 0.0 collective-permute-done
  62.4 0.0 collective-permute-done.1
  62.4 1.9 %shard_map.93 = f32[100,1024]{1,0:T(8,128)} custom-call(bf16[64,256]{1,0:T(8,128)(2,1)S(1)} %get-tuple-element.162.r0, bf16[64,256]{1,0:T(8,128)(2,1)S(1)} %get-tuple-element.163.r1, bf16[64,128]{1,0:T(8,128)(2,1)S(1)} %get-tuple-element.164.r2, bf16[64,128]{1,0:T(8,128)(2,1)S(1)} %get-tuple-element.165.r3, f32[4,16,384]{2,1,0:T(8,128)S(1)} %get-tuple-element.166.compact, ...), custom_call_target="tpu_custom_call" | custom-call | tf_op jit(solution)/shard_map/pallas_call | solution.py:425
Async XLA Ops:
  1.5 20.2 %collective-permute-start.4 = (bf16[64,256]{1,0:T(8,128)(2,1)S(1)}, bf16[64,256]{1,0:T(8,128)(2,1)S(1)}, u32[]{:S(2)}, u32[]{:S(2)}) collective-permute-start(bf16[64,256]{1,0:T(8,128)(2,1)S(1)} %get-tuple-element.350), channel_id=1, source_target_pairs={{8,16},{24,32},{40,48},{56,64},{72,80},{88,96},{104,112},{120,128}... | collective-permute-start | bytes 98312 | tf_op jit(solution)/shard_map/ppermute | solution.py:346
  12.1 9.7 %collective-permute-start.5 = (bf16[64,256]{1,0:T(8,128)(2,1)S(1)}, bf16[64,256]{1,0:T(8,128)(2,1)S(1)}, u32[]{:S(2)}, u32[]{:S(2)}) collective-permute-start(bf16[64,256]{1,0:T(8,128)(2,1)S(1)} %get-tuple-element.351), channel_id=1, source_target_pairs={{0,8},{16,24},{32,40},{48,56},{64,72},{80,88},{96,104},{112,120},{... | collective-permute-start | bytes 98312 | tf_op jit(solution)/shard_map/ppermute | solution.py:346
  14.0 7.7 %collective-permute-start.6 = (bf16[64,128]{1,0:T(8,128)(2,1)S(1)}, bf16[64,128]{1,0:T(8,128)(2,1)S(1)}, u32[]{:S(2)}, u32[]{:S(2)}) collective-permute-start(bf16[64,128]{1,0:T(8,128)(2,1)S(1)} %get-tuple-element.352), channel_id=1, source_target_pairs={{1,2},{3,4},{5,6},{2,1},{4,3},{6,5},{9,10},{11,12},{13,14},{10,9},... | collective-permute-start | bytes 49160 | tf_op jit(solution)/shard_map/ppermute | solution.py:346
  17.9 3.7 %collective-permute-start.7 = (bf16[64,128]{1,0:T(8,128)(2,1)S(1)}, bf16[64,128]{1,0:T(8,128)(2,1)S(1)}, u32[]{:S(2)}, u32[]{:S(2)}) collective-permute-start(bf16[64,128]{1,0:T(8,128)(2,1)S(1)} %get-tuple-element.353), channel_id=1, source_target_pairs={{0,1},{2,3},{4,5},{6,7},{1,0},{3,2},{5,4},{7,6},{8,9},{10,11},{12,... | collective-permute-start | bytes 49160 | tf_op jit(solution)/shard_map/ppermute | solution.py:346
  22.8 12.2 %collective-permute-start = (bf16[64,256]{1,0:T(8,128)(2,1)S(1)}, bf16[64,256]{1,0:T(8,128)(2,1)S(1)}, u32[]{:S(2)}, u32[]{:S(2)}) collective-permute-start(bf16[64,256]{1,0:T(8,128)(2,1)S(1)} %get-tuple-element.390), channel_id=1, source_target_pairs={{8,16},{24,32},{40,48},{56,64},{72,80},{88,96},{104,112},{120,128}... | collective-permute-start | bytes 98312 | tf_op jit(solution)/shard_map/while/body/eval_jaxpr/ppermute | solution.py:346
  25.6 9.5 %collective-permute-start.1 = (bf16[64,256]{1,0:T(8,128)(2,1)S(1)}, bf16[64,256]{1,0:T(8,128)(2,1)S(1)}, u32[]{:S(2)}, u32[]{:S(2)}) collective-permute-start(bf16[64,256]{1,0:T(8,128)(2,1)S(1)} %get-tuple-element.391), channel_id=1, source_target_pairs={{0,8},{16,24},{32,40},{48,56},{64,72},{80,88},{96,104},{112,120},{... | collective-permute-start | bytes 98312 | tf_op jit(solution)/shard_map/while/body/eval_jaxpr/ppermute | solution.py:346
  28.4 6.6 %collective-permute-start.2 = (bf16[64,128]{1,0:T(8,128)(2,1)S(1)}, bf16[64,128]{1,0:T(8,128)(2,1)S(1)}, u32[]{:S(2)}, u32[]{:S(2)}) collective-permute-start(bf16[64,128]{1,0:T(8,128)(2,1)S(1)} %get-tuple-element.392), channel_id=1, source_target_pairs={{1,2},{3,4},{5,6},{2,1},{4,3},{6,5},{9,10},{11,12},{13,14},{10,9},... | collective-permute-start | bytes 49160 | tf_op jit(solution)/shard_map/while/body/eval_jaxpr/ppermute | solution.py:346
  31.9 3.1 %collective-permute-start.3 = (bf16[64,128]{1,0:T(8,128)(2,1)S(1)}, bf16[64,128]{1,0:T(8,128)(2,1)S(1)}, u32[]{:S(2)}, u32[]{:S(2)}) collective-permute-start(bf16[64,128]{1,0:T(8,128)(2,1)S(1)} %get-tuple-element.393), channel_id=1, source_target_pairs={{0,1},{2,3},{4,5},{6,7},{1,0},{3,2},{5,4},{7,6},{8,9},{10,11},{12,... | collective-permute-start | bytes 49160 | tf_op jit(solution)/shard_map/while/body/eval_jaxpr/ppermute | solution.py:346
  36.2 12.9 %collective-permute-start = (bf16[64,256]{1,0:T(8,128)(2,1)S(1)}, bf16[64,256]{1,0:T(8,128)(2,1)S(1)}, u32[]{:S(2)}, u32[]{:S(2)}) collective-permute-start(bf16[64,256]{1,0:T(8,128)(2,1)S(1)} %get-tuple-element.390), channel_id=1, source_target_pairs={{8,16},{24,32},{40,48},{56,64},{72,80},{88,96},{104,112},{120,128}... | collective-permute-start | bytes 98312 | tf_op jit(solution)/shard_map/while/body/eval_jaxpr/ppermute | solution.py:346
  41.1 7.9 %collective-permute-start.1 = (bf16[64,256]{1,0:T(8,128)(2,1)S(1)}, bf16[64,256]{1,0:T(8,128)(2,1)S(1)}, u32[]{:S(2)}, u32[]{:S(2)}) collective-permute-start(bf16[64,256]{1,0:T(8,128)(2,1)S(1)} %get-tuple-element.391), channel_id=1, source_target_pairs={{0,8},{16,24},{32,40},{48,56},{64,72},{80,88},{96,104},{112,120},{... | collective-permute-start | bytes 98312 | tf_op jit(solution)/shard_map/while/body/eval_jaxpr/ppermute | solution.py:346
  43.1 6.0 %collective-permute-start.2 = (bf16[64,128]{1,0:T(8,128)(2,1)S(1)}, bf16[64,128]{1,0:T(8,128)(2,1)S(1)}, u32[]{:S(2)}, u32[]{:S(2)}) collective-permute-start(bf16[64,128]{1,0:T(8,128)(2,1)S(1)} %get-tuple-element.392), channel_id=1, source_target_pairs={{1,2},{3,4},{5,6},{2,1},{4,3},{6,5},{9,10},{11,12},{13,14},{10,9},... | collective-permute-start | bytes 49160 | tf_op jit(solution)/shard_map/while/body/eval_jaxpr/ppermute | solution.py:346
  45.4 3.6 %collective-permute-start.3 = (bf16[64,128]{1,0:T(8,128)(2,1)S(1)}, bf16[64,128]{1,0:T(8,128)(2,1)S(1)}, u32[]{:S(2)}, u32[]{:S(2)}) collective-permute-start(bf16[64,128]{1,0:T(8,128)(2,1)S(1)} %get-tuple-element.393), channel_id=1, source_target_pairs={{0,1},{2,3},{4,5},{6,7},{1,0},{3,2},{5,4},{7,6},{8,9},{10,11},{12,... | collective-permute-start | bytes 49160 | tf_op jit(solution)/shard_map/while/body/eval_jaxpr/ppermute | solution.py:346
  50.2 12.2 %collective-permute-start = (bf16[64,256]{1,0:T(8,128)(2,1)S(1)}, bf16[64,256]{1,0:T(8,128)(2,1)S(1)}, u32[]{:S(2)}, u32[]{:S(2)}) collective-permute-start(bf16[64,256]{1,0:T(8,128)(2,1)S(1)} %get-tuple-element.390), channel_id=1, source_target_pairs={{8,16},{24,32},{40,48},{56,64},{72,80},{88,96},{104,112},{120,128}... | collective-permute-start | bytes 98312 | tf_op jit(solution)/shard_map/while/body/eval_jaxpr/ppermute | solution.py:346
  53.8 8.6 %collective-permute-start.1 = (bf16[64,256]{1,0:T(8,128)(2,1)S(1)}, bf16[64,256]{1,0:T(8,128)(2,1)S(1)}, u32[]{:S(2)}, u32[]{:S(2)}) collective-permute-start(bf16[64,256]{1,0:T(8,128)(2,1)S(1)} %get-tuple-element.391), channel_id=1, source_target_pairs={{0,8},{16,24},{32,40},{48,56},{64,72},{80,88},{96,104},{112,120},{... | collective-permute-start | bytes 98312 | tf_op jit(solution)/shard_map/while/body/eval_jaxpr/ppermute | solution.py:346
  55.8 6.6 %collective-permute-start.2 = (bf16[64,128]{1,0:T(8,128)(2,1)S(1)}, bf16[64,128]{1,0:T(8,128)(2,1)S(1)}, u32[]{:S(2)}, u32[]{:S(2)}) collective-permute-start(bf16[64,128]{1,0:T(8,128)(2,1)S(1)} %get-tuple-element.392), channel_id=1, source_target_pairs={{1,2},{3,4},{5,6},{2,1},{4,3},{6,5},{9,10},{11,12},{13,14},{10,9},... | collective-permute-start | bytes 49160 | tf_op jit(solution)/shard_map/while/body/eval_jaxpr/ppermute | solution.py:346
  58.8 3.6 %collective-permute-start.3 = (bf16[64,128]{1,0:T(8,128)(2,1)S(1)}, bf16[64,128]{1,0:T(8,128)(2,1)S(1)}, u32[]{:S(2)}, u32[]{:S(2)}) collective-permute-start(bf16[64,128]{1,0:T(8,128)(2,1)S(1)} %get-tuple-element.393), channel_id=1, source_target_pairs={{0,1},{2,3},{4,5},{6,7},{1,0},{3,2},{5,4},{7,6},{8,9},{10,11},{12,... | collective-permute-start | bytes 49160 | tf_op jit(solution)/shard_map/while/body/eval_jaxpr/ppermute | solution.py:346

commit v6 on v5

--- a/solution.py
+++ b/solution.py
@@ -264,16 +264,16 @@
     local_parts(state[...], state, compact[0], volume, lift, trace, base, kept)
 
 
-def scatter(delta, rank):
+def scatter(delta, rank, here):
     parts, second = two_parts(delta)
-    found = mm(parts, hot(rank, MAX_LIVE))
+    found = mm(parts, hot(rank - here.start, delta.shape[1]))
     return found[: delta.shape[0]] + found[second:]
 
 
 def local_kernel(
     state, delta, compact, ranks, sent, volume, lift, trace, new_state, new_compact, new_ranks, new_sent, base, kept
 ):
-    values = state[...] + scatter(delta[...], ranks[0:1])
+    values = state[...] + scatter(delta[...], ranks[0:1], ALL)
     new_state[...] = values
     tables = [compact[l] for l in range(1, compact.shape[0])]
     for l, table in enumerate(tables):
@@ -323,8 +323,18 @@
 
 
 def last_kernel(r0, r1, r2, r3, compact, base, ranks, powers, lift, state, advanced, held, sem):
-    total = taylor_terms((r0, r1, r2, r3), compact[0], ALL, base, powers, lift)
-    held[...] = state[...] + scatter(total, ranks[0:1])
+    rows = compact[0]
+
+    def part(here, before):
+        total = taylor_terms((r0, r1, r2, r3), rows, here, base, powers, lift)
+        held[...] = before[...] + scatter(total, ranks[0:1], here)
+
+    part(FIRST, state)
+
+    @pl.when(many(rows))
+    def _():
+        part(OTHERS, held)
+
     copy = pltpu.make_async_copy(held, advanced, sem)
     copy.start()
     copy.wait()

time: 64.8 us -> 64.7 us (level)
  no operation moved by 1% of the time
where the time goes in v6:
time: 64.7 us; the launch traced here: 64.2 us
  starting transfers between devices  51.9 us (80%)
  Pallas kernels  11.9 us (18%)
    ppermute x16, starting transfers between devices, swapped(): return lax.ppermute(block, axis, pairs + [(j, i) for i, j in pairs])  51.9 us
    pallas_call x7, Pallas kernels, call(): pl.pallas_call(kernel, out_shape=outs, input_output_aliases=aliases, comp...  8.62 us
    pallas_call x1, Pallas kernels, local(): pl.pallas_call(last_kernel, out_specs=pl.BlockSpec(memory_space=pltpu.Mem...  1.76 us
    pallas_call x1, Pallas kernels, local(): pl.pallas_call(first_kernel, in_specs=[pl.BlockSpec(memory_space=pltpu.Me...  1.48 us
  transfers between devices with their start and end apart: 16, of which 0 were waited for; matrix products, arithmetic and copies ran while one was open for 0% of the time, Pallas kernels for 8%

profile of v6, /device:TPU:35, one launch (start us, length us, event | category | flops | bytes accessed | tf_op | source)
XLA Modules:
  0.0 64.2 jit_solution(9678360190531696282)
XLA Ops:
  0.0 1.5 %shard_map.91 = (bf16[64,256]{1,0:T(8,128)(2,1)S(1)}, bf16[64,256]{1,0:T(8,128)(2,1)S(1)}, bf16[64,128]{1,0:T(8,128)(2,1)S(1)}, bf16[64,128]{1,0:T(8,128)(2,1)S(...) custom-call(f32[100,1024]{1,0:T(8,128)} %refs_0_.1, ...), custom_call_target="tpu_custom_call" | custom-call | tf_op jit(solution)/shard_map/pallas_call | solution.py:386
  1.5 10.6 %collective-permute-start.4 = (bf16[64,256]{1,0:T(8,128)(2,1)S(1)}, bf16[64,256]{1,0:T(8,128)(2,1)S(1)}, u32[]{:S(2)}, u32[]{:S(2)}) collective-permute-start(bf16[64,256]{1,0:T(8,128)(2,1)S(1)} %get-tuple-element.350), channel_id=1, source_target_pairs={{8,16},{24,32},{40,48},{56,64},{72,80},{88,96},{104,112},{120,128}... | collective-permute-start | bytes 98312 | tf_op jit(solution)/shard_map/ppermute | solution.py:356
  12.1 1.9 %collective-permute-start.5 = (bf16[64,256]{1,0:T(8,128)(2,1)S(1)}, bf16[64,256]{1,0:T(8,128)(2,1)S(1)}, u32[]{:S(2)}, u32[]{:S(2)}) collective-permute-start(bf16[64,256]{1,0:T(8,128)(2,1)S(1)} %get-tuple-element.351), channel_id=1, source_target_pairs={{0,8},{16,24},{32,40},{48,56},{64,72},{80,88},{96,104},{112,120},{... | collective-permute-start | bytes 98312 | tf_op jit(solution)/shard_map/ppermute | solution.py:356
  14.0 4.0 %collective-permute-start.6 = (bf16[64,128]{1,0:T(8,128)(2,1)S(1)}, bf16[64,128]{1,0:T(8,128)(2,1)S(1)}, u32[]{:S(2)}, u32[]{:S(2)}) collective-permute-start(bf16[64,128]{1,0:T(8,128)(2,1)S(1)} %get-tuple-element.352), channel_id=1, source_target_pairs={{1,2},{3,4},{5,6},{2,1},{4,3},{6,5},{9,10},{11,12},{13,14},{10,9},... | collective-permute-start | bytes 49160 | tf_op jit(solution)/shard_map/ppermute | solution.py:356
  17.9 1.9 %collective-permute-start.7 = (bf16[64,128]{1,0:T(8,128)(2,1)S(1)}, bf16[64,128]{1,0:T(8,128)(2,1)S(1)}, u32[]{:S(2)}, u32[]{:S(2)}) collective-permute-start(bf16[64,128]{1,0:T(8,128)(2,1)S(1)} %get-tuple-element.353), channel_id=1, source_target_pairs={{0,1},{2,3},{4,5},{6,7},{1,0},{3,2},{5,4},{7,6},{8,9},{10,11},{12,... | collective-permute-start | bytes 49160 | tf_op jit(solution)/shard_map/ppermute | solution.py:356
  19.9 1.8 %shard_map.92 = (f32[4,16,384]{2,1,0:T(8,128)S(1)}, s32[8,1024]{1,0:T(8,128)S(1)}, s32[4,768]{1,0:T(4,128)S(1)}, f32[100,384]{1,0:T(8,128)S(1)}, f32[100,384]{1,...) custom-call(f32[100,1024]{1,0:T(8,128)S(1)} %get-tuple-element.354.state, ...), custom_call_target="tpu_custom_call" | custom-call | flops 1000000 | bytes 1048576 | tf_op jit(solution)/shard_map/pallas_call | solution.py:345
  21.7 0.0 collective-permute-done.6
  21.7 0.0 collective-permute-done.7
  21.7 0.0 collective-permute-done.4
  21.7 0.0 collective-permute-done.5
  21.7 40.7 %while.36 = (s32[]{:T(128)}, bf16[64,256]{1,0:T(8,128)(2,1)S(1)}, bf16[64,256]{1,0:T(8,128)(2,1)S(1)}, bf16[64,128]{1,0:T(8,128)(2,1)S(1)}, bf16[64,128]{1,0:T(8...) while((s32[]{:T(128)}, bf16[64,256]{1,0:T(8,128)(2,1)S(1)}, ...), condition=%wide.region_1.0_spmd, body=%wide.region_0.0_spmd.sunk | while | flops 2000002 | bytes 2490709 | solution.py:432
  21.7 1.1 %eval_jaxpr.2 = (f32[100,384]{1,0:T(8,128)S(1)}, bf16[64,256]{1,0:T(8,128)(2,1)S(1)}, bf16[64,256]{1,0:T(8,128)(2,1)S(1)}, bf16[64,128]{1,0:T(8,128)(2,1)S(1)}, bf16[64,128]{1,0:T(8,128)(2,1)S(1)}) custom-call(bf16[64,256]{1,0:T(8,128)(2,1)S(1)} %get-tuple-element.366.r0, ...), custom_call_target="tpu_custom_call", output_to_operand_aliasing={{1}: (4, {}), {2}: (5, {}), {3}: (6, {}), {4}: (7, {})} | custom-call | flops 1000000 | bytes 1048576 | tf_op jit(solution)/shard_map/while/body/eval_jaxpr/pallas_call | solution.py:345
  22.8 2.7 %collective-permute-start = (bf16[64,256]{1,0:T(8,128)(2,1)S(1)}, bf16[64,256]{1,0:T(8,128)(2,1)S(1)}, u32[]{:S(2)}, u32[]{:S(2)}) collective-permute-start(bf16[64,256]{1,0:T(8,128)(2,1)S(1)} %get-tuple-element.390), channel_id=1, source_target_pairs={{8,16},{24,32},{40,48},{56,64},{72,80},{88,96},{104,112},{120,128}... | collective-permute-start | bytes 98312 | tf_op jit(solution)/shard_map/while/body/eval_jaxpr/ppermute | solution.py:356
  25.6 2.8 %collective-permute-start.1 = (bf16[64,256]{1,0:T(8,128)(2,1)S(1)}, bf16[64,256]{1,0:T(8,128)(2,1)S(1)}, u32[]{:S(2)}, u32[]{:S(2)}) collective-permute-start(bf16[64,256]{1,0:T(8,128)(2,1)S(1)} %get-tuple-element.391), channel_id=1, source_target_pairs={{0,8},{16,24},{32,40},{48,56},{64,72},{80,88},{96,104},{112,120},{... | collective-permute-start | bytes 98312 | tf_op jit(solution)/shard_map/while/body/eval_jaxpr/ppermute | solution.py:356
  28.4 3.5 %collective-permute-start.2 = (bf16[64,128]{1,0:T(8,128)(2,1)S(1)}, bf16[64,128]{1,0:T(8,128)(2,1)S(1)}, u32[]{:S(2)}, u32[]{:S(2)}) collective-permute-start(bf16[64,128]{1,0:T(8,128)(2,1)S(1)} %get-tuple-element.392), channel_id=1, source_target_pairs={{1,2},{3,4},{5,6},{2,1},{4,3},{6,5},{9,10},{11,12},{13,14},{10,9},... | collective-permute-start | bytes 49160 | tf_op jit(solution)/shard_map/while/body/eval_jaxpr/ppermute | solution.py:356
  31.9 1.9 %collective-permute-start.3 = (bf16[64,128]{1,0:T(8,128)(2,1)S(1)}, bf16[64,128]{1,0:T(8,128)(2,1)S(1)}, u32[]{:S(2)}, u32[]{:S(2)}) collective-permute-start(bf16[64,128]{1,0:T(8,128)(2,1)S(1)} %get-tuple-element.393), channel_id=1, source_target_pairs={{0,1},{2,3},{4,5},{6,7},{1,0},{3,2},{5,4},{7,6},{8,9},{10,11},{12,... | collective-permute-start | bytes 49160 | tf_op jit(solution)/shard_map/while/body/eval_jaxpr/ppermute | solution.py:356
  33.8 1.2 %eval_jaxpr.3 = (f32[100,1024]{1,0:T(8,128)S(1)}, f32[4,16,384]{2,1,0:T(8,128)S(1)}, s32[8,1024]{1,0:T(8,128)S(1)}, s32[4,768]{1,0:T(4,128)S(1)}, f32[100,384]{1,0:T(8,128)S(1)}, /*index=5*/f32[100,384]{1,0:T(8,128)S(1)}) custom-call(f32[100,1024]{1,0:T(8,128)S(1)} %get-tuple-element.374.stat, ...), custom_call_target="tpu_custom_call", output_to_operand_aliasing={{0}: (0, {}), {1}: (2, {}), {2}: (3, {}), {3}: (4, {})} | custom-call | flops 1000000 | bytes 1048576 | tf_op jit(solution)/shard_map/while/body/eval_jaxpr/pallas_call | solution.py:345
  35.0 0.0 collective-permute-done.2
  35.0 0.0 collective-permute-done.3
  35.0 0.0 collective-permute-done
  35.1 0.0 collective-permute-done.1
  35.1 1.1 %eval_jaxpr.2 = (f32[100,384]{1,0:T(8,128)S(1)}, bf16[64,256]{1,0:T(8,128)(2,1)S(1)}, bf16[64,256]{1,0:T(8,128)(2,1)S(1)}, bf16[64,128]{1,0:T(8,128)(2,1)S(1)}, bf16[64,128]{1,0:T(8,128)(2,1)S(1)}) custom-call(bf16[64,256]{1,0:T(8,128)(2,1)S(1)} %get-tuple-element.366.r0, ...), custom_call_target="tpu_custom_call", output_to_operand_aliasing={{1}: (4, {}), {2}: (5, {}), {3}: (6, {}), {4}: (7, {})} | custom-call | flops 1000000 | bytes 1048576 | tf_op jit(solution)/shard_map/while/body/eval_jaxpr/pallas_call | solution.py:345
  36.2 5.0 %collective-permute-start = (bf16[64,256]{1,0:T(8,128)(2,1)S(1)}, bf16[64,256]{1,0:T(8,128)(2,1)S(1)}, u32[]{:S(2)}, u32[]{:S(2)}) collective-permute-start(bf16[64,256]{1,0:T(8,128)(2,1)S(1)} %get-tuple-element.390), channel_id=1, source_target_pairs={{8,16},{24,32},{40,48},{56,64},{72,80},{88,96},{104,112},{120,128}... | collective-permute-start | bytes 98312 | tf_op jit(solution)/shard_map/while/body/eval_jaxpr/ppermute | solution.py:356
  41.1 1.9 %collective-permute-start.1 = (bf16[64,256]{1,0:T(8,128)(2,1)S(1)}, bf16[64,256]{1,0:T(8,128)(2,1)S(1)}, u32[]{:S(2)}, u32[]{:S(2)}) collective-permute-start(bf16[64,256]{1,0:T(8,128)(2,1)S(1)} %get-tuple-element.391), channel_id=1, source_target_pairs={{0,8},{16,24},{32,40},{48,56},{64,72},{80,88},{96,104},{112,120},{... | collective-permute-start | bytes 98312 | tf_op jit(solution)/shard_map/while/body/eval_jaxpr/ppermute | solution.py:356
  43.1 2.4 %collective-permute-start.2 = (bf16[64,128]{1,0:T(8,128)(2,1)S(1)}, bf16[64,128]{1,0:T(8,128)(2,1)S(1)}, u32[]{:S(2)}, u32[]{:S(2)}) collective-permute-start(bf16[64,128]{1,0:T(8,128)(2,1)S(1)} %get-tuple-element.392), channel_id=1, source_target_pairs={{1,2},{3,4},{5,6},{2,1},{4,3},{6,5},{9,10},{11,12},{13,14},{10,9},... | collective-permute-start | bytes 49160 | tf_op jit(solution)/shard_map/while/body/eval_jaxpr/ppermute | solution.py:356
  45.4 2.4 %collective-permute-start.3 = (bf16[64,128]{1,0:T(8,128)(2,1)S(1)}, bf16[64,128]{1,0:T(8,128)(2,1)S(1)}, u32[]{:S(2)}, u32[]{:S(2)}) collective-permute-start(bf16[64,128]{1,0:T(8,128)(2,1)S(1)} %get-tuple-element.393), channel_id=1, source_target_pairs={{0,1},{2,3},{4,5},{6,7},{1,0},{3,2},{5,4},{7,6},{8,9},{10,11},{12,... | collective-permute-start | bytes 49160 | tf_op jit(solution)/shard_map/while/body/eval_jaxpr/ppermute | solution.py:356
  47.9 1.2 %eval_jaxpr.3 = (f32[100,1024]{1,0:T(8,128)S(1)}, f32[4,16,384]{2,1,0:T(8,128)S(1)}, s32[8,1024]{1,0:T(8,128)S(1)}, s32[4,768]{1,0:T(4,128)S(1)}, f32[100,384]{1,0:T(8,128)S(1)}, /*index=5*/f32[100,384]{1,0:T(8,128)S(1)}) custom-call(f32[100,1024]{1,0:T(8,128)S(1)} %get-tuple-element.374.stat, ...), custom_call_target="tpu_custom_call", output_to_operand_aliasing={{0}: (0, {}), {1}: (2, {}), {2}: (3, {}), {3}: (4, {})} | custom-call | flops 1000000 | bytes 1048576 | tf_op jit(solution)/shard_map/while/body/eval_jaxpr/pallas_call | solution.py:345
  49.0 0.0 collective-permute-done.2
  49.0 0.0 collective-permute-done.3
  49.1 0.0 collective-permute-done
  49.1 0.0 collective-permute-done.1
  49.1 1.1 %eval_jaxpr.2 = (f32[100,384]{1,0:T(8,128)S(1)}, bf16[64,256]{1,0:T(8,128)(2,1)S(1)}, bf16[64,256]{1,0:T(8,128)(2,1)S(1)}, bf16[64,128]{1,0:T(8,128)(2,1)S(1)}, bf16[64,128]{1,0:T(8,128)(2,1)S(1)}) custom-call(bf16[64,256]{1,0:T(8,128)(2,1)S(1)} %get-tuple-element.366.r0, ...), custom_call_target="tpu_custom_call", output_to_operand_aliasing={{1}: (4, {}), {2}: (5, {}), {3}: (6, {}), {4}: (7, {})} | custom-call | flops 1000000 | bytes 1048576 | tf_op jit(solution)/shard_map/while/body/eval_jaxpr/pallas_call | solution.py:345
  50.2 3.6 %collective-permute-start = (bf16[64,256]{1,0:T(8,128)(2,1)S(1)}, bf16[64,256]{1,0:T(8,128)(2,1)S(1)}, u32[]{:S(2)}, u32[]{:S(2)}) collective-permute-start(bf16[64,256]{1,0:T(8,128)(2,1)S(1)} %get-tuple-element.390), channel_id=1, source_target_pairs={{8,16},{24,32},{40,48},{56,64},{72,80},{88,96},{104,112},{120,128}... | collective-permute-start | bytes 98312 | tf_op jit(solution)/shard_map/while/body/eval_jaxpr/ppermute | solution.py:356
  53.8 1.9 %collective-permute-start.1 = (bf16[64,256]{1,0:T(8,128)(2,1)S(1)}, bf16[64,256]{1,0:T(8,128)(2,1)S(1)}, u32[]{:S(2)}, u32[]{:S(2)}) collective-permute-start(bf16[64,256]{1,0:T(8,128)(2,1)S(1)} %get-tuple-element.391), channel_id=1, source_target_pairs={{0,8},{16,24},{32,40},{48,56},{64,72},{80,88},{96,104},{112,120},{... | collective-permute-start | bytes 98312 | tf_op jit(solution)/shard_map/while/body/eval_jaxpr/ppermute | solution.py:356
  55.8 3.0 %collective-permute-start.2 = (bf16[64,128]{1,0:T(8,128)(2,1)S(1)}, bf16[64,128]{1,0:T(8,128)(2,1)S(1)}, u32[]{:S(2)}, u32[]{:S(2)}) collective-permute-start(bf16[64,128]{1,0:T(8,128)(2,1)S(1)} %get-tuple-element.392), channel_id=1, source_target_pairs={{1,2},{3,4},{5,6},{2,1},{4,3},{6,5},{9,10},{11,12},{13,14},{10,9},... | collective-permute-start | bytes 49160 | tf_op jit(solution)/shard_map/while/body/eval_jaxpr/ppermute | solution.py:356
  58.8 2.4 %collective-permute-start.3 = (bf16[64,128]{1,0:T(8,128)(2,1)S(1)}, bf16[64,128]{1,0:T(8,128)(2,1)S(1)}, u32[]{:S(2)}, u32[]{:S(2)}) collective-permute-start(bf16[64,128]{1,0:T(8,128)(2,1)S(1)} %get-tuple-element.393), channel_id=1, source_target_pairs={{0,1},{2,3},{4,5},{6,7},{1,0},{3,2},{5,4},{7,6},{8,9},{10,11},{12,... | collective-permute-start | bytes 49160 | tf_op jit(solution)/shard_map/while/body/eval_jaxpr/ppermute | solution.py:356
  61.2 1.2 %eval_jaxpr.3 = (f32[100,1024]{1,0:T(8,128)S(1)}, f32[4,16,384]{2,1,0:T(8,128)S(1)}, s32[8,1024]{1,0:T(8,128)S(1)}, s32[4,768]{1,0:T(4,128)S(1)}, f32[100,384]{1,0:T(8,128)S(1)}, /*index=5*/f32[100,384]{1,0:T(8,128)S(1)}) custom-call(f32[100,1024]{1,0:T(8,128)S(1)} %get-tuple-element.374.stat, ...), custom_call_target="tpu_custom_call", output_to_operand_aliasing={{0}: (0, {}), {1}: (2, {}), {2}: (3, {}), {3}: (4, {})} | custom-call | flops 1000000 | bytes 1048576 | tf_op jit(solution)/shard_map/while/body/eval_jaxpr/pallas_call | solution.py:345
  62.4 0.0 collective-permute-done.2
  62.4 0.0 collective-permute-done.3
  62.4 0.0 collective-permute-done
  62.4 0.0 collective-permute-done.1
  62.4 1.8 %shard_map.93 = f32[100,1024]{1,0:T(8,128)} custom-call(bf16[64,256]{1,0:T(8,128)(2,1)S(1)} %get-tuple-element.162.r0, bf16[64,256]{1,0:T(8,128)(2,1)S(1)} %get-tuple-element.163.r1, bf16[64,128]{1,0:T(8,128)(2,1)S(1)} %get-tuple-element.164.r2, bf16[64,128]{1,0:T(8,128)(2,1)S(1)} %get-tuple-element.165.r3, f32[4,16,384]{2,1,0:T(8,128)S(1)} %get-tuple-element.166.compact, ...), custom_call_target="tpu_custom_call" | custom-call | tf_op jit(solution)/shard_map/pallas_call | solution.py:435
Async XLA Ops:
  1.5 20.2 %collective-permute-start.4 = (bf16[64,256]{1,0:T(8,128)(2,1)S(1)}, bf16[64,256]{1,0:T(8,128)(2,1)S(1)}, u32[]{:S(2)}, u32[]{:S(2)}) collective-permute-start(bf16[64,256]{1,0:T(8,128)(2,1)S(1)} %get-tuple-element.350), channel_id=1, source_target_pairs={{8,16},{24,32},{40,48},{56,64},{72,80},{88,96},{104,112},{120,128}... | collective-permute-start | bytes 98312 | tf_op jit(solution)/shard_map/ppermute | solution.py:356
  12.1 9.7 %collective-permute-start.5 = (bf16[64,256]{1,0:T(8,128)(2,1)S(1)}, bf16[64,256]{1,0:T(8,128)(2,1)S(1)}, u32[]{:S(2)}, u32[]{:S(2)}) collective-permute-start(bf16[64,256]{1,0:T(8,128)(2,1)S(1)} %get-tuple-element.351), channel_id=1, source_target_pairs={{0,8},{16,24},{32,40},{48,56},{64,72},{80,88},{96,104},{112,120},{... | collective-permute-start | bytes 98312 | tf_op jit(solution)/shard_map/ppermute | solution.py:356
  14.0 7.7 %collective-permute-start.6 = (bf16[64,128]{1,0:T(8,128)(2,1)S(1)}, bf16[64,128]{1,0:T(8,128)(2,1)S(1)}, u32[]{:S(2)}, u32[]{:S(2)}) collective-permute-start(bf16[64,128]{1,0:T(8,128)(2,1)S(1)} %get-tuple-element.352), channel_id=1, source_target_pairs={{1,2},{3,4},{5,6},{2,1},{4,3},{6,5},{9,10},{11,12},{13,14},{10,9},... | collective-permute-start | bytes 49160 | tf_op jit(solution)/shard_map/ppermute | solution.py:356
  17.9 3.7 %collective-permute-start.7 = (bf16[64,128]{1,0:T(8,128)(2,1)S(1)}, bf16[64,128]{1,0:T(8,128)(2,1)S(1)}, u32[]{:S(2)}, u32[]{:S(2)}) collective-permute-start(bf16[64,128]{1,0:T(8,128)(2,1)S(1)} %get-tuple-element.353), channel_id=1, source_target_pairs={{0,1},{2,3},{4,5},{6,7},{1,0},{3,2},{5,4},{7,6},{8,9},{10,11},{12,... | collective-permute-start | bytes 49160 | tf_op jit(solution)/shard_map/ppermute | solution.py:356
  22.8 12.2 %collective-permute-start = (bf16[64,256]{1,0:T(8,128)(2,1)S(1)}, bf16[64,256]{1,0:T(8,128)(2,1)S(1)}, u32[]{:S(2)}, u32[]{:S(2)}) collective-permute-start(bf16[64,256]{1,0:T(8,128)(2,1)S(1)} %get-tuple-element.390), channel_id=1, source_target_pairs={{8,16},{24,32},{40,48},{56,64},{72,80},{88,96},{104,112},{120,128}... | collective-permute-start | bytes 98312 | tf_op jit(solution)/shard_map/while/body/eval_jaxpr/ppermute | solution.py:356
  25.6 9.5 %collective-permute-start.1 = (bf16[64,256]{1,0:T(8,128)(2,1)S(1)}, bf16[64,256]{1,0:T(8,128)(2,1)S(1)}, u32[]{:S(2)}, u32[]{:S(2)}) collective-permute-start(bf16[64,256]{1,0:T(8,128)(2,1)S(1)} %get-tuple-element.391), channel_id=1, source_target_pairs={{0,8},{16,24},{32,40},{48,56},{64,72},{80,88},{96,104},{112,120},{... | collective-permute-start | bytes 98312 | tf_op jit(solution)/shard_map/while/body/eval_jaxpr/ppermute | solution.py:356
  28.4 6.6 %collective-permute-start.2 = (bf16[64,128]{1,0:T(8,128)(2,1)S(1)}, bf16[64,128]{1,0:T(8,128)(2,1)S(1)}, u32[]{:S(2)}, u32[]{:S(2)}) collective-permute-start(bf16[64,128]{1,0:T(8,128)(2,1)S(1)} %get-tuple-element.392), channel_id=1, source_target_pairs={{1,2},{3,4},{5,6},{2,1},{4,3},{6,5},{9,10},{11,12},{13,14},{10,9},... | collective-permute-start | bytes 49160 | tf_op jit(solution)/shard_map/while/body/eval_jaxpr/ppermute | solution.py:356
  31.9 3.1 %collective-permute-start.3 = (bf16[64,128]{1,0:T(8,128)(2,1)S(1)}, bf16[64,128]{1,0:T(8,128)(2,1)S(1)}, u32[]{:S(2)}, u32[]{:S(2)}) collective-permute-start(bf16[64,128]{1,0:T(8,128)(2,1)S(1)} %get-tuple-element.393), channel_id=1, source_target_pairs={{0,1},{2,3},{4,5},{6,7},{1,0},{3,2},{5,4},{7,6},{8,9},{10,11},{12,... | collective-permute-start | bytes 49160 | tf_op jit(solution)/shard_map/while/body/eval_jaxpr/ppermute | solution.py:356
  36.2 12.9 %collective-permute-start = (bf16[64,256]{1,0:T(8,128)(2,1)S(1)}, bf16[64,256]{1,0:T(8,128)(2,1)S(1)}, u32[]{:S(2)}, u32[]{:S(2)}) collective-permute-start(bf16[64,256]{1,0:T(8,128)(2,1)S(1)} %get-tuple-element.390), channel_id=1, source_target_pairs={{8,16},{24,32},{40,48},{56,64},{72,80},{88,96},{104,112},{120,128}... | collective-permute-start | bytes 98312 | tf_op jit(solution)/shard_map/while/body/eval_jaxpr/ppermute | solution.py:356
  41.1 7.9 %collective-permute-start.1 = (bf16[64,256]{1,0:T(8,128)(2,1)S(1)}, bf16[64,256]{1,0:T(8,128)(2,1)S(1)}, u32[]{:S(2)}, u32[]{:S(2)}) collective-permute-start(bf16[64,256]{1,0:T(8,128)(2,1)S(1)} %get-tuple-element.391), channel_id=1, source_target_pairs={{0,8},{16,24},{32,40},{48,56},{64,72},{80,88},{96,104},{112,120},{... | collective-permute-start | bytes 98312 | tf_op jit(solution)/shard_map/while/body/eval_jaxpr/ppermute | solution.py:356
  43.1 6.0 %collective-permute-start.2 = (bf16[64,128]{1,0:T(8,128)(2,1)S(1)}, bf16[64,128]{1,0:T(8,128)(2,1)S(1)}, u32[]{:S(2)}, u32[]{:S(2)}) collective-permute-start(bf16[64,128]{1,0:T(8,128)(2,1)S(1)} %get-tuple-element.392), channel_id=1, source_target_pairs={{1,2},{3,4},{5,6},{2,1},{4,3},{6,5},{9,10},{11,12},{13,14},{10,9},... | collective-permute-start | bytes 49160 | tf_op jit(solution)/shard_map/while/body/eval_jaxpr/ppermute | solution.py:356
  45.4 3.6 %collective-permute-start.3 = (bf16[64,128]{1,0:T(8,128)(2,1)S(1)}, bf16[64,128]{1,0:T(8,128)(2,1)S(1)}, u32[]{:S(2)}, u32[]{:S(2)}) collective-permute-start(bf16[64,128]{1,0:T(8,128)(2,1)S(1)} %get-tuple-element.393), channel_id=1, source_target_pairs={{0,1},{2,3},{4,5},{6,7},{1,0},{3,2},{5,4},{7,6},{8,9},{10,11},{12,... | collective-permute-start | bytes 49160 | tf_op jit(solution)/shard_map/while/body/eval_jaxpr/ppermute | solution.py:356
  50.2 12.2 %collective-permute-start = (bf16[64,256]{1,0:T(8,128)(2,1)S(1)}, bf16[64,256]{1,0:T(8,128)(2,1)S(1)}, u32[]{:S(2)}, u32[]{:S(2)}) collective-permute-start(bf16[64,256]{1,0:T(8,128)(2,1)S(1)} %get-tuple-element.390), channel_id=1, source_target_pairs={{8,16},{24,32},{40,48},{56,64},{72,80},{88,96},{104,112},{120,128}... | collective-permute-start | bytes 98312 | tf_op jit(solution)/shard_map/while/body/eval_jaxpr/ppermute | solution.py:356
  53.8 8.6 %collective-permute-start.1 = (bf16[64,256]{1,0:T(8,128)(2,1)S(1)}, bf16[64,256]{1,0:T(8,128)(2,1)S(1)}, u32[]{:S(2)}, u32[]{:S(2)}) collective-permute-start(bf16[64,256]{1,0:T(8,128)(2,1)S(1)} %get-tuple-element.391), channel_id=1, source_target_pairs={{0,8},{16,24},{32,40},{48,56},{64,72},{80,88},{96,104},{112,120},{... | collective-permute-start | bytes 98312 | tf_op jit(solution)/shard_map/while/body/eval_jaxpr/ppermute | solution.py:356
  55.8 6.6 %collective-permute-start.2 = (bf16[64,128]{1,0:T(8,128)(2,1)S(1)}, bf16[64,128]{1,0:T(8,128)(2,1)S(1)}, u32[]{:S(2)}, u32[]{:S(2)}) collective-permute-start(bf16[64,128]{1,0:T(8,128)(2,1)S(1)} %get-tuple-element.392), channel_id=1, source_target_pairs={{1,2},{3,4},{5,6},{2,1},{4,3},{6,5},{9,10},{11,12},{13,14},{10,9},... | collective-permute-start | bytes 49160 | tf_op jit(solution)/shard_map/while/body/eval_jaxpr/ppermute | solution.py:356
  58.8 3.6 %collective-permute-start.3 = (bf16[64,128]{1,0:T(8,128)(2,1)S(1)}, bf16[64,128]{1,0:T(8,128)(2,1)S(1)}, u32[]{:S(2)}, u32[]{:S(2)}) collective-permute-start(bf16[64,128]{1,0:T(8,128)(2,1)S(1)} %get-tuple-element.393), channel_id=1, source_target_pairs={{0,1},{2,3},{4,5},{6,7},{1,0},{3,2},{5,4},{7,6},{8,9},{10,11},{12,... | collective-permute-start | bytes 49160 | tf_op jit(solution)/shard_map/while/body/eval_jaxpr/ppermute | solution.py:356

commit v7 on v6

--- a/solution.py
+++ b/solution.py
@@ -69,7 +69,7 @@
     start = -(-rows // 16) * 16
     top = values.astype(BF16).astype(F32)
     gap = jnp.zeros((start - rows, values.shape[1]), F32)
-    return jnp.concatenate([jnp.concatenate([top, gap], axis=0), values - top], axis=0).astype(BF16), start
+    return jnp.concatenate([top, gap, values - top, gap], axis=0).astype(BF16), start
 
 
 def three_parts(values):
@@ -234,8 +234,7 @@
         picked.append(choose(mm(trace[...], near[:, now]), face[:, now], 0, ROWS, 0.0))
     picked = by_face(jnp.concatenate(picked, axis=1)).astype(BF16)
     if kept is not None:
-        rest = stack(jnp.concatenate([parts[rows:].astype(F32), jnp.zeros((rows - comps, elems), F32)], axis=0))
-        rest = choose(mm(rest.astype(BF16), hot(low[:, :count], BLOCK)), block[:, :count], 0, rows)
+        rest = choose(mm(stack(parts[rows:]), hot(low[:, :count], BLOCK)), block[:, :count], 0, rows)
         kept[:, here] = mine.astype(F32) + rest[:comps]
     base[:, here] = mm(volume[...], mine) + mm(lift[...], picked)
 
@@ -267,7 +266,7 @@
 def scatter(delta, rank, here):
     parts, second = two_parts(delta)
     found = mm(parts, hot(rank - here.start, delta.shape[1]))
-    return found[: delta.shape[0]] + found[second:]
+    return found[: delta.shape[0]] + found[second : second + delta.shape[0]]
 
 
 def local_kernel(

time: 64.7 us -> 65 us (level)
  the two profiles are of different devices: /device:TPU:35 before, /device:TPU:59 now
where the time goes in v7:
time: 65 us; the launch traced here: 63.9 us
  starting transfers between devices  51.6 us (79%)
  Pallas kernels  11.9 us (18%)
    ppermute x16, starting transfers between devices, swapped(): return lax.ppermute(block, axis, pairs + [(j, i) for i, j in pairs])  51.6 us
    pallas_call x7, Pallas kernels, call(): pl.pallas_call(kernel, out_shape=outs, input_output_aliases=aliases, comp...  8.62 us
    pallas_call x1, Pallas kernels, local(): pl.pallas_call(last_kernel, out_specs=pl.BlockSpec(memory_space=pltpu.Mem...  1.76 us
    pallas_call x1, Pallas kernels, local(): pl.pallas_call(first_kernel, in_specs=[pl.BlockSpec(memory_space=pltpu.Me...  1.48 us
  transfers between devices with their start and end apart: 16, of which 0 were waited for; matrix products, arithmetic and copies ran while one was open for 0% of the time, Pallas kernels for 8%

profile of v7, /device:TPU:59, one launch (start us, length us, event | category | flops | bytes accessed | tf_op | source)
XLA Modules:
  0.0 63.9 jit_solution(3901211168439076219)
XLA Ops:
  0.0 1.5 %shard_map.91 = (bf16[64,256]{1,0:T(8,128)(2,1)S(1)}, bf16[64,256]{1,0:T(8,128)(2,1)S(1)}, bf16[64,128]{1,0:T(8,128)(2,1)S(1)}, bf16[64,128]{1,0:T(8,128)(2,1)S(...) custom-call(f32[100,1024]{1,0:T(8,128)} %refs_0_.1, ...), custom_call_target="tpu_custom_call" | custom-call | tf_op jit(solution)/shard_map/pallas_call | solution.py:385
  1.5 11.5 %collective-permute-start.4 = (bf16[64,256]{1,0:T(8,128)(2,1)S(1)}, bf16[64,256]{1,0:T(8,128)(2,1)S(1)}, u32[]{:S(2)}, u32[]{:S(2)}) collective-permute-start(bf16[64,256]{1,0:T(8,128)(2,1)S(1)} %get-tuple-element.350), channel_id=1, source_target_pairs={{8,16},{24,32},{40,48},{56,64},{72,80},{88,96},{104,112},{120,128}... | collective-permute-start | bytes 98312 | tf_op jit(solution)/shard_map/ppermute | solution.py:355
  13.0 1.9 %collective-permute-start.5 = (bf16[64,256]{1,0:T(8,128)(2,1)S(1)}, bf16[64,256]{1,0:T(8,128)(2,1)S(1)}, u32[]{:S(2)}, u32[]{:S(2)}) collective-permute-start(bf16[64,256]{1,0:T(8,128)(2,1)S(1)} %get-tuple-element.351), channel_id=1, source_target_pairs={{0,8},{16,24},{32,40},{48,56},{64,72},{80,88},{96,104},{112,120},{... | collective-permute-start | bytes 98312 | tf_op jit(solution)/shard_map/ppermute | solution.py:355
  14.9 4.0 %collective-permute-start.6 = (bf16[64,128]{1,0:T(8,128)(2,1)S(1)}, bf16[64,128]{1,0:T(8,128)(2,1)S(1)}, u32[]{:S(2)}, u32[]{:S(2)}) collective-permute-start(bf16[64,128]{1,0:T(8,128)(2,1)S(1)} %get-tuple-element.352), channel_id=1, source_target_pairs={{1,2},{3,4},{5,6},{2,1},{4,3},{6,5},{9,10},{11,12},{13,14},{10,9},... | collective-permute-start | bytes 49160 | tf_op jit(solution)/shard_map/ppermute | solution.py:355
  18.8 1.9 %collective-permute-start.7 = (bf16[64,128]{1,0:T(8,128)(2,1)S(1)}, bf16[64,128]{1,0:T(8,128)(2,1)S(1)}, u32[]{:S(2)}, u32[]{:S(2)}) collective-permute-start(bf16[64,128]{1,0:T(8,128)(2,1)S(1)} %get-tuple-element.353), channel_id=1, source_target_pairs={{0,1},{2,3},{4,5},{6,7},{1,0},{3,2},{5,4},{7,6},{8,9},{10,11},{12,... | collective-permute-start | bytes 49160 | tf_op jit(solution)/shard_map/ppermute | solution.py:355
  20.8 1.8 %shard_map.92 = (f32[4,16,384]{2,1,0:T(8,128)S(1)}, s32[8,1024]{1,0:T(8,128)S(1)}, s32[4,768]{1,0:T(4,128)S(1)}, f32[100,384]{1,0:T(8,128)S(1)}, f32[100,384]{1,...) custom-call(f32[100,1024]{1,0:T(8,128)S(1)} %get-tuple-element.354.state, ...), custom_call_target="tpu_custom_call" | custom-call | flops 1000000 | bytes 1048576 | tf_op jit(solution)/shard_map/pallas_call | solution.py:344
  22.6 0.0 collective-permute-done.6
  22.6 0.0 collective-permute-done.7
  22.6 0.0 collective-permute-done.4
  22.6 0.0 collective-permute-done.5
  22.6 39.5 %while.36 = (s32[]{:T(128)}, bf16[64,256]{1,0:T(8,128)(2,1)S(1)}, bf16[64,256]{1,0:T(8,128)(2,1)S(1)}, bf16[64,128]{1,0:T(8,128)(2,1)S(1)}, bf16[64,128]{1,0:T(8...) while((s32[]{:T(128)}, bf16[64,256]{1,0:T(8,128)(2,1)S(1)}, ...), condition=%wide.region_1.0_spmd, body=%wide.region_0.0_spmd.sunk | while | flops 2000002 | bytes 2490709 | solution.py:431
  22.6 1.1 %eval_jaxpr.2 = (f32[100,384]{1,0:T(8,128)S(1)}, bf16[64,256]{1,0:T(8,128)(2,1)S(1)}, bf16[64,256]{1,0:T(8,128)(2,1)S(1)}, bf16[64,128]{1,0:T(8,128)(2,1)S(1)}, bf16[64,128]{1,0:T(8,128)(2,1)S(1)}) custom-call(bf16[64,256]{1,0:T(8,128)(2,1)S(1)} %get-tuple-element.366.r0, ...), custom_call_target="tpu_custom_call", output_to_operand_aliasing={{1}: (4, {}), {2}: (5, {}), {3}: (6, {}), {4}: (7, {})} | custom-call | flops 1000000 | bytes 1048576 | tf_op jit(solution)/shard_map/while/body/eval_jaxpr/pallas_call | solution.py:344
  23.7 2.7 %collective-permute-start = (bf16[64,256]{1,0:T(8,128)(2,1)S(1)}, bf16[64,256]{1,0:T(8,128)(2,1)S(1)}, u32[]{:S(2)}, u32[]{:S(2)}) collective-permute-start(bf16[64,256]{1,0:T(8,128)(2,1)S(1)} %get-tuple-element.390), channel_id=1, source_target_pairs={{8,16},{24,32},{40,48},{56,64},{72,80},{88,96},{104,112},{120,128}... | collective-permute-start | bytes 98312 | tf_op jit(solution)/shard_map/while/body/eval_jaxpr/ppermute | solution.py:355
  26.5 2.8 %collective-permute-start.1 = (bf16[64,256]{1,0:T(8,128)(2,1)S(1)}, bf16[64,256]{1,0:T(8,128)(2,1)S(1)}, u32[]{:S(2)}, u32[]{:S(2)}) collective-permute-start(bf16[64,256]{1,0:T(8,128)(2,1)S(1)} %get-tuple-element.391), channel_id=1, source_target_pairs={{0,8},{16,24},{32,40},{48,56},{64,72},{80,88},{96,104},{112,120},{... | collective-permute-start | bytes 98312 | tf_op jit(solution)/shard_map/while/body/eval_jaxpr/ppermute | solution.py:355
  29.3 3.5 %collective-permute-start.2 = (bf16[64,128]{1,0:T(8,128)(2,1)S(1)}, bf16[64,128]{1,0:T(8,128)(2,1)S(1)}, u32[]{:S(2)}, u32[]{:S(2)}) collective-permute-start(bf16[64,128]{1,0:T(8,128)(2,1)S(1)} %get-tuple-element.392), channel_id=1, source_target_pairs={{1,2},{3,4},{5,6},{2,1},{4,3},{6,5},{9,10},{11,12},{13,14},{10,9},... | collective-permute-start | bytes 49160 | tf_op jit(solution)/shard_map/while/body/eval_jaxpr/ppermute | solution.py:355
  32.8 1.9 %collective-permute-start.3 = (bf16[64,128]{1,0:T(8,128)(2,1)S(1)}, bf16[64,128]{1,0:T(8,128)(2,1)S(1)}, u32[]{:S(2)}, u32[]{:S(2)}) collective-permute-start(bf16[64,128]{1,0:T(8,128)(2,1)S(1)} %get-tuple-element.393), channel_id=1, source_target_pairs={{0,1},{2,3},{4,5},{6,7},{1,0},{3,2},{5,4},{7,6},{8,9},{10,11},{12,... | collective-permute-start | bytes 49160 | tf_op jit(solution)/shard_map/while/body/eval_jaxpr/ppermute | solution.py:355
  34.7 1.2 %eval_jaxpr.3 = (f32[100,1024]{1,0:T(8,128)S(1)}, f32[4,16,384]{2,1,0:T(8,128)S(1)}, s32[8,1024]{1,0:T(8,128)S(1)}, s32[4,768]{1,0:T(4,128)S(1)}, f32[100,384]{1,0:T(8,128)S(1)}, /*index=5*/f32[100,384]{1,0:T(8,128)S(1)}) custom-call(f32[100,1024]{1,0:T(8,128)S(1)} %get-tuple-element.374.stat, ...), custom_call_target="tpu_custom_call", output_to_operand_aliasing={{0}: (0, {}), {1}: (2, {}), {2}: (3, {}), {3}: (4, {})} | custom-call | flops 1000000 | bytes 1048576 | tf_op jit(solution)/shard_map/while/body/eval_jaxpr/pallas_call | solution.py:344
  35.9 0.0 collective-permute-done.2
  35.9 0.0 collective-permute-done.3
  35.9 0.0 collective-permute-done
  36.0 0.0 collective-permute-done.1
  36.0 1.1 %eval_jaxpr.2 = (f32[100,384]{1,0:T(8,128)S(1)}, bf16[64,256]{1,0:T(8,128)(2,1)S(1)}, bf16[64,256]{1,0:T(8,128)(2,1)S(1)}, bf16[64,128]{1,0:T(8,128)(2,1)S(1)}, bf16[64,128]{1,0:T(8,128)(2,1)S(1)}) custom-call(bf16[64,256]{1,0:T(8,128)(2,1)S(1)} %get-tuple-element.366.r0, ...), custom_call_target="tpu_custom_call", output_to_operand_aliasing={{1}: (4, {}), {2}: (5, {}), {3}: (6, {}), {4}: (7, {})} | custom-call | flops 1000000 | bytes 1048576 | tf_op jit(solution)/shard_map/while/body/eval_jaxpr/pallas_call | solution.py:344
  37.1 3.7 %collective-permute-start = (bf16[64,256]{1,0:T(8,128)(2,1)S(1)}, bf16[64,256]{1,0:T(8,128)(2,1)S(1)}, u32[]{:S(2)}, u32[]{:S(2)}) collective-permute-start(bf16[64,256]{1,0:T(8,128)(2,1)S(1)} %get-tuple-element.390), channel_id=1, source_target_pairs={{8,16},{24,32},{40,48},{56,64},{72,80},{88,96},{104,112},{120,128}... | collective-permute-start | bytes 98312 | tf_op jit(solution)/shard_map/while/body/eval_jaxpr/ppermute | solution.py:355
  40.8 1.9 %collective-permute-start.1 = (bf16[64,256]{1,0:T(8,128)(2,1)S(1)}, bf16[64,256]{1,0:T(8,128)(2,1)S(1)}, u32[]{:S(2)}, u32[]{:S(2)}) collective-permute-start(bf16[64,256]{1,0:T(8,128)(2,1)S(1)} %get-tuple-element.391), channel_id=1, source_target_pairs={{0,8},{16,24},{32,40},{48,56},{64,72},{80,88},{96,104},{112,120},{... | collective-permute-start | bytes 98312 | tf_op jit(solution)/shard_map/while/body/eval_jaxpr/ppermute | solution.py:355
  42.8 2.4 %collective-permute-start.2 = (bf16[64,128]{1,0:T(8,128)(2,1)S(1)}, bf16[64,128]{1,0:T(8,128)(2,1)S(1)}, u32[]{:S(2)}, u32[]{:S(2)}) collective-permute-start(bf16[64,128]{1,0:T(8,128)(2,1)S(1)} %get-tuple-element.392), channel_id=1, source_target_pairs={{1,2},{3,4},{5,6},{2,1},{4,3},{6,5},{9,10},{11,12},{13,14},{10,9},... | collective-permute-start | bytes 49160 | tf_op jit(solution)/shard_map/while/body/eval_jaxpr/ppermute | solution.py:355
  45.1 2.4 %collective-permute-start.3 = (bf16[64,128]{1,0:T(8,128)(2,1)S(1)}, bf16[64,128]{1,0:T(8,128)(2,1)S(1)}, u32[]{:S(2)}, u32[]{:S(2)}) collective-permute-start(bf16[64,128]{1,0:T(8,128)(2,1)S(1)} %get-tuple-element.393), channel_id=1, source_target_pairs={{0,1},{2,3},{4,5},{6,7},{1,0},{3,2},{5,4},{7,6},{8,9},{10,11},{12,... | collective-permute-start | bytes 49160 | tf_op jit(solution)/shard_map/while/body/eval_jaxpr/ppermute | solution.py:355
  47.5 1.2 %eval_jaxpr.3 = (f32[100,1024]{1,0:T(8,128)S(1)}, f32[4,16,384]{2,1,0:T(8,128)S(1)}, s32[8,1024]{1,0:T(8,128)S(1)}, s32[4,768]{1,0:T(4,128)S(1)}, f32[100,384]{1,0:T(8,128)S(1)}, /*index=5*/f32[100,384]{1,0:T(8,128)S(1)}) custom-call(f32[100,1024]{1,0:T(8,128)S(1)} %get-tuple-element.374.stat, ...), custom_call_target="tpu_custom_call", output_to_operand_aliasing={{0}: (0, {}), {1}: (2, {}), {2}: (3, {}), {3}: (4, {})} | custom-call | flops 1000000 | bytes 1048576 | tf_op jit(solution)/shard_map/while/body/eval_jaxpr/pallas_call | solution.py:344
  48.7 0.0 collective-permute-done.2
  48.7 0.0 collective-permute-done.3
  48.7 0.0 collective-permute-done
  48.8 0.0 collective-permute-done.1
  48.8 1.1 %eval_jaxpr.2 = (f32[100,384]{1,0:T(8,128)S(1)}, bf16[64,256]{1,0:T(8,128)(2,1)S(1)}, bf16[64,256]{1,0:T(8,128)(2,1)S(1)}, bf16[64,128]{1,0:T(8,128)(2,1)S(1)}, bf16[64,128]{1,0:T(8,128)(2,1)S(1)}) custom-call(bf16[64,256]{1,0:T(8,128)(2,1)S(1)} %get-tuple-element.366.r0, ...), custom_call_target="tpu_custom_call", output_to_operand_aliasing={{1}: (4, {}), {2}: (5, {}), {3}: (6, {}), {4}: (7, {})} | custom-call | flops 1000000 | bytes 1048576 | tf_op jit(solution)/shard_map/while/body/eval_jaxpr/pallas_call | solution.py:344
  49.9 3.6 %collective-permute-start = (bf16[64,256]{1,0:T(8,128)(2,1)S(1)}, bf16[64,256]{1,0:T(8,128)(2,1)S(1)}, u32[]{:S(2)}, u32[]{:S(2)}) collective-permute-start(bf16[64,256]{1,0:T(8,128)(2,1)S(1)} %get-tuple-element.390), channel_id=1, source_target_pairs={{8,16},{24,32},{40,48},{56,64},{72,80},{88,96},{104,112},{120,128}... | collective-permute-start | bytes 98312 | tf_op jit(solution)/shard_map/while/body/eval_jaxpr/ppermute | solution.py:355
  53.5 1.9 %collective-permute-start.1 = (bf16[64,256]{1,0:T(8,128)(2,1)S(1)}, bf16[64,256]{1,0:T(8,128)(2,1)S(1)}, u32[]{:S(2)}, u32[]{:S(2)}) collective-permute-start(bf16[64,256]{1,0:T(8,128)(2,1)S(1)} %get-tuple-element.391), channel_id=1, source_target_pairs={{0,8},{16,24},{32,40},{48,56},{64,72},{80,88},{96,104},{112,120},{... | collective-permute-start | bytes 98312 | tf_op jit(solution)/shard_map/while/body/eval_jaxpr/ppermute | solution.py:355
  55.5 3.0 %collective-permute-start.2 = (bf16[64,128]{1,0:T(8,128)(2,1)S(1)}, bf16[64,128]{1,0:T(8,128)(2,1)S(1)}, u32[]{:S(2)}, u32[]{:S(2)}) collective-permute-start(bf16[64,128]{1,0:T(8,128)(2,1)S(1)} %get-tuple-element.392), channel_id=1, source_target_pairs={{1,2},{3,4},{5,6},{2,1},{4,3},{6,5},{9,10},{11,12},{13,14},{10,9},... | collective-permute-start | bytes 49160 | tf_op jit(solution)/shard_map/while/body/eval_jaxpr/ppermute | solution.py:355
  58.5 2.4 %collective-permute-start.3 = (bf16[64,128]{1,0:T(8,128)(2,1)S(1)}, bf16[64,128]{1,0:T(8,128)(2,1)S(1)}, u32[]{:S(2)}, u32[]{:S(2)}) collective-permute-start(bf16[64,128]{1,0:T(8,128)(2,1)S(1)} %get-tuple-element.393), channel_id=1, source_target_pairs={{0,1},{2,3},{4,5},{6,7},{1,0},{3,2},{5,4},{7,6},{8,9},{10,11},{12,... | collective-permute-start | bytes 49160 | tf_op jit(solution)/shard_map/while/body/eval_jaxpr/ppermute | solution.py:355
  60.9 1.2 %eval_jaxpr.3 = (f32[100,1024]{1,0:T(8,128)S(1)}, f32[4,16,384]{2,1,0:T(8,128)S(1)}, s32[8,1024]{1,0:T(8,128)S(1)}, s32[4,768]{1,0:T(4,128)S(1)}, f32[100,384]{1,0:T(8,128)S(1)}, /*index=5*/f32[100,384]{1,0:T(8,128)S(1)}) custom-call(f32[100,1024]{1,0:T(8,128)S(1)} %get-tuple-element.374.stat, ...), custom_call_target="tpu_custom_call", output_to_operand_aliasing={{0}: (0, {}), {1}: (2, {}), {2}: (3, {}), {3}: (4, {})} | custom-call | flops 1000000 | bytes 1048576 | tf_op jit(solution)/shard_map/while/body/eval_jaxpr/pallas_call | solution.py:344
  62.1 0.0 collective-permute-done.2
  62.1 0.0 collective-permute-done.3
  62.1 0.0 collective-permute-done
  62.1 0.0 collective-permute-done.1
  62.1 1.8 %shard_map.93 = f32[100,1024]{1,0:T(8,128)} custom-call(bf16[64,256]{1,0:T(8,128)(2,1)S(1)} %get-tuple-element.162.r0, bf16[64,256]{1,0:T(8,128)(2,1)S(1)} %get-tuple-element.163.r1, bf16[64,128]{1,0:T(8,128)(2,1)S(1)} %get-tuple-element.164.r2, bf16[64,128]{1,0:T(8,128)(2,1)S(1)} %get-tuple-element.165.r3, f32[4,16,384]{2,1,0:T(8,128)S(1)} %get-tuple-element.166.compact, ...), custom_call_target="tpu_custom_call" | custom-call | tf_op jit(solution)/shard_map/pallas_call | solution.py:434
Async XLA Ops:
  1.5 21.1 %collective-permute-start.4 = (bf16[64,256]{1,0:T(8,128)(2,1)S(1)}, bf16[64,256]{1,0:T(8,128)(2,1)S(1)}, u32[]{:S(2)}, u32[]{:S(2)}) collective-permute-start(bf16[64,256]{1,0:T(8,128)(2,1)S(1)} %get-tuple-element.350), channel_id=1, source_target_pairs={{8,16},{24,32},{40,48},{56,64},{72,80},{88,96},{104,112},{120,128}... | collective-permute-start | bytes 98312 | tf_op jit(solution)/shard_map/ppermute | solution.py:355
  13.0 9.7 %collective-permute-start.5 = (bf16[64,256]{1,0:T(8,128)(2,1)S(1)}, bf16[64,256]{1,0:T(8,128)(2,1)S(1)}, u32[]{:S(2)}, u32[]{:S(2)}) collective-permute-start(bf16[64,256]{1,0:T(8,128)(2,1)S(1)} %get-tuple-element.351), channel_id=1, source_target_pairs={{0,8},{16,24},{32,40},{48,56},{64,72},{80,88},{96,104},{112,120},{... | collective-permute-start | bytes 98312 | tf_op jit(solution)/shard_map/ppermute | solution.py:355
  14.9 7.7 %collective-permute-start.6 = (bf16[64,128]{1,0:T(8,128)(2,1)S(1)}, bf16[64,128]{1,0:T(8,128)(2,1)S(1)}, u32[]{:S(2)}, u32[]{:S(2)}) collective-permute-start(bf16[64,128]{1,0:T(8,128)(2,1)S(1)} %get-tuple-element.352), channel_id=1, source_target_pairs={{1,2},{3,4},{5,6},{2,1},{4,3},{6,5},{9,10},{11,12},{13,14},{10,9},... | collective-permute-start | bytes 49160 | tf_op jit(solution)/shard_map/ppermute | solution.py:355
  18.8 3.7 %collective-permute-start.7 = (bf16[64,128]{1,0:T(8,128)(2,1)S(1)}, bf16[64,128]{1,0:T(8,128)(2,1)S(1)}, u32[]{:S(2)}, u32[]{:S(2)}) collective-permute-start(bf16[64,128]{1,0:T(8,128)(2,1)S(1)} %get-tuple-element.353), channel_id=1, source_target_pairs={{0,1},{2,3},{4,5},{6,7},{1,0},{3,2},{5,4},{7,6},{8,9},{10,11},{12,... | collective-permute-start | bytes 49160 | tf_op jit(solution)/shard_map/ppermute | solution.py:355
  23.7 12.2 %collective-permute-start = (bf16[64,256]{1,0:T(8,128)(2,1)S(1)}, bf16[64,256]{1,0:T(8,128)(2,1)S(1)}, u32[]{:S(2)}, u32[]{:S(2)}) collective-permute-start(bf16[64,256]{1,0:T(8,128)(2,1)S(1)} %get-tuple-element.390), channel_id=1, source_target_pairs={{8,16},{24,32},{40,48},{56,64},{72,80},{88,96},{104,112},{120,128}... | collective-permute-start | bytes 98312 | tf_op jit(solution)/shard_map/while/body/eval_jaxpr/ppermute | solution.py:355
  26.5 9.5 %collective-permute-start.1 = (bf16[64,256]{1,0:T(8,128)(2,1)S(1)}, bf16[64,256]{1,0:T(8,128)(2,1)S(1)}, u32[]{:S(2)}, u32[]{:S(2)}) collective-permute-start(bf16[64,256]{1,0:T(8,128)(2,1)S(1)} %get-tuple-element.391), channel_id=1, source_target_pairs={{0,8},{16,24},{32,40},{48,56},{64,72},{80,88},{96,104},{112,120},{... | collective-permute-start | bytes 98312 | tf_op jit(solution)/shard_map/while/body/eval_jaxpr/ppermute | solution.py:355
  29.3 6.6 %collective-permute-start.2 = (bf16[64,128]{1,0:T(8,128)(2,1)S(1)}, bf16[64,128]{1,0:T(8,128)(2,1)S(1)}, u32[]{:S(2)}, u32[]{:S(2)}) collective-permute-start(bf16[64,128]{1,0:T(8,128)(2,1)S(1)} %get-tuple-element.392), channel_id=1, source_target_pairs={{1,2},{3,4},{5,6},{2,1},{4,3},{6,5},{9,10},{11,12},{13,14},{10,9},... | collective-permute-start | bytes 49160 | tf_op jit(solution)/shard_map/while/body/eval_jaxpr/ppermute | solution.py:355
  32.8 3.1 %collective-permute-start.3 = (bf16[64,128]{1,0:T(8,128)(2,1)S(1)}, bf16[64,128]{1,0:T(8,128)(2,1)S(1)}, u32[]{:S(2)}, u32[]{:S(2)}) collective-permute-start(bf16[64,128]{1,0:T(8,128)(2,1)S(1)} %get-tuple-element.393), channel_id=1, source_target_pairs={{0,1},{2,3},{4,5},{6,7},{1,0},{3,2},{5,4},{7,6},{8,9},{10,11},{12,... | collective-permute-start | bytes 49160 | tf_op jit(solution)/shard_map/while/body/eval_jaxpr/ppermute | solution.py:355
  37.1 11.7 %collective-permute-start = (bf16[64,256]{1,0:T(8,128)(2,1)S(1)}, bf16[64,256]{1,0:T(8,128)(2,1)S(1)}, u32[]{:S(2)}, u32[]{:S(2)}) collective-permute-start(bf16[64,256]{1,0:T(8,128)(2,1)S(1)} %get-tuple-element.390), channel_id=1, source_target_pairs={{8,16},{24,32},{40,48},{56,64},{72,80},{88,96},{104,112},{120,128}... | collective-permute-start | bytes 98312 | tf_op jit(solution)/shard_map/while/body/eval_jaxpr/ppermute | solution.py:355
  40.8 7.9 %collective-permute-start.1 = (bf16[64,256]{1,0:T(8,128)(2,1)S(1)}, bf16[64,256]{1,0:T(8,128)(2,1)S(1)}, u32[]{:S(2)}, u32[]{:S(2)}) collective-permute-start(bf16[64,256]{1,0:T(8,128)(2,1)S(1)} %get-tuple-element.391), channel_id=1, source_target_pairs={{0,8},{16,24},{32,40},{48,56},{64,72},{80,88},{96,104},{112,120},{... | collective-permute-start | bytes 98312 | tf_op jit(solution)/shard_map/while/body/eval_jaxpr/ppermute | solution.py:355
  42.8 6.0 %collective-permute-start.2 = (bf16[64,128]{1,0:T(8,128)(2,1)S(1)}, bf16[64,128]{1,0:T(8,128)(2,1)S(1)}, u32[]{:S(2)}, u32[]{:S(2)}) collective-permute-start(bf16[64,128]{1,0:T(8,128)(2,1)S(1)} %get-tuple-element.392), channel_id=1, source_target_pairs={{1,2},{3,4},{5,6},{2,1},{4,3},{6,5},{9,10},{11,12},{13,14},{10,9},... | collective-permute-start | bytes 49160 | tf_op jit(solution)/shard_map/while/body/eval_jaxpr/ppermute | solution.py:355
  45.1 3.6 %collective-permute-start.3 = (bf16[64,128]{1,0:T(8,128)(2,1)S(1)}, bf16[64,128]{1,0:T(8,128)(2,1)S(1)}, u32[]{:S(2)}, u32[]{:S(2)}) collective-permute-start(bf16[64,128]{1,0:T(8,128)(2,1)S(1)} %get-tuple-element.393), channel_id=1, source_target_pairs={{0,1},{2,3},{4,5},{6,7},{1,0},{3,2},{5,4},{7,6},{8,9},{10,11},{12,... | collective-permute-start | bytes 49160 | tf_op jit(solution)/shard_map/while/body/eval_jaxpr/ppermute | solution.py:355
  49.9 12.2 %collective-permute-start = (bf16[64,256]{1,0:T(8,128)(2,1)S(1)}, bf16[64,256]{1,0:T(8,128)(2,1)S(1)}, u32[]{:S(2)}, u32[]{:S(2)}) collective-permute-start(bf16[64,256]{1,0:T(8,128)(2,1)S(1)} %get-tuple-element.390), channel_id=1, source_target_pairs={{8,16},{24,32},{40,48},{56,64},{72,80},{88,96},{104,112},{120,128}... | collective-permute-start | bytes 98312 | tf_op jit(solution)/shard_map/while/body/eval_jaxpr/ppermute | solution.py:355
  53.5 8.6 %collective-permute-start.1 = (bf16[64,256]{1,0:T(8,128)(2,1)S(1)}, bf16[64,256]{1,0:T(8,128)(2,1)S(1)}, u32[]{:S(2)}, u32[]{:S(2)}) collective-permute-start(bf16[64,256]{1,0:T(8,128)(2,1)S(1)} %get-tuple-element.391), channel_id=1, source_target_pairs={{0,8},{16,24},{32,40},{48,56},{64,72},{80,88},{96,104},{112,120},{... | collective-permute-start | bytes 98312 | tf_op jit(solution)/shard_map/while/body/eval_jaxpr/ppermute | solution.py:355
  55.5 6.6 %collective-permute-start.2 = (bf16[64,128]{1,0:T(8,128)(2,1)S(1)}, bf16[64,128]{1,0:T(8,128)(2,1)S(1)}, u32[]{:S(2)}, u32[]{:S(2)}) collective-permute-start(bf16[64,128]{1,0:T(8,128)(2,1)S(1)} %get-tuple-element.392), channel_id=1, source_target_pairs={{1,2},{3,4},{5,6},{2,1},{4,3},{6,5},{9,10},{11,12},{13,14},{10,9},... | collective-permute-start | bytes 49160 | tf_op jit(solution)/shard_map/while/body/eval_jaxpr/ppermute | solution.py:355
  58.5 3.6 %collective-permute-start.3 = (bf16[64,128]{1,0:T(8,128)(2,1)S(1)}, bf16[64,128]{1,0:T(8,128)(2,1)S(1)}, u32[]{:S(2)}, u32[]{:S(2)}) collective-permute-start(bf16[64,128]{1,0:T(8,128)(2,1)S(1)} %get-tuple-element.393), channel_id=1, source_target_pairs={{0,1},{2,3},{4,5},{6,7},{1,0},{3,2},{5,4},{7,6},{8,9},{10,11},{12,... | collective-permute-start | bytes 49160 | tf_op jit(solution)/shard_map/while/body/eval_jaxpr/ppermute | solution.py:355
